TPU v7x, 32 devices: a whole 2x2x4 slice. The times are simulated.
32 devices in a mesh: seq: 8 (over z, x), tensor: 4 (over y, core).
Axes of the slice: x: 2, y: 2, z: 4, core: 2. Of those that a mesh axis runs over, the one named last changes fastest.
Arguments:
- hidden_in: bfloat16 [1024, 4096], P(('seq', 'tensor')), may hold values from -30 to 30
- prev_amax: float32 [], replicated, may hold values from 5 to 9
- w_x: bfloat16 [4096, 8192], P('seq', 'tensor'), may hold values from -0.09375 to 0.09375
- w_bc: bfloat16 [4096, 8, 2, 128], P('seq', 'tensor'), may hold values from -0.046875 to 0.046875
- w_dt: bfloat16 [4096, 128], P('seq', 'tensor'), may hold values from -0.09375 to 0.09375
- conv_x: float32 [4, 8192], P(None, 'tensor'), may hold values from -4 to 4
- conv_bc: float32 [4, 8, 2, 128], P(None, 'tensor'), may hold values from -4 to 4
- conv_state_x: bfloat16 [3, 8192], P(None, 'tensor'), may hold values from -6 to 6
- conv_state_bc: bfloat16 [3, 8, 2, 128], P(None, 'tensor'), may hold values from -3 to 3
- dt_bias: float32 [128], P('tensor'), may hold values from -2 to 1
- decay_rate: float32 [128], P('tensor'), may hold values from 9.765625e-05 to 0.12
- skip: float32 [128], P('tensor'), may hold values from 0.5 to 4
- init_state: float32 [128, 64, 128], P('tensor'), may hold values from -48 to 48
- norm_gain: float32 [8192], P('tensor'), may hold values from 0.1 to 1.9
- w_out: bfloat16 [8192, 4096], P('tensor', 'seq'), may hold values from -0.0625 to 0.0625
Outputs:
- layer_out: bfloat16 [1024, 4096], P(('seq', 'tensor'))
- abs_max: float32 [], replicated
All inputs are finite; a program needn't handle non-finite values.
Results may differ from a plain program's by a relative error of at most 0.019.
Values may be sent and summed in bfloat16 or wider, within the bound.
No kernel may reach another device: no remote copies, remote signals or barrier semaphores. Data moves between devices by JAX's collectives and lax.ppermute only.
A program may use at most 64 MiB of HBM per device.

v0:
```python
import functools

import jax
import jax.numpy as jnp
from jax import lax
from jax.experimental import pallas as pl
from jax.experimental.pallas import tpu as pltpu
from jax.sharding import PartitionSpec as P

HEADS = 128
HEAD_DIM = 64
STATE = 128
GROUPS = 8
KERNEL = 4
SPAN = 128


epsilon = 1e-05
quant_range = 448.0


def from_behind(value, axis, steps):
    count = lax.axis_size(axis)
    first, last = (max(0, -steps), min(count, count - steps))
    return lax.ppermute(value, axis, [(source, source + steps) for source in range(first, last)])


def carried_in(shard, axis, combine, identity):
    count, here = (lax.axis_size(axis), lax.axis_index(axis))
    everything = jax.tree.map(
        lambda part, kind: lax.all_gather(part.astype(kind), axis),
        shard,
        (jnp.bfloat16, jnp.bfloat16),
    )
    start = jax.tree.map(
        lambda part, zero: jnp.broadcast_to(jnp.asarray(zero, part.dtype), part.shape),
        shard,
        identity,
    )

    def turn(k, before):
        reached = k < here
        new = combine(
            before, jax.tree.map(lambda part, own: part[k].astype(own.dtype), everything, shard)
        )
        return jax.tree.map(lambda a, b: jnp.where(reached, a, b), new, before)

    return lax.fori_loop(0, count, turn, start)


def depthwise(before, projected, conv_taps, length):
    extended = jnp.concatenate([before, projected], axis=0)
    summed = conv_taps[0] * extended[0:length]
    for offset in range(1, KERNEL):
        summed = summed + conv_taps[offset] * extended[offset : offset + length]
    return jax.nn.silu(summed).astype(jnp.bfloat16)


def combine(earlier, later):
    return (earlier[0] * later[0], later[0][:, None, None] * earlier[1] + later[1])


def by_tokens(
    hidden_in,
    prev_amax,
    w_x,
    w_bc,
    w_dt,
    conv_x,
    conv_bc,
    conv_state_x,
    conv_state_bc,
    dt_bias,
    decay_rate,
    skip,
    init_state,
    norm_gain,
    w_out,
):
    margin = KERNEL - 1
    gathered = lax.all_gather(hidden_in, "tensor", axis=0, tiled=True)
    abs_max = lax.pmax(jnp.max(jnp.abs(gathered.astype(jnp.float32))), "seq")
    in_scale = prev_amax / quant_range
    leading = lax.axis_index("seq") == 0
    row_count = gathered.shape[0]
    bc_width = w_bc.shape[1] * w_bc.shape[2] * w_bc.shape[3]
    bc_rows = jnp.reshape(w_bc, (w_bc.shape[0], bc_width))
    scaled = gathered.astype(jnp.float32) * (quant_range / prev_amax)
    quant = jnp.clip(scaled, -quant_range, quant_range).astype(jnp.bfloat16)
    pieces = (
        lax.all_gather(w_x, "seq", axis=0, tiled=True),
        lax.all_gather(bc_rows, "seq", axis=0, tiled=True),
        lax.all_gather(w_dt, "seq", axis=0, tiled=True),
    )
    x_proj, bc_proj, dt_proj = tuple(
        (
            jnp.dot(quant, weight_piece, preferred_element_type=jnp.float32)
            for weight_piece in pieces
        )
    )
    x_whole = (x_proj * in_scale).astype(jnp.bfloat16)
    bc_whole = (bc_proj * in_scale).astype(jnp.bfloat16)
    dt_raw = dt_proj * in_scale
    state_bc = jnp.reshape(conv_state_bc, (margin, bc_width))
    received = from_behind(
        (x_whole[row_count - margin :], bc_whole[row_count - margin :]), "seq", 1
    )
    x_edge = jnp.where(leading, conv_state_x, received[0])
    bc_edge = jnp.where(leading, state_bc, received[1])
    x_act = depthwise(x_edge, x_whole, conv_x, row_count)
    bc_act = depthwise(bc_edge, bc_whole, jnp.reshape(conv_bc, (KERNEL, bc_width)), row_count)
    step_size = jax.nn.softplus(dt_raw + dt_bias)
    heads_here = step_size.shape[1]
    groups_here = w_bc.shape[1]
    per_group = HEADS // GROUPS
    blocks = row_count // SPAN
    x_blocks = x_act.reshape(blocks, SPAN, heads_here, HEAD_DIM)
    bc_blocks = bc_act.reshape(blocks, SPAN, groups_here, 2, STATE)
    in_map = bc_blocks[:, :, :, 0]
    out_map = bc_blocks[:, :, :, 1]
    step_blocks = step_size.reshape(blocks, SPAN, heads_here)
    cum_blocks = jnp.cumsum(-step_blocks * decay_rate, axis=1)
    index_row = jnp.arange(SPAN, dtype=jnp.int32)
    lower_mask = index_row[:, None] >= index_row[None, :]
    intersection = jnp.einsum(
        "ctgn,cugn->cgtu", out_map, in_map, preferred_element_type=jnp.float32
    )
    intersection = jnp.repeat(intersection, per_group, axis=1)
    cum_heads = jnp.transpose(cum_blocks, (0, 2, 1))
    log_gap = cum_heads[:, :, :, None] - cum_heads[:, :, None, :]
    decay = jnp.exp(jnp.where(lower_mask[None, None], log_gap, -1e30))
    step_heads = jnp.transpose(step_blocks, (0, 2, 1))
    weights = (intersection * decay * step_heads[:, :, None, :]).astype(jnp.bfloat16)
    local_part = jnp.einsum(
        "chtu,cuhp->cthp", weights, x_blocks, preferred_element_type=jnp.float32
    )
    last_cum = cum_blocks[:, SPAN - 1, :]
    x_weighted = (
        x_blocks.astype(jnp.float32)
        * (step_blocks * jnp.exp(last_cum[:, None, :] - cum_blocks))[:, :, :, None]
    ).astype(jnp.bfloat16)
    in_heads = jnp.repeat(in_map, per_group, axis=2)
    added = jnp.einsum("cuhp,cuhn->chpn", x_weighted, in_heads, preferred_element_type=jnp.float32)

    def carry_on(carried, element):
        block_decay, block_added = element
        return (block_decay[:, None, None] * carried + block_added, carried)

    empty_state = jnp.zeros((heads_here, HEAD_DIM, STATE), jnp.float32)
    device_state, entering = lax.scan(carry_on, empty_state, (jnp.exp(last_cum), added))
    device_decay = jnp.exp(jnp.sum(last_cum, axis=0))
    seeded = device_state + jnp.where(leading, device_decay[:, None, None] * init_state, 0.0)
    identity = (jnp.ones_like(device_decay), jnp.zeros_like(device_state))
    scanned = carried_in((device_decay, seeded), "seq", combine, identity)
    incoming = jnp.where(leading, init_state, scanned[1])
    prefix = jnp.exp(jnp.cumsum(last_cum, axis=0) - last_cum)
    states_in = entering + prefix[:, :, None, None] * incoming[None]
    out_heads = jnp.repeat(out_map, per_group, axis=2).astype(jnp.float32)
    carried_part = (
        jnp.einsum("cthn,chpn->cthp", out_heads, states_in, precision=lax.Precision.HIGHEST)
        * jnp.exp(cum_blocks)[:, :, :, None]
    )
    ssm_out = local_part + carried_part + skip[None, None, :, None] * x_blocks.astype(jnp.float32)
    ssm_out = ssm_out.reshape(row_count, heads_here * HEAD_DIM)
    squares = lax.psum(jnp.sum(ssm_out * ssm_out, axis=1), "tensor")
    mean_sq = squares / (HEADS * HEAD_DIM)
    normed = (ssm_out * lax.rsqrt(mean_sq + epsilon)[:, None] * norm_gain).astype(jnp.bfloat16)
    partial_out = jnp.dot(
        normed, lax.all_gather(w_out, "seq", axis=1, tiled=True), preferred_element_type=jnp.float32
    )
    layer_out = lax.psum_scatter(
        partial_out.astype(jnp.bfloat16), "tensor", scatter_dimension=0, tiled=True
    )
    return (layer_out, abs_max)


PAIR = 2
LINE = 4
PARTS = 2
ROWS = 8
SMEM = pl.BlockSpec(memory_space=pltpu.SMEM)
HIGHEST = lax.Precision.HIGHEST


def splits(mesh):
    count, ranks = (mesh.shape["seq"], mesh.shape["tensor"])
    heads_all, groups_here = (HEADS // ranks, GROUPS // ranks)
    if count != PAIR * LINE or groups_here != PAIR or ranks & (ranks - 1):
        return False
    heads_here = heads_all // count
    return 2 * heads_here == ROWS and heads_here * HEAD_DIM == 2 * SPAN


def nt_dot(a, b, **kw):
    return lax.dot_general(
        a, b, (((1,), (1,)), ((), ())), preferred_element_type=jnp.float32, **kw
    )


def project_kernel(place_ref, factor_ref, *refs):
    outs = LINE + 4
    ranks = len(refs) - 6 - outs
    hidden = refs[:ranks]
    own_x, other_x, own_bc, other_bc, own_dt, other_dt = refs[ranks : ranks + 6]
    x_refs = refs[ranks + 6 : ranks + 6 + LINE]
    bc_ref, largest_ref, quant_ref, dt_buf = refs[ranks + 6 + LINE :]
    side, z = (place_ref[1], place_ref[2])
    step = pl.program_id(0)
    factor = factor_ref[0]
    depth = own_x.shape[0]
    largest = None
    for j in range(ranks):
        for half in range(PAIR):
            values = hidden[j][:, :, half * depth : (half + 1) * depth].astype(jnp.float32)
            scaled = jnp.clip(values * factor, -quant_range, quant_range)
            quant_ref[half, :, j] = scaled.astype(jnp.bfloat16)
            top = jnp.max(jnp.abs(values).reshape(-1, ROWS, depth), axis=0)
            largest = top if largest is None else jnp.maximum(largest, top)
    width = largest_ref.shape[1]
    top = largest[:, :width]
    for at in range(width, depth, width):
        top = jnp.maximum(top, largest[:, at : at + width])

    @pl.when(step == 0)
    def _():
        largest_ref[...] = top

    @pl.when(step > 0)
    def _():
        largest_ref[...] = jnp.maximum(largest_ref[...], top)

    rows = quant_ref.shape[1] * quant_ref.shape[2] * quant_ref.shape[3]
    near = quant_ref[side].reshape(rows, depth)
    far = quant_ref[1 - side].reshape(rows, depth)

    def both(own, other):
        return jnp.dot(near, own, preferred_element_type=jnp.float32) + jnp.dot(
            far, other, preferred_element_type=jnp.float32
        )

    at_rows = pl.ds(pl.multiple_of(step * rows, rows), rows)
    dt_buf[...] = (nt_dot(own_dt[...], near) + nt_dot(other_dt[...], far)).reshape(dt_buf.shape)
    channels = x_refs[0].shape[1]
    tokens = pl.num_programs(0) * rows
    extra = rows // channels * ROWS
    upper = lax.broadcasted_iota(jnp.int32, (ROWS, channels), 0) < ROWS // 2
    for m in reversed(range(LINE)):
        owner = z ^ m
        cut = pl.ds(pl.multiple_of(owner * channels, channels), channels)
        x_refs[m][at_rows] = both(own_x[:, cut], other_x[:, cut]).astype(jnp.bfloat16)
        dt = dt_buf[owner]
        pieces = [
            split_parts(dt[:, at : at + channels], upper) for at in range(0, rows, channels)
        ]
        x_refs[m][pl.ds(pl.multiple_of(tokens + step * extra, 16), extra)] = jnp.concatenate(
            pieces, axis=0
        ).astype(jnp.bfloat16)
    bc_ref[at_rows] = both(own_bc[...], other_bc[...]).astype(jnp.bfloat16)


def split_parts(values, upper):
    top = values.astype(jnp.bfloat16).astype(jnp.float32)
    return jnp.where(upper, top, values - top)


def project(place, factor, hidden, weights, part):
    count, own, wide = hidden[0].shape
    ranks = len(hidden)
    w_x, other_x = weights[:2]
    depth, x_wide = other_x.shape
    channels = x_wide // LINE
    here = count // PARTS
    steps = max(1, 2 // PARTS)
    each = here // steps
    tokens = here * ranks * own
    extra = tokens // channels * ROWS

    def fixed(array):
        return pl.BlockSpec(array.shape, lambda i, p: (0,) * array.ndim)

    payload = jax.ShapeDtypeStruct((tokens + extra, channels), jnp.bfloat16)
    maps = jax.ShapeDtypeStruct((tokens, weights[2].shape[1]), jnp.bfloat16)
    largest = jax.ShapeDtypeStruct((ROWS, 128), jnp.float32)
    outs = [payload] * LINE + [maps, largest]
    first = part * steps
    return pl.pallas_call(
        project_kernel,
        grid_spec=pltpu.PrefetchScalarGridSpec(
            num_scalar_prefetch=1,
            grid=(steps,),
            in_specs=[SMEM]
            + [pl.BlockSpec((each, own, wide), lambda i, p: (first + i, 0, 0))] * ranks
            + [pl.BlockSpec((depth, x_wide), lambda i, p: (0, p[1]))]
            + [fixed(w) for w in weights[1:]],
            out_specs=[fixed(out) for out in outs],
            scratch_shapes=[
                pltpu.VMEM((PAIR, each, ranks, own, depth), jnp.bfloat16),
                pltpu.VMEM((LINE, ROWS, each * ranks * own), jnp.float32),
            ],
        ),
        out_shape=outs,
        compiler_params=pltpu.CompilerParams(vmem_limit_bytes=40 * 2**20),
        cost_estimate=pl.CostEstimate(
            flops=2 * tokens * wide * (x_wide + maps.shape[1]),
            bytes_accessed=2 * tokens * (wide + x_wide),
            transcendentals=0,
        ),
        name="project",
    )(place, factor, *hidden, *weights)


def onward_kernel(own_ref, received_ref, out_ref):
    rows, channels = own_ref.shape
    tokens = rows * channels // (channels + ROWS)
    total = own_ref[:tokens].astype(jnp.float32) + received_ref[:tokens].astype(jnp.float32)
    out_ref[:tokens] = total.astype(jnp.bfloat16)
    upper = lax.broadcasted_iota(jnp.int32, (ROWS, channels), 0) < ROWS // 2
    extra = own_ref[tokens:].astype(jnp.float32) + received_ref[tokens:].astype(jnp.float32)
    pieces = []
    for at in range(0, rows - tokens, ROWS):
        piece = extra[at : at + ROWS]
        pieces.append(split_parts(piece + pltpu.roll(piece, ROWS // 2, 0), upper))
    out_ref[tokens:] = jnp.concatenate(pieces, axis=0).astype(jnp.bfloat16)


def onward(own, received):
    whole = pl.BlockSpec(own.shape, lambda: (0, 0))
    return pl.pallas_call(
        onward_kernel,
        in_specs=[whole, whole],
        out_specs=whole,
        out_shape=jax.ShapeDtypeStruct(own.shape, own.dtype),
        compiler_params=pltpu.CompilerParams(vmem_limit_bytes=20 * 2**20),
        cost_estimate=pl.CostEstimate(
            flops=own.size, bytes_accessed=6 * own.size, transcendentals=0
        ),
        name="onward",
    )(own, received)


def scan_kernel(first, place_ref, scale_ref, *refs):
    x_refs, bc_refs = (refs[:4], refs[4:7])
    small_ref, largest_ref, carry_ref, out_ref, carry_out_ref, x_buf, bc_buf = refs[7:]
    tokens, channels = bc_refs[0].shape
    blocks = tokens // SPAN
    heads = channels // HEAD_DIM
    rank, z = (place_ref[0], place_ref[2])
    ranks = place_ref.shape[0] - 3
    own = SPAN // ranks
    edge = ROWS
    in_scale = scale_ref[0]
    at_end = (z == 0) | (z == LINE - 1)
    if first:
        x_buf[:edge] = small_ref[:edge]
        bc_buf[:edge] = small_ref[edge : 2 * edge]
        state = carry_ref[...].T
    else:
        x_buf[:edge] = carry_ref[STATE : STATE + edge]
        bc_buf[:edge] = carry_ref[STATE + edge :]
        state = carry_ref[:STATE]

    for block in range(blocks):
        for true_rank in range(ranks):
            source = block * SPAN + (true_rank ^ rank) * own
            source = pl.ds(pl.multiple_of(source, own), own)
            at = edge + block * SPAN + true_rank * own
            at = slice(at, at + own)
            total = sum(ref[source].astype(jnp.float32) for ref in x_refs) * in_scale
            x_buf[at] = total.astype(jnp.bfloat16).astype(jnp.float32)
            near, far, done = (ref[source].astype(jnp.float32) for ref in bc_refs)
            total = ((near + far) * in_scale).astype(jnp.bfloat16).astype(jnp.float32)
            bc_buf[at] = jnp.where(at_end, done, total)

    taps = 2 * edge

    def activate(buf, row, block):
        start = edge - (KERNEL - 1) + block * SPAN
        summed = small_ref[row : row + 1] * buf[start : start + SPAN]
        for k in range(1, KERNEL):
            summed = summed + small_ref[row + k : row + k + 1] * buf[start + k : start + k + SPAN]
        return (summed / (1.0 + jnp.exp(-summed))).astype(jnp.bfloat16)

    skip = small_ref[taps + 2 * KERNEL : taps + 2 * KERNEL + 1]
    gain = small_ref[taps + 2 * KERNEL + 1 : taps + 2 * KERNEL + 2]
    bias = small_ref[4 * edge :, :SPAN]
    rate = small_ref[4 * edge :, SPAN:]

    up = lax.broadcasted_iota(jnp.int32, (SPAN, SPAN), 0)
    across = lax.broadcasted_iota(jnp.int32, (SPAN, SPAN), 1)
    lane = lax.broadcasted_iota(jnp.int32, (SPAN, channels), 1)
    lower = up >= across
    upper = (up <= across).astype(jnp.float32)
    lanes = across[:ROWS]

    dt = sum(ref[tokens:].astype(jnp.float32) for ref in x_refs)
    steps = []
    wide = channels // SPAN
    for block in range(blocks):
        tile = dt[block // wide * ROWS : (block // wide + 1) * ROWS]
        cut = tile[:, block % wide * SPAN : (block % wide + 1) * SPAN]
        cut = (cut + pltpu.roll(cut, ROWS // 2, 0)) * in_scale
        bit = 1
        while bit < ranks:
            shift = bit * own
            flipped = jnp.where(
                (lanes // shift) % 2 == 1,
                pltpu.roll(cut, shift, 1),
                pltpu.roll(cut, SPAN - shift, 1),
            )
            cut = jnp.where((rank & bit) != 0, flipped, cut)
            bit *= 2
        raw = cut + bias
        steps.append(jnp.maximum(raw, 0.0) + jnp.log1p(jnp.exp(-jnp.abs(raw))))
    drops = jnp.concatenate([-step * rate for step in steps], axis=0)
    cums = jnp.dot(drops, upper, precision=HIGHEST, preferred_element_type=jnp.float32)

    sums = jnp.zeros((SPAN, SPAN), jnp.float32)
    for block in range(blocks):
        x_act = activate(x_buf, taps, block)
        bc_act = activate(bc_buf, taps + KERNEL, block)
        in_map, out_map = (bc_act[:, :STATE], bc_act[:, STATE:])
        step, cum = (steps[block], cums[block * ROWS : (block + 1) * ROWS])
        last = cum[:, SPAN - 1 : SPAN]
        turned = jnp.concatenate(
            [
                cum,
                step * jnp.exp(last - cum),
                jnp.exp(cum),
                jnp.zeros((SPAN - 3 * ROWS, SPAN), jnp.float32),
            ],
            axis=0,
        ).T

        def spread(row):
            result = jnp.broadcast_to(turned[:, row : row + 1], (SPAN, channels))
            for h in range(1, heads):
                result = jnp.where(lane >= h * HEAD_DIM, turned[:, row + h : row + h + 1], result)
            return result

        inner = jnp.where(lower, nt_dot(out_map, in_map), 0.0)
        x_wide = x_act.astype(jnp.float32)
        weights, spaced = ([], [])
        for h in range(heads):
            gap = jnp.where(lower, turned[:, h : h + 1] - cum[h : h + 1], 0.0)
            weights.append((inner * jnp.exp(gap) * step[h : h + 1]).astype(jnp.bfloat16))
            inside = (lane >= h * HEAD_DIM) & (lane < (h + 1) * HEAD_DIM)
            spaced.append(jnp.where(inside, x_wide, 0.0).astype(jnp.bfloat16))
        local_part = jnp.dot(
            jnp.concatenate(weights, axis=1),
            jnp.concatenate(spaced, axis=0),
            preferred_element_type=jnp.float32,
        )
        grown = spread(2 * ROWS)
        x_weighted = (x_wide * spread(ROWS)).astype(jnp.bfloat16)
        added = lax.dot_general(
            in_map, x_weighted, (((0,), (0,)), ((), ())), preferred_element_type=jnp.float32
        )
        high = state.astype(jnp.bfloat16)
        rest = state - high.astype(jnp.float32)
        middle = rest.astype(jnp.bfloat16)
        low = (rest - middle.astype(jnp.float32)).astype(jnp.bfloat16)
        carried = jnp.dot(out_map, high, preferred_element_type=jnp.float32)
        carried = carried + jnp.dot(out_map, middle, preferred_element_type=jnp.float32)
        carried = carried + jnp.dot(out_map, low, preferred_element_type=jnp.float32)
        ssm_out = local_part + grown * carried + skip * x_wide
        state = grown[SPAN - 1 : SPAN] * state + added
        out_ref[block * SPAN : (block + 1) * SPAN] = (ssm_out * gain).astype(jnp.bfloat16)
        summed = jnp.sum(ssm_out * ssm_out, axis=1, keepdims=True)
        sums = jnp.where(across == block, summed, sums)

    whole = sums.T[:ROWS]
    top = whole.astype(jnp.bfloat16).astype(jnp.float32)
    largest = jnp.broadcast_to(jnp.max(largest_ref[...]), (ROWS, channels))
    extra = jnp.concatenate([jnp.concatenate([top, whole - top], axis=1), largest], axis=0)
    out_ref[tokens:] = extra.astype(jnp.bfloat16)
    carry_out_ref[:STATE] = state
    carry_out_ref[STATE : STATE + edge] = x_buf[tokens : tokens + edge]
    carry_out_ref[STATE + edge :] = bc_buf[tokens : tokens + edge]


def scan(place, in_scale, sums, maps, small, largest, carry, first):
    channels = sums[0].shape[1]
    tokens = maps[0].shape[0]

    def fixed(array):
        return pl.BlockSpec(array.shape, lambda i, p: (0, 0))

    held = pl.BlockSpec((channels, STATE), lambda i, p: (p[1] * LINE + p[2], 0))
    outs = [
        jax.ShapeDtypeStruct((tokens + 2 * ROWS, channels), jnp.bfloat16),
        jax.ShapeDtypeStruct((STATE + 2 * ROWS, channels), jnp.float32),
    ]
    return pl.pallas_call(
        functools.partial(scan_kernel, first),
        grid_spec=pltpu.PrefetchScalarGridSpec(
            num_scalar_prefetch=1,
            grid=(1,),
            in_specs=[SMEM]
            + [fixed(array) for array in (*sums, *maps, small, largest)]
            + [held if first else fixed(carry)],
            out_specs=[fixed(out) for out in outs],
            scratch_shapes=[
                pltpu.VMEM((tokens + ROWS, channels), jnp.float32),
                pltpu.VMEM((tokens + ROWS, 2 * STATE), jnp.float32),
            ],
        ),
        out_shape=outs,
        compiler_params=pltpu.CompilerParams(vmem_limit_bytes=40 * 2**20),
        cost_estimate=pl.CostEstimate(
            flops=8 * tokens * SPAN * channels,
            bytes_accessed=8 * tokens * channels,
            transcendentals=tokens * (channels + 8 * SPAN),
        ),
        name="scan",
    )(place, in_scale, *sums, *maps, small, largest, carry)


def by_heads(
    hidden_in,
    prev_amax,
    w_x,
    w_bc,
    w_dt,
    conv_x,
    conv_bc,
    conv_state_x,
    conv_state_bc,
    dt_bias,
    decay_rate,
    skip,
    init_state,
    norm_gain,
    w_out,
):
    margin = KERNEL - 1
    count, here = (lax.axis_size("seq"), lax.axis_index("seq"))
    ranks, rank = (lax.axis_size("tensor"), lax.axis_index("tensor"))
    z, side = (here // PAIR, here % PAIR)
    place_of = side * LINE + z
    f32, bf16 = (jnp.float32, jnp.bfloat16)
    own, width = hidden_in.shape
    depth = w_x.shape[0]
    channels = w_x.shape[1] // count
    heads_here = w_dt.shape[1] // count
    in_scale = (prev_amax / quant_range).reshape(1)
    factor = (quant_range / prev_amax).reshape(1)
    place = jnp.stack([rank, side, z] + [rank] * ranks).astype(jnp.int32)

    def pick(array, axis, index):
        return lax.dynamic_index_in_dim(array, index, axis, keepdims=False)

    def along(value, pairs):
        moves = [(a * PAIR + x, b * PAIR + x) for a, b in pairs for x in range(PAIR)]
        return lax.ppermute(value, "seq", moves)

    def across(value):
        return lax.ppermute(value, "seq", [(s, s ^ 1) for s in range(count)])

    half = w_x.shape[1] // PAIR
    x_send = lax.dynamic_slice_in_dim(w_x, (1 - side) * half, half, axis=1)
    bc_own = pick(w_bc, 1, side).reshape(depth, 2 * STATE)
    bc_send = pick(w_bc, 1, 1 - side).reshape(depth, 2 * STATE)
    x_send, bc_send, hidden_in = lax.optimization_barrier((x_send, bc_send, hidden_in))
    x_other = across(x_send)
    bc_other = across(bc_send)
    dt_rows = w_dt.T.reshape(PAIR, LINE, 1, heads_here, depth)
    dt_rows = jnp.broadcast_to(dt_rows, (PAIR, LINE, ROWS // heads_here, heads_here, depth))
    dt_rows = dt_rows.reshape(PAIR, LINE * ROWS, depth)
    dt_own = pick(dt_rows, 0, side)
    dt_other = across(pick(dt_rows, 0, 1 - side))

    pieces = hidden_in.reshape(own, LINE, 1, PAIR * depth).transpose(1, 2, 0, 3)
    pieces = jnp.broadcast_to(pieces, (LINE, PAIR, own, PAIR * depth))
    pieces = pieces.reshape(count, own, PAIR * depth)
    rows = [lax.all_to_all(pieces, "seq", split_axis=0, concat_axis=0, tiled=True)]
    for j in range(1, ranks):
        bit = j & -j
        rows.append(lax.ppermute(rows[j - bit], "tensor", [(t, t ^ bit) for t in range(ranks)]))

    def of_heads(array):
        return jnp.repeat(array, HEAD_DIM)[None]

    by_channel = jnp.concatenate(
        [conv_state_x.astype(f32), conv_x, of_heads(skip), norm_gain[None]], axis=0
    )
    by_channel = lax.dynamic_slice_in_dim(by_channel, place_of * channels, channels, axis=1)
    by_map = jnp.concatenate([conv_state_bc.astype(f32), conv_bc], axis=0)
    by_map = pick(by_map, 1, side).reshape(margin + KERNEL, 2 * STATE)
    by_head = jnp.stack([dt_bias, decay_rate]).reshape(2, count, heads_here)
    by_head = jnp.tile(pick(by_head, 1, place_of).T, (ROWS // heads_here, 1))
    by_head = jnp.repeat(by_head, SPAN, axis=1)
    blank = jnp.zeros((ROWS - margin, channels), f32)
    small = jnp.concatenate(
        [
            blank,
            by_channel[:margin],
            blank,
            by_map[:margin],
            by_channel[margin : margin + KERNEL],
            by_map[margin:],
            by_channel[margin + KERNEL :],
            jnp.zeros((2 * ROWS - 2 * KERNEL - 2, channels), f32),
            by_head,
        ],
        axis=0,
    )

    start, end = (0, LINE - 1)
    at_end = (z == start) | (z == end)
    next_start, next_end = (1, LINE - 2)
    weights = (w_x, x_other, bc_own, bc_other, dt_own, dt_other)
    carry = init_state.reshape(-1, STATE)
    totals, tops = ([], [])
    for part in range(PARTS):
        mine, near, over, far, maps, largest = project(place, factor, rows, weights, part)
        map_hop = along(maps, [(start, next_start), (end, next_end)])
        hop_far = along(far, [(start, next_start), (end, next_end)])
        hop_over = along(over, [(start, next_start), (end, next_end)])
        got_near = along(near, [(s, s ^ 1) for s in range(LINE)])
        map_sum = (maps.astype(f32) + map_hop.astype(f32)).astype(bf16)
        map_far = along(map_sum, [(next_start, next_end), (next_end, next_start)])
        map_done = ((map_sum.astype(f32) + map_far.astype(f32)) * in_scale).astype(bf16)
        map_done, got_near = lax.optimization_barrier((map_done, got_near))
        map_done = along(map_done, [(next_start, start), (next_end, end)])
        sent_end = onward(over, hop_far)
        hop_over, sent_end = lax.optimization_barrier((hop_over, sent_end))
        got_end = along(sent_end, [(next_start, end), (next_end, start)])
        got_next = along(onward(far, hop_over), [(next_start, next_end), (next_end, next_start)])
        gained, carry = scan(
            place,
            in_scale,
            [mine, got_near, got_end, got_next],
            [map_sum, map_far, map_done],
            small,
            largest,
            carry,
            part == 0,
        )
        tokens = gained.shape[0] - 2 * ROWS
        beside = along(gained, [(s, s ^ 1) for s in range(LINE)])
        middle = [(next_start, next_end), (next_end, next_start)]
        outward = [(next_start, start), (next_end, end)]
        facing = along(gained, middle)
        beyond = along(beside, middle)
        second = jnp.where(at_end, along(facing, outward), facing)
        third = jnp.where(at_end, along(beyond, outward), beyond)
        two, three = (jnp.where(at_end, 2, 3), jnp.where(at_end, 3, 2))
        got = ((0, gained), (1, beside), (two, second), (three, third))
        total = squares = top = None
        for m, block in got:
            for x, piece in enumerate((block, across(block))):
                at = ((side ^ x) * LINE + (z ^ m)) * channels
                w_rows = lax.dynamic_slice_in_dim(w_out, at, channels, axis=0)
                product = jnp.dot(piece, w_rows, preferred_element_type=f32)
                tail = piece[tokens:].astype(f32)
                low, high = (tail[:ROWS, :SPAN] + tail[:ROWS, SPAN:], tail[ROWS:, :SPAN])
                if total is None:
                    total, squares, top = (product, low, high)
                else:
                    total = total + product
                    squares = squares + low
                    top = jnp.maximum(top, high)
        tops.append(top)
        wide = w_out.shape[1]
        blocks = tokens // SPAN
        kept = total[:tokens].reshape(blocks, ranks, own, wide)
        for bit in (1 << b for b in range(ranks.bit_length() - 1)):
            pairs = [(t, t ^ bit) for t in range(ranks)]
            squares = squares + lax.ppermute(squares, "tensor", pairs)
            keeps = (rank // bit) % 2
            halves = kept.reshape(blocks, -1, 2, own, wide)
            received = lax.ppermute(pick(halves, 2, 1 - keeps).astype(bf16), "tensor", pairs)
            kept = pick(halves, 2, keeps) + received.astype(f32)
        kept = kept.reshape(blocks, own, wide)
        mean_sq = squares[:blocks].reshape(blocks, ranks, own) / (HEADS * HEAD_DIM)
        factors = lax.rsqrt(pick(mean_sq, 1, rank) + epsilon)
        totals.append((kept * factors[:, :, None]).astype(bf16))
    final = jnp.concatenate(totals, axis=0)
    final = lax.all_to_all(final, "seq", split_axis=0, concat_axis=0, tiled=True)
    layer_out = final.transpose(1, 0, 2).reshape(own, count * final.shape[2])
    abs_max = jnp.max(functools.reduce(jnp.maximum, tops))
    return (layer_out, abs_max)


def solution(mesh):
    return jax.shard_map(
        by_heads if splits(mesh) else by_tokens,
        mesh=mesh,
        in_specs=(
            P(("seq", "tensor"), None),
            P(),
            P("seq", "tensor"),
            P("seq", "tensor", None, None),
            P("seq", "tensor"),
            P(None, "tensor"),
            P(None, "tensor", None, None),
            P(None, "tensor"),
            P(None, "tensor", None, None),
            P("tensor"),
            P("tensor"),
            P("tensor"),
            P("tensor", None, None),
            P("tensor"),
            P("tensor", "seq"),
        ),
        out_specs=(P(("seq", "tensor"), None), P()),
        check_vma=False,
    )
```

profile of v0, /device:TPU:0, one launch (start us, length us, event | category | flops | bytes accessed | tf_op | source)
XLA Modules:
  0.0 243.9 jit_solution(1191113468005056197)
XLA Ops:
  0.7 2.2 constant_dynamic-slice_fusion.4
  3.7 2.3 constant_dynamic-slice_fusion.6
  7.2 7.3 %all-to-all-start = ((bf16[8,32,1024]{2,1,0:T(8,128)(2,1)}), bf16[8,32,1024]{2,1,0:T(8,128)(2,1)S(1)}, u32[]{:S(2)}, u32[]{:S(2)}) async-start(bf16[8,32,1024]{2,1,0:T(8,128)(2,1)} %bitcast.7), calls=%async_computation | async-start | bytes 1048576 | tf_op jit(solution)/shard_map/all_to_all | solution.py:575
  14.4 2.0 collective-permute-start.3
  16.4 12.5 %all-to-all-done.refs_0_ = bf16[8,32,1024]{2,1,0:T(8,128)(2,1)S(1)} async-done(((bf16[8,32,1024]{2,1,0:T(8,128)(2,1)}), bf16[8,32,1024]{2,1,0:T(8,128)(2,1)S(1)}, u32[]{:S(2)}, u32[]{:S(2)}) %all-to-all-start) | async-done | bytes 524320 | tf_op jit(solution)/shard_map/all_to_all | solution.py:575
  30.4 10.8 %collective-permute-done.1.refs_2_ = bf16[8,32,1024]{2,1,0:T(8,128)(2,1)S(1)} collective-permute-done((bf16[8,32,1024]{2,1,0:T(8,128)(2,1)S(1)}, bf16[8,32,1024]{2,1,0:T(8,128)(2,1)S(1)}, u32[]{:S(2)}, u32[]{:S(2)}) %collective-permute-start.1) | collective-permute-done | bytes 524320 | tf_op jit(solution)/shard_map/ppermute | solution.py:578
  41.2 2.0 collective-permute-start.4
  45.3 5.9 %collective-permute-done.5.refs_9_ = bf16[32,512]{1,0:T(8,128)(2,1)S(1)} collective-permute-done((bf16[32,512]{1,0:T(8,128)(2,1)S(1)}, bf16[32,512]{1,0:T(8,128)(2,1)S(1)}, u32[]{:S(2)}, u32[]{:S(2)}) %collective-permute-start.5) | collective-permute-done | bytes 32800 | tf_op jit(solution)/shard_map/ppermute | solution.py:557
  52.8 4.8 %project.2 = (bf16[528,256]{1,0:T(8,128)(2,1)S(1)}, bf16[528,256]{1,0:T(8,128)(2,1)S(1)}, bf16[528,256]{1,0:T(8,128)(2,1)S(1)}, bf16[528,256]{1,0:T(8,128)(2,1)S...) custom-call(s32[7]{0:T(128)S(1)} %stack.28.place_ref, f32[1]{0:T(128)} %bitcast.4.factor_ref, ...), custom_call_target="tpu_custom_call" | custom-call | flops 1342177280 | bytes 2097152 | tf_op jit(solution)/shard_map/project/pallas_call | solution.py:286
  60.5 4.2 %collective-permute-start.6 = (bf16[512,256]{1,0:T(8,128)(2,1)}, bf16[512,256]{1,0:T(8,128)(2,1)}, u32[]{:S(2)}, u32[]{:S(2)}) collective-permute-start(bf16[512,256]{1,0:T(8,128)(2,1)} %get-tuple-element.32), channel_id=1, source_target_pairs={{0,8},{4,12},{24,16},{28,20},{1,9},{5,13},{25,17},{29,21},{2,10},{... | collective-permute-start | bytes 786440 | tf_op jit(solution)/shard_map/ppermute | solution.py:554
  64.7 4.8 %project.3 = (bf16[528,256]{1,0:T(8,128)(2,1)S(1)}, bf16[528,256]{1,0:T(8,128)(2,1)S(1)}, bf16[528,256]{1,0:T(8,128)(2,1)S(1)}, bf16[528,256]{1,0:T(8,128)(2,1)S...) custom-call(s32[7]{0:T(128)S(1)} %stack.28.place_ref, f32[1]{0:T(128)} %bitcast.4.factor_ref, ...), custom_call_target="tpu_custom_call" | custom-call | flops 1342177280 | bytes 2097152 | tf_op jit(solution)/shard_map/project/pallas_call | solution.py:286
  76.6 2.0 collective-permute-start.31
  78.6 2.1 collective-permute-start.30
  83.6 3.1 %collective-permute-done.10.received_ref = bf16[528,256]{1,0:T(8,128)(2,1)S(1)} collective-permute-done((bf16[528,256]{1,0:T(8,128)(2,1)}, bf16[528,256]{1,0:T(8,128)(2,1)S(1)}, u32[]{:S(2)}, u32[]{:S(2)}) %collective-permute-start.10) | collective-permute-done | bytes 270368 | tf_op jit(solution)/shard_map/ppermute | solution.py:554
  87.3 2.4 collective-permute-start.8
  89.7 2.7 %collective-permute-done.9.received_ref = bf16[528,256]{1,0:T(8,128)(2,1)S(1)} collective-permute-done((bf16[528,256]{1,0:T(8,128)(2,1)}, bf16[528,256]{1,0:T(8,128)(2,1)S(1)}, u32[]{:S(2)}, u32[]{:S(2)}) %collective-permute-start.9) | collective-permute-done | bytes 270368 | tf_op jit(solution)/shard_map/ppermute | solution.py:554
  99.2 5.1 %collective-permute-start.29 = (bf16[528,256]{1,0:T(8,128)(2,1)S(1)}, bf16[528,256]{1,0:T(8,128)(2,1)S(1)}, u32[]{:S(2)}, u32[]{:S(2)}) collective-permute-start(bf16[528,256]{1,0:T(8,128)(2,1)S(1)} %copy-done.22), channel_id=1, source_target_pairs={{0,8},{4,12},{8,0},{12,4},{16,24},{20,28},{24,16},{28,20},{1,9},{5... | collective-permute-start | bytes 811016 | tf_op jit(solution)/shard_map/ppermute | solution.py:554
  105.2 1.7 onward.6
  118.7 4.9 %collective-permute-done.11.refs_2_ = bf16[528,256]{1,0:T(8,128)(2,1)} collective-permute-done((bf16[528,256]{1,0:T(8,128)(2,1)}, bf16[528,256]{1,0:T(8,128)(2,1)}, u32[]{:S(2)}, u32[]{:S(2)}) %collective-permute-start.11) | collective-permute-done | bytes 270368 | tf_op jit(solution)/shard_map/ppermute | solution.py:554
  123.6 11.2 %collective-permute-done.13.refs_6_ = bf16[512,256]{1,0:T(8,128)(2,1)} collective-permute-done((bf16[512,256]{1,0:T(8,128)(2,1)}, bf16[512,256]{1,0:T(8,128)(2,1)}, u32[]{:S(2)}, u32[]{:S(2)}) %collective-permute-start.13) | collective-permute-done | bytes 262176 | tf_op jit(solution)/shard_map/ppermute | solution.py:554
  138.0 5.2 %scan.2 = (bf16[528,256]{1,0:T(8,128)(2,1)S(1)}, f32[144,256]{1,0:T(8,128)S(1)}) custom-call(s32[7]{0:T(128)S(1)} %stack.28.place_ref, f32[1]{0:T(128)} %bitcast.3.scale_ref, bf16[528,256]{1,0:T(8,128)(2,1)S(1)} %copy-done.18, bf16[528,256]{1,0:T(8,128)(2,1)} %collective-permute-done.8.refs_1_, bf16[528,256]{1,0:T(8,128)(2,1)} %collective-permute-done.11.refs_2_, ...), custom_call_target="tpu_custom_call" | custom-call | flops 134217728 | bytes 1048576 | tf_op jit(solution)/shard_map/scan/pallas_call | solution.py:493
  145.4 5.6 %scan.3 = (bf16[528,256]{1,0:T(8,128)(2,1)S(1)}, f32[144,256]{1,0:T(8,128)}) custom-call(s32[7]{0:T(128)S(1)} %stack.28.place_ref, f32[1]{0:T(128)} %bitcast.3.scale_ref, bf16[528,256]{1,0:T(8,128)(2,1)S(1)} %copy-done.4, bf16[528,256]{1,0:T(8,128)(2,1)S(1)} %collective-permute-done.29.refs_1_, bf16[528,256]{1,0:T(8,128)(2,1)} %collective-permute-done.32.refs_2_, ...), custom_call_target="tpu_custom_call" | custom-call | flops 134217728 | bytes 1048576 | tf_op jit(solution)/shard_map/scan/pallas_call | solution.py:493
  151.7 2.9 %collective-permute-start.36 = (bf16[528,256]{1,0:T(8,128)(2,1)S(1)}, bf16[528,256]{1,0:T(8,128)(2,1)S(1)}, u32[]{:S(2)}, u32[]{:S(2)}) collective-permute-start(bf16[528,256]{1,0:T(8,128)(2,1)S(1)} %get-tuple-element.53), channel_id=1, source_target_pairs={{0,8},{4,12},{8,0},{12,4},{16,24},{20,28},{24,16},{28,20},{1,9},{5... | collective-permute-start | bytes 811016 | tf_op jit(solution)/shard_map/ppermute | solution.py:554
  156.6 2.3 collective-permute-done.36
  159.7 8.7 %collective-permute-done.14 = bf16[528,256]{1,0:T(8,128)(2,1)S(1)} collective-permute-done((bf16[528,256]{1,0:T(8,128)(2,1)S(1)}, bf16[528,256]{1,0:T(8,128)(2,1)S(1)}, u32[]{:S(2)}, u32[]{:S(2)}) %collective-permute-start.14) | collective-permute-done | bytes 270368 | tf_op jit(solution)/shard_map/ppermute | solution.py:557
  174.4 6.0 %collective-permute-done.18 = bf16[528,256]{1,0:T(8,128)(2,1)S(1)} collective-permute-done((bf16[528,256]{1,0:T(8,128)(2,1)S(1)}, bf16[528,256]{1,0:T(8,128)(2,1)S(1)}, u32[]{:S(2)}, u32[]{:S(2)}) %collective-permute-start.18) | collective-permute-done | bytes 270368 | tf_op jit(solution)/shard_map/ppermute | solution.py:554
  182.1 7.7 %collective-permute-done.39 = bf16[528,256]{1,0:T(8,128)(2,1)S(1)} collective-permute-done((bf16[528,256]{1,0:T(8,128)(2,1)S(1)}, bf16[528,256]{1,0:T(8,128)(2,1)S(1)}, u32[]{:S(2)}, u32[]{:S(2)}) %collective-permute-start.39) | collective-permute-done | bytes 270368 | tf_op jit(solution)/shard_map/ppermute | solution.py:554
  195.5 5.1 %collective-permute-done.21 = bf16[528,256]{1,0:T(8,128)(2,1)S(1)} collective-permute-done((bf16[528,256]{1,0:T(8,128)(2,1)S(1)}, bf16[528,256]{1,0:T(8,128)(2,1)S(1)}, u32[]{:S(2)}, u32[]{:S(2)}) %collective-permute-start.21) | collective-permute-done | bytes 270368 | tf_op jit(solution)/shard_map/ppermute | solution.py:554
  201.6 1.9 collective-permute-done.42
  225.3 3.1 %collective-permute-done.24 = bf16[4,1,32,512]{3,2,1,0:T(8,128)(2,1)S(1)} collective-permute-done((bf16[4,1,32,512]{3,2,1,0:T(8,128)(2,1)S(1)}, bf16[4,1,32,512]{3,2,1,0:T(8,128)(2,1)S(1)}, u32[]{:S(2)}, u32[]{:S(2)}) %collective-permute-start.24) | collective-permute-done | bytes 131104 | tf_op jit(solution)/shard_map/ppermute | solution.py:672
  230.7 4.2 %all-to-all-start.1 = ((bf16[8,32,512]{2,1,0:T(8,128)(2,1)}), bf16[8,32,512]{2,1,0:T(8,128)(2,1)S(1)}, u32[]{:S(2)}, u32[]{:S(2)}) async-start(bf16[8,32,512]{2,1,0:T(8,128)(2,1)} %pad_maximum_fusion), calls=%async_computation.1 | async-start | bytes 524288 | tf_op jit(solution)/shard_map/all_to_all | solution.py:679
  236.3 6.9 %all-to-all-done.1 = bf16[8,32,512]{2,1,0:T(8,128)(2,1)S(1)} async-done(((bf16[8,32,512]{2,1,0:T(8,128)(2,1)}), bf16[8,32,512]{2,1,0:T(8,128)(2,1)S(1)}, u32[]{:S(2)}, u32[]{:S(2)}) %all-to-all-start.1) | async-done | bytes 262176 | tf_op jit(solution)/shard_map/all_to_all | solution.py:679
  (258 shorter events, 87.6 us)
Async XLA Ops:
  7.2 21.7 %all-to-all-start = ((bf16[8,32,1024]{2,1,0:T(8,128)(2,1)}), bf16[8,32,1024]{2,1,0:T(8,128)(2,1)S(1)}, u32[]{:S(2)}, u32[]{:S(2)}) async-start(bf16[8,32,1024]{2,1,0:T(8,128)(2,1)} %bitcast.7), calls=%async_computation | async-start | bytes 1048576 | tf_op jit(solution)/shard_map/all_to_all | solution.py:575
  14.4 36.8 %collective-permute-start.3 = (bf16[512,1024]{1,0:T(8,128)(2,1)}, bf16[512,1024]{1,0:T(8,128)(2,1)}, u32[]{:S(2)}, u32[]{:S(2)}) collective-permute-start(bf16[512,1024]{1,0:T(8,128)(2,1)} %constant_dynamic-slice_fusion.6), channel_id=1, source_target_pairs={{0,4},{4,0},{8,12},{12,8},{16,20},{20,16},{24,28},{28,24},{1,5},{5... | collective-permute-start | bytes 3145736 | tf_op jit(solution)/shard_map/ppermute | solution.py:557
  28.9 12.3 %collective-permute-start.1 = (bf16[8,32,1024]{2,1,0:T(8,128)(2,1)S(1)}, bf16[8,32,1024]{2,1,0:T(8,128)(2,1)S(1)}, u32[]{:S(2)}, u32[]{:S(2)}) collective-permute-start(bf16[8,32,1024]{2,1,0:T(8,128)(2,1)S(1)} %all-to-all-done.refs_0_), channel_id=1, source_target_pairs={{0,2},{1,3},{2,0},{3,1},{4,6},{5,7},{6,4},{7,5},{8,10},{9,11},{10,... | collective-permute-start | bytes 1572872 | tf_op jit(solution)/shard_map/ppermute | solution.py:578
  30.4 20.8 %collective-permute-start = (bf16[8,32,1024]{2,1,0:T(8,128)(2,1)S(1)}, bf16[8,32,1024]{2,1,0:T(8,128)(2,1)}, u32[]{:S(2)}, u32[]{:S(2)}) collective-permute-start(bf16[8,32,1024]{2,1,0:T(8,128)(2,1)S(1)} %all-to-all-done.refs_0_), channel_id=1, source_target_pairs={{0,1},{1,0},{2,3},{3,2},{4,5},{5,4},{6,7},{7,6},{8,9},{9,8},{10,11... | collective-permute-start | bytes 1572872 | tf_op jit(solution)/shard_map/ppermute | solution.py:578
  41.2 10.0 %collective-permute-start.2 = (bf16[8,32,1024]{2,1,0:T(8,128)(2,1)S(1)}, bf16[8,32,1024]{2,1,0:T(8,128)(2,1)}, u32[]{:S(2)}, u32[]{:S(2)}) collective-permute-start(bf16[8,32,1024]{2,1,0:T(8,128)(2,1)S(1)} %collective-permute-done.1.refs_2_), channel_id=1, source_target_pairs={{0,1},{1,0},{2,3},{3,2},{4,5},{5,4},{6,7},{7,6},{8,9},{9,8},{10,11... | collective-permute-start | bytes 1572872 | tf_op jit(solution)/shard_map/ppermute | solution.py:578
  60.5 18.1 %collective-permute-start.6 = (bf16[512,256]{1,0:T(8,128)(2,1)}, bf16[512,256]{1,0:T(8,128)(2,1)}, u32[]{:S(2)}, u32[]{:S(2)}) collective-permute-start(bf16[512,256]{1,0:T(8,128)(2,1)} %get-tuple-element.32), channel_id=1, source_target_pairs={{0,8},{4,12},{24,16},{28,20},{1,9},{5,13},{25,17},{29,21},{2,10},{... | collective-permute-start | bytes 786440 | tf_op jit(solution)/shard_map/ppermute | solution.py:554
  74.0 12.6 %collective-permute-start.10 = (bf16[528,256]{1,0:T(8,128)(2,1)}, bf16[528,256]{1,0:T(8,128)(2,1)S(1)}, u32[]{:S(2)}, u32[]{:S(2)}) collective-permute-start(bf16[528,256]{1,0:T(8,128)(2,1)} %copy-done.9), channel_id=1, source_target_pairs={{0,8},{4,12},{24,16},{28,20},{1,9},{5,13},{25,17},{29,21},{2,10},{... | collective-permute-start | bytes 811016 | tf_op jit(solution)/shard_map/ppermute | solution.py:554
  75.3 17.1 %collective-permute-start.9 = (bf16[528,256]{1,0:T(8,128)(2,1)}, bf16[528,256]{1,0:T(8,128)(2,1)S(1)}, u32[]{:S(2)}, u32[]{:S(2)}) collective-permute-start(bf16[528,256]{1,0:T(8,128)(2,1)} %copy-done.11), channel_id=1, source_target_pairs={{0,8},{4,12},{24,16},{28,20},{1,9},{5,13},{25,17},{29,21},{2,10},{... | collective-permute-start | bytes 811016 | tf_op jit(solution)/shard_map/ppermute | solution.py:554
  76.6 22.5 %collective-permute-start.31 = (bf16[528,256]{1,0:T(8,128)(2,1)}, bf16[528,256]{1,0:T(8,128)(2,1)}, u32[]{:S(2)}, u32[]{:S(2)}) collective-permute-start(bf16[528,256]{1,0:T(8,128)(2,1)} %copy-done.5), channel_id=1, source_target_pairs={{0,8},{4,12},{24,16},{28,20},{1,9},{5,13},{25,17},{29,21},{2,10},{... | collective-permute-start | bytes 811016 | tf_op jit(solution)/shard_map/ppermute | solution.py:554
  78.6 28.4 %collective-permute-start.30 = (bf16[528,256]{1,0:T(8,128)(2,1)}, bf16[528,256]{1,0:T(8,128)(2,1)}, u32[]{:S(2)}, u32[]{:S(2)}) collective-permute-start(bf16[528,256]{1,0:T(8,128)(2,1)} %copy-done.7), channel_id=1, source_target_pairs={{0,8},{4,12},{24,16},{28,20},{1,9},{5,13},{25,17},{29,21},{2,10},{... | collective-permute-start | bytes 811016 | tf_op jit(solution)/shard_map/ppermute | solution.py:554
  81.9 27.5 %collective-permute-start.7 = (bf16[512,256]{1,0:T(8,128)(2,1)S(1)}, bf16[512,256]{1,0:T(8,128)(2,1)S(1)}, u32[]{:S(2)}, u32[]{:S(2)}) collective-permute-start(bf16[512,256]{1,0:T(8,128)(2,1)S(1)} %add_convert_fusion.1.refs_4_), channel_id=1, source_target_pairs={{8,16},{12,20},{16,8},{20,12},{9,17},{13,21},{17,9},{21,13},{10,18... | collective-permute-start | bytes 786440 | tf_op jit(solution)/shard_map/ppermute | solution.py:554
  87.3 24.1 %collective-permute-start.8 = (bf16[528,256]{1,0:T(8,128)(2,1)}, bf16[528,256]{1,0:T(8,128)(2,1)}, u32[]{:S(2)}, u32[]{:S(2)}) collective-permute-start(bf16[528,256]{1,0:T(8,128)(2,1)} %copy-done.23), channel_id=1, source_target_pairs={{0,8},{4,12},{8,0},{12,4},{16,24},{20,28},{24,16},{28,20},{1,9},{5... | collective-permute-start | bytes 811016 | tf_op jit(solution)/shard_map/ppermute | solution.py:554
  93.1 19.7 %collective-permute-start.28 = (bf16[512,256]{1,0:T(8,128)(2,1)S(1)}, bf16[512,256]{1,0:T(8,128)(2,1)S(1)}, u32[]{:S(2)}, u32[]{:S(2)}) collective-permute-start(bf16[512,256]{1,0:T(8,128)(2,1)S(1)} %add_convert_fusion.refs_4_), channel_id=1, source_target_pairs={{8,16},{12,20},{16,8},{20,12},{9,17},{13,21},{17,9},{21,13},{10,18... | collective-permute-start | bytes 786440 | tf_op jit(solution)/shard_map/ppermute | solution.py:554
  99.2 15.8 %collective-permute-start.29 = (bf16[528,256]{1,0:T(8,128)(2,1)S(1)}, bf16[528,256]{1,0:T(8,128)(2,1)S(1)}, u32[]{:S(2)}, u32[]{:S(2)}) collective-permute-start(bf16[528,256]{1,0:T(8,128)(2,1)S(1)} %copy-done.22), channel_id=1, source_target_pairs={{0,8},{4,12},{8,0},{12,4},{16,24},{20,28},{24,16},{28,20},{1,9},{5... | collective-permute-start | bytes 811016 | tf_op jit(solution)/shard_map/ppermute | solution.py:554
  109.4 14.2 %collective-permute-start.11 = (bf16[528,256]{1,0:T(8,128)(2,1)}, bf16[528,256]{1,0:T(8,128)(2,1)}, u32[]{:S(2)}, u32[]{:S(2)}) collective-permute-start(bf16[528,256]{1,0:T(8,128)(2,1)} %onward.4), channel_id=1, source_target_pairs={{8,24},{12,28},{16,0},{20,4},{9,25},{13,29},{17,1},{21,5},{10,26},... | collective-permute-start | bytes 811016 | tf_op jit(solution)/shard_map/ppermute | solution.py:554
  111.5 33.9 %collective-permute-start.33 = (bf16[528,256]{1,0:T(8,128)(2,1)}, bf16[528,256]{1,0:T(8,128)(2,1)}, u32[]{:S(2)}, u32[]{:S(2)}) collective-permute-start(bf16[528,256]{1,0:T(8,128)(2,1)} %onward.7), channel_id=1, source_target_pairs={{8,16},{12,20},{16,8},{20,12},{9,17},{13,21},{17,9},{21,13},{10,18... | collective-permute-start | bytes 811016 | tf_op jit(solution)/shard_map/ppermute | solution.py:554
  112.9 32.6 %collective-permute-start.32 = (bf16[528,256]{1,0:T(8,128)(2,1)}, bf16[528,256]{1,0:T(8,128)(2,1)}, u32[]{:S(2)}, u32[]{:S(2)}) collective-permute-start(bf16[528,256]{1,0:T(8,128)(2,1)} %onward.6), channel_id=1, source_target_pairs={{8,24},{12,28},{16,0},{20,4},{9,25},{13,29},{17,1},{21,5},{10,26},... | collective-permute-start | bytes 811016 | tf_op jit(solution)/shard_map/ppermute | solution.py:554
  114.9 19.9 %collective-permute-start.13 = (bf16[512,256]{1,0:T(8,128)(2,1)}, bf16[512,256]{1,0:T(8,128)(2,1)}, u32[]{:S(2)}, u32[]{:S(2)}) collective-permute-start(bf16[512,256]{1,0:T(8,128)(2,1)} %multiply_convert_fusion.1), channel_id=1, source_target_pairs={{8,0},{12,4},{16,24},{20,28},{9,1},{13,5},{17,25},{21,29},{10,2},{... | collective-permute-start | bytes 786440 | tf_op jit(solution)/shard_map/ppermute | solution.py:554
  117.0 28.5 %collective-permute-start.34 = (bf16[512,256]{1,0:T(8,128)(2,1)}, bf16[512,256]{1,0:T(8,128)(2,1)}, u32[]{:S(2)}, u32[]{:S(2)}) collective-permute-start(bf16[512,256]{1,0:T(8,128)(2,1)} %multiply_convert_fusion), channel_id=1, source_target_pairs={{8,0},{12,4},{16,24},{20,28},{9,1},{13,5},{17,25},{21,29},{10,2},{... | collective-permute-start | bytes 786440 | tf_op jit(solution)/shard_map/ppermute | solution.py:554
  143.2 28.9 %collective-permute-start.17 = (bf16[528,256]{1,0:T(8,128)(2,1)S(1)}, bf16[528,256]{1,0:T(8,128)(2,1)S(1)}, u32[]{:S(2)}, u32[]{:S(2)}) collective-permute-start(bf16[528,256]{1,0:T(8,128)(2,1)S(1)} %get-tuple-element.41), channel_id=1, source_target_pairs={{8,16},{12,20},{16,8},{20,12},{9,17},{13,21},{17,9},{21,13},{10,18... | collective-permute-start | bytes 811016 | tf_op jit(solution)/shard_map/ppermute | solution.py:554
  144.1 11.4 %collective-permute-start.15 = (bf16[528,256]{1,0:T(8,128)(2,1)S(1)}, bf16[528,256]{1,0:T(8,128)(2,1)S(1)}, u32[]{:S(2)}, u32[]{:S(2)}) collective-permute-start(bf16[528,256]{1,0:T(8,128)(2,1)S(1)} %get-tuple-element.41), channel_id=1, source_target_pairs={{0,8},{4,12},{8,0},{12,4},{16,24},{20,28},{24,16},{28,20},{1,9},{5... | collective-permute-start | bytes 811016 | tf_op jit(solution)/shard_map/ppermute | solution.py:554
  151.0 23.0 %collective-permute-start.38 = (bf16[528,256]{1,0:T(8,128)(2,1)S(1)}, bf16[528,256]{1,0:T(8,128)(2,1)S(1)}, u32[]{:S(2)}, u32[]{:S(2)}) collective-permute-start(bf16[528,256]{1,0:T(8,128)(2,1)S(1)} %get-tuple-element.53), channel_id=1, source_target_pairs={{8,16},{12,20},{16,8},{20,12},{9,17},{13,21},{17,9},{21,13},{10,18... | collective-permute-start | bytes 811016 | tf_op jit(solution)/shard_map/ppermute | solution.py:554
  154.5 15.2 %collective-permute-start.35 = (bf16[528,256]{1,0:T(8,128)(2,1)S(1)}, bf16[528,256]{1,0:T(8,128)(2,1)S(1)}, u32[]{:S(2)}, u32[]{:S(2)}) collective-permute-start(bf16[528,256]{1,0:T(8,128)(2,1)S(1)} %get-tuple-element.53), channel_id=1, source_target_pairs={{0,4},{4,0},{8,12},{12,8},{16,20},{20,16},{24,28},{28,24},{1,5},{5... | collective-permute-start | bytes 811016 | tf_op jit(solution)/shard_map/ppermute | solution.py:557
  155.5 12.9 %collective-permute-start.14 = (bf16[528,256]{1,0:T(8,128)(2,1)S(1)}, bf16[528,256]{1,0:T(8,128)(2,1)S(1)}, u32[]{:S(2)}, u32[]{:S(2)}) collective-permute-start(bf16[528,256]{1,0:T(8,128)(2,1)S(1)} %get-tuple-element.41), channel_id=1, source_target_pairs={{0,4},{4,0},{8,12},{12,8},{16,20},{20,16},{24,28},{28,24},{1,5},{5... | collective-permute-start | bytes 811016 | tf_op jit(solution)/shard_map/ppermute | solution.py:557
  159.0 32.1 %collective-permute-start.20 = (bf16[528,256]{1,0:T(8,128)(2,1)S(1)}, bf16[528,256]{1,0:T(8,128)(2,1)S(1)}, u32[]{:S(2)}, u32[]{:S(2)}) collective-permute-start(bf16[528,256]{1,0:T(8,128)(2,1)S(1)} %collective-permute-done.15), channel_id=1, source_target_pairs={{8,16},{12,20},{16,8},{20,12},{9,17},{13,21},{17,9},{21,13},{10,18... | collective-permute-start | bytes 811016 | tf_op jit(solution)/shard_map/ppermute | solution.py:554
  168.4 23.9 %collective-permute-start.41 = (bf16[528,256]{1,0:T(8,128)(2,1)S(1)}, bf16[528,256]{1,0:T(8,128)(2,1)S(1)}, u32[]{:S(2)}, u32[]{:S(2)}) collective-permute-start(bf16[528,256]{1,0:T(8,128)(2,1)S(1)} %collective-permute-done.36), channel_id=1, source_target_pairs={{8,16},{12,20},{16,8},{20,12},{9,17},{13,21},{17,9},{21,13},{10,18... | collective-permute-start | bytes 811016 | tf_op jit(solution)/shard_map/ppermute | solution.py:554
  169.7 25.5 %collective-permute-start.37 = (bf16[528,256]{1,0:T(8,128)(2,1)S(1)}, bf16[528,256]{1,0:T(8,128)(2,1)S(1)}, u32[]{:S(2)}, u32[]{:S(2)}) collective-permute-start(bf16[528,256]{1,0:T(8,128)(2,1)S(1)} %collective-permute-done.36), channel_id=1, source_target_pairs={{0,4},{4,0},{8,12},{12,8},{16,20},{20,16},{24,28},{28,24},{1,5},{5... | collective-permute-start | bytes 811016 | tf_op jit(solution)/shard_map/ppermute | solution.py:557
  174.0 19.6 %collective-permute-start.16 = (bf16[528,256]{1,0:T(8,128)(2,1)S(1)}, bf16[528,256]{1,0:T(8,128)(2,1)S(1)}, u32[]{:S(2)}, u32[]{:S(2)}) collective-permute-start(bf16[528,256]{1,0:T(8,128)(2,1)S(1)} %collective-permute-done.15), channel_id=1, source_target_pairs={{0,4},{4,0},{8,12},{12,8},{16,20},{20,16},{24,28},{28,24},{1,5},{5... | collective-permute-start | bytes 811016 | tf_op jit(solution)/shard_map/ppermute | solution.py:557
  189.8 15.3 %collective-permute-start.19 = (bf16[528,256]{1,0:T(8,128)(2,1)S(1)}, bf16[528,256]{1,0:T(8,128)(2,1)S(1)}, u32[]{:S(2)}, u32[]{:S(2)}) collective-permute-start(bf16[528,256]{1,0:T(8,128)(2,1)S(1)} %broadcast_select_fusion.3), channel_id=1, source_target_pairs={{0,4},{4,0},{8,12},{12,8},{16,20},{20,16},{24,28},{28,24},{1,5},{5... | collective-permute-start | bytes 811016 | tf_op jit(solution)/shard_map/ppermute | solution.py:557
  191.1 14.4 %collective-permute-start.40 = (bf16[528,256]{1,0:T(8,128)(2,1)S(1)}, bf16[528,256]{1,0:T(8,128)(2,1)S(1)}, u32[]{:S(2)}, u32[]{:S(2)}) collective-permute-start(bf16[528,256]{1,0:T(8,128)(2,1)S(1)} %broadcast_select_fusion.1), channel_id=1, source_target_pairs={{0,4},{4,0},{8,12},{12,8},{16,20},{20,16},{24,28},{28,24},{1,5},{5... | collective-permute-start | bytes 811016 | tf_op jit(solution)/shard_map/ppermute | solution.py:557
  209.1 12.9 %collective-permute-start.23 = (bf16[4,2,32,512]{3,2,1,0:T(8,128)(2,1)}, bf16[4,2,32,512]{3,2,1,0:T(8,128)(2,1)S(1)}, u32[]{:S(2)}, u32[]{:S(2)}) collective-permute-start(bf16[4,2,32,512]{3,2,1,0:T(8,128)(2,1)} %fusion), channel_id=1, source_target_pairs={{0,1},{1,0},{2,3},{3,2},{4,5},{5,4},{6,7},{7,6},{8,9},{9,8},{10,11... | collective-permute-start | bytes 786440 | tf_op jit(solution)/shard_map/ppermute | solution.py:672
  230.7 12.5 %all-to-all-start.1 = ((bf16[8,32,512]{2,1,0:T(8,128)(2,1)}), bf16[8,32,512]{2,1,0:T(8,128)(2,1)S(1)}, u32[]{:S(2)}, u32[]{:S(2)}) async-start(bf16[8,32,512]{2,1,0:T(8,128)(2,1)} %pad_maximum_fusion), calls=%async_computation.1 | async-start | bytes 524288 | tf_op jit(solution)/shard_map/all_to_all | solution.py:679
  (59 other events, 579.1 us)
where the time goes:
time: 245 us; the launch traced here: 244 us
  waiting for transfers between devices  96.8 us (40%)
  starting transfers between devices  71.8 us (29%)
  local copies, waits for them, and re-layouts  31 us (13%)
  Pallas kernels  24.8 us (10%)
  other arithmetic  12.3 us (5%)
  matrix products  4.83 us (2%)
    ppermute x26, waiting for transfers between devices, along(): return lax.ppermute(value, 'seq', moves)  45 us
    ppermute x26, starting transfers between devices, along(): return lax.ppermute(value, 'seq', moves)  40.6 us
    unnamed x88, local copies, waits for them, and re-layouts  18.2 us
    ppermute x11, waiting for transfers between devices, across(): return lax.ppermute(value, 'seq', [(s, s ^ 1) for s in range(count)])  16.3 us
    all_to_all x1, waiting for transfers between devices, by_heads(): lax.all_to_all(pieces, 'seq', split_axis=0, concat_axis=0, tiled=True)  12.5 us
    ppermute x11, starting transfers between devices, across(): return lax.ppermute(value, 'seq', [(s, s ^ 1) for s in range(count)])  12.4 us
    ppermute x3, waiting for transfers between devices, by_heads(): lax.ppermute(rows[j - bit], 'tensor', [(t, t ^ bit) for t in range(ranks)])  10.8 us
    pallas_call x2, Pallas kernels, scan(): pl.pallas_call(functools.partial(scan_kernel, first), grid_spec=pltpu.Pre...  10.8 us
  transfers between devices with their start and end apart: 50, of which 19 were waited for; matrix products, arithmetic and copies ran while one was open for 10% of the time, Pallas kernels for 8%

commit v1 on v0

--- a/solution.py
+++ b/solution.py
@@ -176,7 +176,7 @@
 
 PAIR = 2
 LINE = 4
-PARTS = 2
+PARTS = 1
 ROWS = 8
 SMEM = pl.BlockSpec(memory_space=pltpu.SMEM)
 HIGHEST = lax.Precision.HIGHEST
@@ -209,13 +209,15 @@
     factor = factor_ref[0]
     depth = own_x.shape[0]
     largest = None
+    each = hidden[0].shape[0]
     for j in range(ranks):
-        for half in range(PAIR):
-            values = hidden[j][:, :, half * depth : (half + 1) * depth].astype(jnp.float32)
-            scaled = jnp.clip(values * factor, -quant_range, quant_range)
-            quant_ref[half, :, j] = scaled.astype(jnp.bfloat16)
-            top = jnp.max(jnp.abs(values).reshape(-1, ROWS, depth), axis=0)
-            largest = top if largest is None else jnp.maximum(largest, top)
+        for k in range(each):
+            for half in range(PAIR):
+                values = hidden[j][k, :, half * depth : (half + 1) * depth].astype(jnp.float32)
+                scaled = jnp.clip(values * factor, -quant_range, quant_range)
+                quant_ref[half, k ^ ((z * PAIR + side) % each), j] = scaled.astype(jnp.bfloat16)
+                top = jnp.max(jnp.abs(values).reshape(-1, ROWS, depth), axis=0)
+                largest = top if largest is None else jnp.maximum(largest, top)
     width = largest_ref.shape[1]
     top = largest[:, :width]
     for at in range(width, depth, width):
@@ -289,7 +291,8 @@
             num_scalar_prefetch=1,
             grid=(steps,),
             in_specs=[SMEM]
-            + [pl.BlockSpec((each, own, wide), lambda i, p: (first + i, 0, 0))] * ranks
+            + [pl.BlockSpec((each, own, wide), lambda i, p: ((first + i) ^ ((p[2] * PAIR + p[1]) // each), 0, 0))]
+            * ranks
             + [pl.BlockSpec((depth, x_wide), lambda i, p: (0, p[1]))]
             + [fixed(w) for w in weights[1:]],
             out_specs=[fixed(out) for out in outs],
@@ -569,10 +572,12 @@
     dt_own = pick(dt_rows, 0, side)
     dt_other = across(pick(dt_rows, 0, 1 - side))
 
-    pieces = hidden_in.reshape(own, LINE, 1, PAIR * depth).transpose(1, 2, 0, 3)
-    pieces = jnp.broadcast_to(pieces, (LINE, PAIR, own, PAIR * depth))
-    pieces = pieces.reshape(count, own, PAIR * depth)
-    rows = [lax.all_to_all(pieces, "seq", split_axis=0, concat_axis=0, tiled=True)]
+    cut = hidden_in.reshape(own, LINE, PAIR * depth)
+    pieces = [pick(cut, 1, z ^ m) for m in range(LINE)]
+    arrived = [pieces[0]]
+    for r in range(1, count):
+        arrived.append(lax.ppermute(pieces[r // PAIR], "seq", [(s, s ^ r) for s in range(count)]))
+    rows = [jnp.stack(arrived)]
     for j in range(1, ranks):
         bit = j & -j
         rows.append(lax.ppermute(rows[j - bit], "tensor", [(t, t ^ bit) for t in range(ranks)]))
@@ -645,10 +650,21 @@
         second = jnp.where(at_end, along(facing, outward), facing)
         third = jnp.where(at_end, along(beyond, outward), beyond)
         two, three = (jnp.where(at_end, 2, 3), jnp.where(at_end, 3, 2))
-        got = ((0, gained), (1, beside), (two, second), (three, third))
+        far_own = across(gained)
+        far_beside = across(beside)
+        second, far_own = lax.optimization_barrier((second, far_own))
+        far_second = across(second)
+        third, far_beside = lax.optimization_barrier((third, far_beside))
+        far_third = across(third)
+        got = (
+            (0, (gained, far_own)),
+            (1, (beside, far_beside)),
+            (two, (second, far_second)),
+            (three, (third, far_third)),
+        )
         total = squares = top = None
-        for m, block in got:
-            for x, piece in enumerate((block, across(block))):
+        for m, pair in got:
+            for x, piece in enumerate(pair):
                 at = ((side ^ x) * LINE + (z ^ m)) * channels
                 w_rows = lax.dynamic_slice_in_dim(w_out, at, channels, axis=0)
                 product = jnp.dot(piece, w_rows, preferred_element_type=f32)

time: 245 us -> 226 us (0.922)
  waiting for transfers between devices: 96.8 us -> 118 us
  starting transfers between devices: 71.8 us -> 54.1 us
  local copies, waits for them, and re-layouts: 31 us -> 16.8 us
  other arithmetic: 12.3 us -> 8.46 us
  Pallas kernels: 24.8 us -> 21.5 us
    ppermute x26 -> x13, starting transfers between devices: 40.6 us -> 19.5 us  [along(): return lax.ppermute(value, 'seq', moves)]
    ppermute x26 -> x13, waiting for transfers between devices: 45 us -> 62.9 us  [along(): return lax.ppermute(value, 'seq', moves)]
    ppermute x0 -> x7, starting transfers between devices: none -> 15.2 us  [by_heads(): lax.ppermute(pieces[r // PAIR], 'seq', [(s, s ^ r) for s in range(count)])]
    all_to_all x1 -> x0, waiting for transfers between devices: 12.5 us -> none  [by_heads(): lax.all_to_all(pieces, 'seq', split_axis=0, concat_axis=0, tiled=True)]
    unnamed x88 -> x47, local copies, waits for them, and re-layouts: 18.2 us -> 7.95 us
    ppermute x11 -> x7, waiting for transfers between devices: 16.3 us -> 26.2 us  [across(): return lax.ppermute(value, 'seq', [(s, s ^ 1) for s in range(count)])]
    ppermute x0 -> x7, waiting for transfers between devices: none -> 8.55 us  [by_heads(): lax.ppermute(pieces[r // PAIR], 'seq', [(s, s ^ r) for s in range(count)])]
    all_to_all x1 -> x0, starting transfers between devices: 7.25 us -> none  [by_heads(): lax.all_to_all(pieces, 'seq', split_axis=0, concat_axis=0, tiled=True)]
  transfers between devices with their start and end apart: 50 -> 35, of which waited for: 19 -> 18; matrix products, arithmetic and copies ran while one was open for 10% -> 6% of each run, Pallas kernels for 8% -> 2%
where the time goes in v1:
time: 226 us
  waiting for transfers between devices  118 us (52%)
  starting transfers between devices  54.1 us (24%)
  Pallas kernels  21.5 us (10%)
  local copies, waits for them, and re-layouts  16.8 us (7%)
  other arithmetic  8.46 us (4%)
  matrix products  4.54 us (2%)
    ppermute x13, waiting for transfers between devices, along(): return lax.ppermute(value, 'seq', moves)  62.9 us
    ppermute x7, waiting for transfers between devices, across(): return lax.ppermute(value, 'seq', [(s, s ^ 1) for s in range(count)])  26.2 us
    ppermute x13, starting transfers between devices, along(): return lax.ppermute(value, 'seq', moves)  19.5 us
    ppermute x7, starting transfers between devices, by_heads(): lax.ppermute(pieces[r // PAIR], 'seq', [(s, s ^ r) for s in range(count)])  15.2 us
    pallas_call x1, Pallas kernels, scan(): pl.pallas_call(functools.partial(scan_kernel, first), grid_spec=pltpu.Pre...  10.2 us
    ppermute x7, starting transfers between devices, across(): return lax.ppermute(value, 'seq', [(s, s ^ 1) for s in range(count)])  9.32 us
    ppermute x7, waiting for transfers between devices, by_heads(): lax.ppermute(pieces[r // PAIR], 'seq', [(s, s ^ r) for s in range(count)])  8.55 us
    unnamed x47, local copies, waits for them, and re-layouts  7.95 us
  transfers between devices with their start and end apart: 35, of which 18 were waited for; matrix products, arithmetic and copies ran while one was open for 6% of the time, Pallas kernels for 2%

profile of v1, /device:TPU:0, one launch (start us, length us, event | category | flops | bytes accessed | tf_op | source)
XLA Modules:
  0.0 225.5 jit_solution(14486166085169032404)
XLA Ops:
  0.7 2.3 %constant_dynamic-slice_fusion.1 = (bf16[512,1,2,128]{3,2,1,0:T(2,128)(2,1)}, bf16[512,1,2,128]{3,2,1,0:T(2,128)(2,1)S(1)}) fusion(bf16[512,2,2,128]{3,2,1,0:T(2,128)(2,1)} %param.18, s32[]{:T(128)S(6)} %select_n.125, s32[]{:T(128)S(6)} %select_n.120), kind=kLoop, calls=%fused_computation.76 | loop fusion | bytes 1048584 | tf_op jit(solution)/shard_map/jit(dynamic_index_in_dim)/dynamic_slice | solution.py:553
  3.7 2.3 %constant_dynamic-slice_fusion.7 = bf16[512,1024]{1,0:T(8,128)(2,1)} fusion(bf16[512,2048]{1,0:T(8,128)(2,1)} %refs_4_.1, s32[]{:T(128)S(6)} %select_n.119), kind=kLoop, calls=%fused_computation.82 | loop fusion | bytes 2097156 | tf_op jit(solution)/shard_map/dynamic_slice | solution.py:563
  6.8 3.1 %collective-permute-start.1 = (bf16[32,1024]{1,0:T(8,128)(2,1)S(1)}, bf16[32,1024]{1,0:T(8,128)(2,1)S(1)}, u32[]{:S(2)}, u32[]{:S(2)}) collective-permute-start(bf16[32,1024]{1,0:T(8,128)(2,1)S(1)} %bitcast.100), channel_id=1, source_target_pairs={{0,8},{4,12},{8,0},{12,4},{16,24},{20,28},{24,16},{28,20},{1,9},{5... | collective-permute-start | bytes 196616 | tf_op jit(solution)/shard_map/ppermute | solution.py:579
  11.3 2.7 %collective-permute-start.3 = (bf16[32,1024]{1,0:T(8,128)(2,1)S(1)}, bf16[32,1024]{1,0:T(8,128)(2,1)S(1)}, u32[]{:S(2)}, u32[]{:S(2)}) collective-permute-start(bf16[32,1024]{1,0:T(8,128)(2,1)S(1)} %bitcast.98), channel_id=1, source_target_pairs={{0,16},{4,20},{8,24},{12,28},{16,0},{20,4},{24,8},{28,12},{1,17},{... | collective-permute-start | bytes 196616 | tf_op jit(solution)/shard_map/ppermute | solution.py:579
  15.9 2.5 %collective-permute-done = bf16[32,1024]{1,0:T(8,128)(2,1)S(1)} collective-permute-done((bf16[32,1024]{1,0:T(8,128)(2,1)S(1)}, bf16[32,1024]{1,0:T(8,128)(2,1)S(1)}, u32[]{:S(2)}, u32[]{:S(2)}) %collective-permute-start) | collective-permute-done | bytes 65568 | tf_op jit(solution)/shard_map/ppermute | solution.py:579
  18.4 5.2 %collective-permute-start.5 = (bf16[32,1024]{1,0:T(8,128)(2,1)S(1)}, bf16[32,1024]{1,0:T(8,128)(2,1)S(1)}, u32[]{:S(2)}, u32[]{:S(2)}) collective-permute-start(bf16[32,1024]{1,0:T(8,128)(2,1)S(1)} %bitcast.102), channel_id=1, source_target_pairs={{0,24},{4,28},{8,16},{12,20},{16,8},{20,12},{24,0},{28,4},{1,25},{... | collective-permute-start | bytes 196616 | tf_op jit(solution)/shard_map/ppermute | solution.py:579
  24.7 1.9 collective-permute-done.5
  26.6 4.1 %collective-permute-done.6 = bf16[32,1024]{1,0:T(8,128)(2,1)S(1)} collective-permute-done((bf16[32,1024]{1,0:T(8,128)(2,1)S(1)}, bf16[32,1024]{1,0:T(8,128)(2,1)S(1)}, u32[]{:S(2)}, u32[]{:S(2)}) %collective-permute-start.6) | collective-permute-done | bytes 65568 | tf_op jit(solution)/shard_map/ppermute | solution.py:579
  33.7 6.1 %collective-permute-done.8.refs_2_ = bf16[8,32,1024]{2,1,0:T(8,128)(2,1)S(1)} collective-permute-done((bf16[8,32,1024]{2,1,0:T(8,128)(2,1)S(1)}, bf16[8,32,1024]{2,1,0:T(8,128)(2,1)S(1)}, u32[]{:S(2)}, u32[]{:S(2)}) %collective-permute-start.8) | collective-permute-done | bytes 524320 | tf_op jit(solution)/shard_map/ppermute | solution.py:583
  39.9 1.9 collective-permute-start.11
  43.8 15.6 %collective-permute-done.12.refs_9_ = bf16[32,512]{1,0:T(8,128)(2,1)S(1)} collective-permute-done((bf16[32,512]{1,0:T(8,128)(2,1)S(1)}, bf16[32,512]{1,0:T(8,128)(2,1)S(1)}, u32[]{:S(2)}, u32[]{:S(2)}) %collective-permute-start.12) | collective-permute-done | bytes 32800 | tf_op jit(solution)/shard_map/ppermute | solution.py:560
  61.1 7.0 %project.1 = (bf16[1056,256]{1,0:T(8,128)(2,1)S(1)}, bf16[1056,256]{1,0:T(8,128)(2,1)S(1)}, bf16[1056,256]{1,0:T(8,128)(2,1)}, bf16[1056,256]{1,0:T(8,128)(2,1)}...) custom-call(s32[7]{0:T(128)S(1)} %stack.55.place_ref, f32[1]{0:T(128)} %bitcast.4.factor_ref, ...), custom_call_target="tpu_custom_call" | custom-call | flops 2684354560 | bytes 4194304 | tf_op jit(solution)/shard_map/project/pallas_call | solution.py:288
  70.2 2.1 collective-permute-start.17
  72.3 2.1 collective-permute-start.16
  74.4 8.1 %collective-permute-done.13 = bf16[1024,256]{1,0:T(8,128)(2,1)S(1)} collective-permute-done((bf16[1024,256]{1,0:T(8,128)(2,1)S(1)}, bf16[1024,256]{1,0:T(8,128)(2,1)S(1)}, u32[]{:S(2)}, u32[]{:S(2)}) %collective-permute-start.13) | collective-permute-done | bytes 524320 | tf_op jit(solution)/shard_map/ppermute | solution.py:557
  83.7 3.7 %collective-permute-start.15 = (bf16[1056,256]{1,0:T(8,128)(2,1)}, bf16[1056,256]{1,0:T(8,128)(2,1)}, u32[]{:S(2)}, u32[]{:S(2)}) collective-permute-start(bf16[1056,256]{1,0:T(8,128)(2,1)} %copy-done.5), channel_id=1, source_target_pairs={{0,8},{4,12},{8,0},{12,4},{16,24},{20,28},{24,16},{28,20},{1,9},{5... | collective-permute-start | bytes 1622024 | tf_op jit(solution)/shard_map/ppermute | solution.py:557
  89.0 5.3 %collective-permute-done.17.received_ref = bf16[1056,256]{1,0:T(8,128)(2,1)} collective-permute-done((bf16[1056,256]{1,0:T(8,128)(2,1)}, bf16[1056,256]{1,0:T(8,128)(2,1)}, u32[]{:S(2)}, u32[]{:S(2)}) %collective-permute-start.17) | collective-permute-done | bytes 540704 | tf_op jit(solution)/shard_map/ppermute | solution.py:557
  94.2 2.1 onward.2
  96.4 9.2 %collective-permute-done.16.received_ref = bf16[1056,256]{1,0:T(8,128)(2,1)} collective-permute-done((bf16[1056,256]{1,0:T(8,128)(2,1)}, bf16[1056,256]{1,0:T(8,128)(2,1)}, u32[]{:S(2)}, u32[]{:S(2)}) %collective-permute-start.16) | collective-permute-done | bytes 540704 | tf_op jit(solution)/shard_map/ppermute | solution.py:557
  105.6 2.2 onward.3
  113.3 13.9 %collective-permute-done.18.refs_2_ = bf16[1056,256]{1,0:T(8,128)(2,1)} collective-permute-done((bf16[1056,256]{1,0:T(8,128)(2,1)}, bf16[1056,256]{1,0:T(8,128)(2,1)}, u32[]{:S(2)}, u32[]{:S(2)}) %collective-permute-start.18) | collective-permute-done | bytes 540704 | tf_op jit(solution)/shard_map/ppermute | solution.py:557
  127.2 4.3 %collective-permute-done.20.refs_6_ = bf16[1024,256]{1,0:T(8,128)(2,1)} collective-permute-done((bf16[1024,256]{1,0:T(8,128)(2,1)}, bf16[1024,256]{1,0:T(8,128)(2,1)}, u32[]{:S(2)}, u32[]{:S(2)}) %collective-permute-start.20) | collective-permute-done | bytes 524320 | tf_op jit(solution)/shard_map/ppermute | solution.py:557
  133.7 10.2 %scan.1 = (bf16[1040,256]{1,0:T(8,128)(2,1)}, f32[144,256]{1,0:T(8,128)}) custom-call(s32[7]{0:T(128)S(1)} %stack.55.place_ref, f32[1]{0:T(128)} %bitcast.3.scale_ref, bf16[1056,256]{1,0:T(8,128)(2,1)S(1)} %copy-done.3, bf16[1056,256]{1,0:T(8,128)(2,1)} %collective-permute-done.15.refs_1_, bf16[1056,256]{1,0:T(8,128)(2,1)} %collective-permute-done.18.refs_2_, ...), custom_call_target="tpu_custom_call" | custom-call | flops 268435456 | bytes 2097152 | tf_op jit(solution)/shard_map/scan/pallas_call | solution.py:496
  149.2 10.6 %collective-permute-done.24 = bf16[1040,256]{1,0:T(8,128)(2,1)S(1)} collective-permute-done((bf16[1040,256]{1,0:T(8,128)(2,1)}, bf16[1040,256]{1,0:T(8,128)(2,1)S(1)}, u32[]{:S(2)}, u32[]{:S(2)}) %collective-permute-start.24) | collective-permute-done | bytes 532512 | tf_op jit(solution)/shard_map/ppermute | solution.py:557
  162.5 3.8 %collective-permute-done.22 = bf16[1040,256]{1,0:T(8,128)(2,1)S(1)} collective-permute-done((bf16[1040,256]{1,0:T(8,128)(2,1)S(1)}, bf16[1040,256]{1,0:T(8,128)(2,1)S(1)}, u32[]{:S(2)}, u32[]{:S(2)}) %collective-permute-start.22) | collective-permute-done | bytes 532512 | tf_op jit(solution)/shard_map/ppermute | solution.py:557
  171.9 7.7 %collective-permute-done.26 = bf16[1040,256]{1,0:T(8,128)(2,1)S(1)} collective-permute-done((bf16[1040,256]{1,0:T(8,128)(2,1)S(1)}, bf16[1040,256]{1,0:T(8,128)(2,1)S(1)}, u32[]{:S(2)}, u32[]{:S(2)}) %collective-permute-start.26) | collective-permute-done | bytes 532512 | tf_op jit(solution)/shard_map/ppermute | solution.py:557
  181.7 4.5 %collective-permute-done.28 = bf16[1040,256]{1,0:T(8,128)(2,1)S(1)} collective-permute-done((bf16[1040,256]{1,0:T(8,128)(2,1)S(1)}, bf16[1040,256]{1,0:T(8,128)(2,1)S(1)}, u32[]{:S(2)}, u32[]{:S(2)}) %collective-permute-start.28) | collective-permute-done | bytes 532512 | tf_op jit(solution)/shard_map/ppermute | solution.py:560
  186.7 6.0 %collective-permute-done.29 = bf16[1040,256]{1,0:T(8,128)(2,1)S(1)} collective-permute-done((bf16[1040,256]{1,0:T(8,128)(2,1)S(1)}, bf16[1040,256]{1,0:T(8,128)(2,1)S(1)}, u32[]{:S(2)}, u32[]{:S(2)}) %collective-permute-start.29) | collective-permute-done | bytes 532512 | tf_op jit(solution)/shard_map/ppermute | solution.py:560
  193.1 1.8 slice_add_fusion
  203.5 5.5 %collective-permute-done.31 = bf16[8,1,32,512]{3,2,1,0:T(8,128)(2,1)} collective-permute-done((bf16[8,1,32,512]{3,2,1,0:T(8,128)(2,1)S(1)}, bf16[8,1,32,512]{3,2,1,0:T(8,128)(2,1)}, u32[]{:S(2)}, u32[]{:S(2)}) %collective-permute-start.31) | collective-permute-done | bytes 262176 | tf_op jit(solution)/shard_map/ppermute | solution.py:688
  210.7 5.9 %all-to-all-start = ((bf16[8,32,512]{2,1,0:T(8,128)(2,1)}), bf16[8,32,512]{2,1,0:T(8,128)(2,1)S(1)}, u32[]{:S(2)}, u32[]{:S(2)}) async-start(bf16[8,32,512]{2,1,0:T(8,128)(2,1)} %fusion.1), calls=%async_computation | async-start | bytes 524288 | tf_op jit(solution)/shard_map/all_to_all | solution.py:695
  217.2 7.6 %all-to-all-done = bf16[8,32,512]{2,1,0:T(8,128)(2,1)S(1)} async-done(((bf16[8,32,512]{2,1,0:T(8,128)(2,1)}), bf16[8,32,512]{2,1,0:T(8,128)(2,1)S(1)}, u32[]{:S(2)}, u32[]{:S(2)}) %all-to-all-start) | async-done | bytes 262176 | tf_op jit(solution)/shard_map/all_to_all | solution.py:695
  (147 shorter events, 52.4 us)
Async XLA Ops:
  6.8 16.8 %collective-permute-start.1 = (bf16[32,1024]{1,0:T(8,128)(2,1)S(1)}, bf16[32,1024]{1,0:T(8,128)(2,1)S(1)}, u32[]{:S(2)}, u32[]{:S(2)}) collective-permute-start(bf16[32,1024]{1,0:T(8,128)(2,1)S(1)} %bitcast.100), channel_id=1, source_target_pairs={{0,8},{4,12},{8,0},{12,4},{16,24},{20,28},{24,16},{28,20},{1,9},{5... | collective-permute-start | bytes 196616 | tf_op jit(solution)/shard_map/ppermute | solution.py:579
  9.9 14.8 %collective-permute-start.2 = (bf16[32,1024]{1,0:T(8,128)(2,1)S(1)}, bf16[32,1024]{1,0:T(8,128)(2,1)S(1)}, u32[]{:S(2)}, u32[]{:S(2)}) collective-permute-start(bf16[32,1024]{1,0:T(8,128)(2,1)S(1)} %bitcast.101), channel_id=1, source_target_pairs={{0,12},{4,8},{8,4},{12,0},{16,28},{20,24},{24,20},{28,16},{1,13},{... | collective-permute-start | bytes 196616 | tf_op jit(solution)/shard_map/ppermute | solution.py:579
  11.3 13.4 %collective-permute-start.3 = (bf16[32,1024]{1,0:T(8,128)(2,1)S(1)}, bf16[32,1024]{1,0:T(8,128)(2,1)S(1)}, u32[]{:S(2)}, u32[]{:S(2)}) collective-permute-start(bf16[32,1024]{1,0:T(8,128)(2,1)S(1)} %bitcast.98), channel_id=1, source_target_pairs={{0,16},{4,20},{8,24},{12,28},{16,0},{20,4},{24,8},{28,12},{1,17},{... | collective-permute-start | bytes 196616 | tf_op jit(solution)/shard_map/ppermute | solution.py:579
  13.9 10.7 %collective-permute-start.4 = (bf16[32,1024]{1,0:T(8,128)(2,1)S(1)}, bf16[32,1024]{1,0:T(8,128)(2,1)S(1)}, u32[]{:S(2)}, u32[]{:S(2)}) collective-permute-start(bf16[32,1024]{1,0:T(8,128)(2,1)S(1)} %bitcast.99), channel_id=1, source_target_pairs={{0,20},{4,16},{8,28},{12,24},{16,4},{20,0},{24,12},{28,8},{1,21},{... | collective-permute-start | bytes 196616 | tf_op jit(solution)/shard_map/ppermute | solution.py:579
  14.0 4.4 %collective-permute-start = (bf16[32,1024]{1,0:T(8,128)(2,1)S(1)}, bf16[32,1024]{1,0:T(8,128)(2,1)S(1)}, u32[]{:S(2)}, u32[]{:S(2)}) collective-permute-start(bf16[32,1024]{1,0:T(8,128)(2,1)S(1)} %bitcast.104), channel_id=1, source_target_pairs={{0,4},{4,0},{8,12},{12,8},{16,20},{20,16},{24,28},{28,24},{1,5},{5... | collective-permute-start | bytes 196616 | tf_op jit(solution)/shard_map/ppermute | solution.py:579
  18.4 8.2 %collective-permute-start.5 = (bf16[32,1024]{1,0:T(8,128)(2,1)S(1)}, bf16[32,1024]{1,0:T(8,128)(2,1)S(1)}, u32[]{:S(2)}, u32[]{:S(2)}) collective-permute-start(bf16[32,1024]{1,0:T(8,128)(2,1)S(1)} %bitcast.102), channel_id=1, source_target_pairs={{0,24},{4,28},{8,16},{12,20},{16,8},{20,12},{24,0},{28,4},{1,25},{... | collective-permute-start | bytes 196616 | tf_op jit(solution)/shard_map/ppermute | solution.py:579
  23.6 7.1 %collective-permute-start.6 = (bf16[32,1024]{1,0:T(8,128)(2,1)S(1)}, bf16[32,1024]{1,0:T(8,128)(2,1)S(1)}, u32[]{:S(2)}, u32[]{:S(2)}) collective-permute-start(bf16[32,1024]{1,0:T(8,128)(2,1)S(1)} %bitcast.103), channel_id=1, source_target_pairs={{0,28},{4,24},{8,20},{12,16},{16,12},{20,8},{24,4},{28,0},{1,29},{... | collective-permute-start | bytes 196616 | tf_op jit(solution)/shard_map/ppermute | solution.py:579
  30.7 9.2 %collective-permute-start.8 = (bf16[8,32,1024]{2,1,0:T(8,128)(2,1)S(1)}, bf16[8,32,1024]{2,1,0:T(8,128)(2,1)S(1)}, u32[]{:S(2)}, u32[]{:S(2)}) collective-permute-start(bf16[8,32,1024]{2,1,0:T(8,128)(2,1)S(1)} %bitcast_dynamic-update-slice_fusion.refs_0_), channel_id=1, source_target_pairs={{0,2},{1,3},{2,0},{3,1},{4,6},{5,7},{6,4},{7,5},{8,10},{9,11},{10,... | collective-permute-start | bytes 1572872 | tf_op jit(solution)/shard_map/ppermute | solution.py:583
  32.3 27.2 %collective-permute-start.10 = (bf16[512,1024]{1,0:T(8,128)(2,1)}, bf16[512,1024]{1,0:T(8,128)(2,1)}, u32[]{:S(2)}, u32[]{:S(2)}) collective-permute-start(bf16[512,1024]{1,0:T(8,128)(2,1)} %constant_dynamic-slice_fusion.7), channel_id=1, source_target_pairs={{0,4},{4,0},{8,12},{12,8},{16,20},{20,16},{24,28},{28,24},{1,5},{5... | collective-permute-start | bytes 3145736 | tf_op jit(solution)/shard_map/ppermute | solution.py:560
  33.7 25.7 %collective-permute-start.7 = (bf16[8,32,1024]{2,1,0:T(8,128)(2,1)S(1)}, bf16[8,32,1024]{2,1,0:T(8,128)(2,1)}, u32[]{:S(2)}, u32[]{:S(2)}) collective-permute-start(bf16[8,32,1024]{2,1,0:T(8,128)(2,1)S(1)} %bitcast_dynamic-update-slice_fusion.refs_0_), channel_id=1, source_target_pairs={{0,1},{1,0},{2,3},{3,2},{4,5},{5,4},{6,7},{7,6},{8,9},{9,8},{10,11... | collective-permute-start | bytes 1572872 | tf_op jit(solution)/shard_map/ppermute | solution.py:583
  39.9 19.6 %collective-permute-start.9 = (bf16[8,32,1024]{2,1,0:T(8,128)(2,1)S(1)}, bf16[8,32,1024]{2,1,0:T(8,128)(2,1)}, u32[]{:S(2)}, u32[]{:S(2)}) collective-permute-start(bf16[8,32,1024]{2,1,0:T(8,128)(2,1)S(1)} %collective-permute-done.8.refs_2_), channel_id=1, source_target_pairs={{0,1},{1,0},{2,3},{3,2},{4,5},{5,4},{6,7},{7,6},{8,9},{9,8},{10,11... | collective-permute-start | bytes 1572872 | tf_op jit(solution)/shard_map/ppermute | solution.py:583
  39.9 19.6 %collective-permute-start.11 = (bf16[512,256]{1,0:T(8,128)(2,1)}, bf16[512,256]{1,0:T(8,128)(2,1)}, u32[]{:S(2)}, u32[]{:S(2)}) collective-permute-start(bf16[512,256]{1,0:T(8,128)(2,1)} %bitcast.83), channel_id=1, source_target_pairs={{0,4},{4,0},{8,12},{12,8},{16,20},{20,16},{24,28},{28,24},{1,5},{5... | collective-permute-start | bytes 786440 | tf_op jit(solution)/shard_map/ppermute | solution.py:560
  41.8 17.6 %collective-permute-start.12 = (bf16[32,512]{1,0:T(8,128)(2,1)S(1)}, bf16[32,512]{1,0:T(8,128)(2,1)S(1)}, u32[]{:S(2)}, u32[]{:S(2)}) collective-permute-start(bf16[32,512]{1,0:T(8,128)(2,1)S(1)} %get-tuple-element.44), channel_id=1, source_target_pairs={{0,4},{4,0},{8,12},{12,8},{16,20},{20,16},{24,28},{28,24},{1,5},{5... | collective-permute-start | bytes 98312 | tf_op jit(solution)/shard_map/ppermute | solution.py:560
  68.9 13.6 %collective-permute-start.13 = (bf16[1024,256]{1,0:T(8,128)(2,1)S(1)}, bf16[1024,256]{1,0:T(8,128)(2,1)S(1)}, u32[]{:S(2)}, u32[]{:S(2)}) collective-permute-start(bf16[1024,256]{1,0:T(8,128)(2,1)S(1)} %get-tuple-element.24), channel_id=1, source_target_pairs={{0,8},{4,12},{24,16},{28,20},{1,9},{5,13},{25,17},{29,21},{2,10},{... | collective-permute-start | bytes 1572872 | tf_op jit(solution)/shard_map/ppermute | solution.py:557
  70.2 24.0 %collective-permute-start.17 = (bf16[1056,256]{1,0:T(8,128)(2,1)}, bf16[1056,256]{1,0:T(8,128)(2,1)}, u32[]{:S(2)}, u32[]{:S(2)}) collective-permute-start(bf16[1056,256]{1,0:T(8,128)(2,1)} %get-tuple-element.28.own_ref), channel_id=1, source_target_pairs={{0,8},{4,12},{24,16},{28,20},{1,9},{5,13},{25,17},{29,21},{2,10},{... | collective-permute-start | bytes 1622024 | tf_op jit(solution)/shard_map/ppermute | solution.py:557
  72.3 33.3 %collective-permute-start.16 = (bf16[1056,256]{1,0:T(8,128)(2,1)}, bf16[1056,256]{1,0:T(8,128)(2,1)}, u32[]{:S(2)}, u32[]{:S(2)}) collective-permute-start(bf16[1056,256]{1,0:T(8,128)(2,1)} %get-tuple-element.27.own_ref), channel_id=1, source_target_pairs={{0,8},{4,12},{24,16},{28,20},{1,9},{5,13},{25,17},{29,21},{2,10},{... | collective-permute-start | bytes 1622024 | tf_op jit(solution)/shard_map/ppermute | solution.py:557
  82.7 27.8 %collective-permute-start.14 = (bf16[1024,256]{1,0:T(8,128)(2,1)S(1)}, bf16[1024,256]{1,0:T(8,128)(2,1)S(1)}, u32[]{:S(2)}, u32[]{:S(2)}) collective-permute-start(bf16[1024,256]{1,0:T(8,128)(2,1)S(1)} %add_convert_fusion.refs_4_), channel_id=1, source_target_pairs={{8,16},{12,20},{16,8},{20,12},{9,17},{13,21},{17,9},{21,13},{10,18... | collective-permute-start | bytes 1572872 | tf_op jit(solution)/shard_map/ppermute | solution.py:557
  83.7 27.8 %collective-permute-start.15 = (bf16[1056,256]{1,0:T(8,128)(2,1)}, bf16[1056,256]{1,0:T(8,128)(2,1)}, u32[]{:S(2)}, u32[]{:S(2)}) collective-permute-start(bf16[1056,256]{1,0:T(8,128)(2,1)} %copy-done.5), channel_id=1, source_target_pairs={{0,8},{4,12},{8,0},{12,4},{16,24},{20,28},{24,16},{28,20},{1,9},{5... | collective-permute-start | bytes 1622024 | tf_op jit(solution)/shard_map/ppermute | solution.py:557
  107.8 5.5 %collective-permute-start.19 = (bf16[1056,256]{1,0:T(8,128)(2,1)}, bf16[1056,256]{1,0:T(8,128)(2,1)}, u32[]{:S(2)}, u32[]{:S(2)}) collective-permute-start(bf16[1056,256]{1,0:T(8,128)(2,1)} %onward.3), channel_id=1, source_target_pairs={{8,16},{12,20},{16,8},{20,12},{9,17},{13,21},{17,9},{21,13},{10,18... | collective-permute-start | bytes 1622024 | tf_op jit(solution)/shard_map/ppermute | solution.py:557
  109.2 17.9 %collective-permute-start.18 = (bf16[1056,256]{1,0:T(8,128)(2,1)}, bf16[1056,256]{1,0:T(8,128)(2,1)}, u32[]{:S(2)}, u32[]{:S(2)}) collective-permute-start(bf16[1056,256]{1,0:T(8,128)(2,1)} %onward.2), channel_id=1, source_target_pairs={{8,24},{12,28},{16,0},{20,4},{9,25},{13,29},{17,1},{21,5},{10,26},... | collective-permute-start | bytes 1622024 | tf_op jit(solution)/shard_map/ppermute | solution.py:557
  111.5 19.9 %collective-permute-start.20 = (bf16[1024,256]{1,0:T(8,128)(2,1)}, bf16[1024,256]{1,0:T(8,128)(2,1)}, u32[]{:S(2)}, u32[]{:S(2)}) collective-permute-start(bf16[1024,256]{1,0:T(8,128)(2,1)} %multiply_convert_fusion), channel_id=1, source_target_pairs={{8,0},{12,4},{16,24},{20,28},{9,1},{13,5},{17,25},{21,29},{10,2},{... | collective-permute-start | bytes 1572872 | tf_op jit(solution)/shard_map/ppermute | solution.py:557
  144.6 15.3 %collective-permute-start.24 = (bf16[1040,256]{1,0:T(8,128)(2,1)}, bf16[1040,256]{1,0:T(8,128)(2,1)S(1)}, u32[]{:S(2)}, u32[]{:S(2)}) collective-permute-start(bf16[1040,256]{1,0:T(8,128)(2,1)} %get-tuple-element.33), channel_id=1, source_target_pairs={{0,8},{4,12},{8,0},{12,4},{16,24},{20,28},{24,16},{28,20},{1,9},{5... | collective-permute-start | bytes 1597448 | tf_op jit(solution)/shard_map/ppermute | solution.py:557
  145.7 20.7 %collective-permute-start.23 = (bf16[1040,256]{1,0:T(8,128)(2,1)}, bf16[1040,256]{1,0:T(8,128)(2,1)S(1)}, u32[]{:S(2)}, u32[]{:S(2)}) collective-permute-start(bf16[1040,256]{1,0:T(8,128)(2,1)} %get-tuple-element.33), channel_id=1, source_target_pairs={{0,4},{4,0},{8,12},{12,8},{16,20},{20,16},{24,28},{28,24},{1,5},{5... | collective-permute-start | bytes 1597448 | tf_op jit(solution)/shard_map/ppermute | solution.py:560
  147.2 19.1 %collective-permute-start.22 = (bf16[1040,256]{1,0:T(8,128)(2,1)S(1)}, bf16[1040,256]{1,0:T(8,128)(2,1)S(1)}, u32[]{:S(2)}, u32[]{:S(2)}) collective-permute-start(bf16[1040,256]{1,0:T(8,128)(2,1)S(1)} %collective-permute-done.21), channel_id=1, source_target_pairs={{8,0},{12,4},{16,24},{20,28},{9,1},{13,5},{17,25},{21,29},{10,2},{... | collective-permute-start | bytes 1597448 | tf_op jit(solution)/shard_map/ppermute | solution.py:557
  159.9 8.5 %collective-permute-start.25 = (bf16[1040,256]{1,0:T(8,128)(2,1)S(1)}, bf16[1040,256]{1,0:T(8,128)(2,1)S(1)}, u32[]{:S(2)}, u32[]{:S(2)}) collective-permute-start(bf16[1040,256]{1,0:T(8,128)(2,1)S(1)} %collective-permute-done.24), channel_id=1, source_target_pairs={{8,16},{12,20},{16,8},{20,12},{9,17},{13,21},{17,9},{21,13},{10,18... | collective-permute-start | bytes 1597448 | tf_op jit(solution)/shard_map/ppermute | solution.py:557
  160.6 19.1 %collective-permute-start.27 = (bf16[1040,256]{1,0:T(8,128)(2,1)S(1)}, bf16[1040,256]{1,0:T(8,128)(2,1)S(1)}, u32[]{:S(2)}, u32[]{:S(2)}) collective-permute-start(bf16[1040,256]{1,0:T(8,128)(2,1)S(1)} %collective-permute-done.24), channel_id=1, source_target_pairs={{0,4},{4,0},{8,12},{12,8},{16,20},{20,16},{24,28},{28,24},{1,5},{5... | collective-permute-start | bytes 1597448 | tf_op jit(solution)/shard_map/ppermute | solution.py:560
  166.4 19.8 %collective-permute-start.28 = (bf16[1040,256]{1,0:T(8,128)(2,1)S(1)}, bf16[1040,256]{1,0:T(8,128)(2,1)S(1)}, u32[]{:S(2)}, u32[]{:S(2)}) collective-permute-start(bf16[1040,256]{1,0:T(8,128)(2,1)S(1)} %broadcast_select_fusion.1), channel_id=1, source_target_pairs={{0,4},{4,0},{8,12},{12,8},{16,20},{20,16},{24,28},{28,24},{1,5},{5... | collective-permute-start | bytes 1597448 | tf_op jit(solution)/shard_map/ppermute | solution.py:560
  168.4 11.2 %collective-permute-start.26 = (bf16[1040,256]{1,0:T(8,128)(2,1)S(1)}, bf16[1040,256]{1,0:T(8,128)(2,1)S(1)}, u32[]{:S(2)}, u32[]{:S(2)}) collective-permute-start(bf16[1040,256]{1,0:T(8,128)(2,1)S(1)} %collective-permute-done.25), channel_id=1, source_target_pairs={{8,0},{12,4},{16,24},{20,28},{9,1},{13,5},{17,25},{21,29},{10,2},{... | collective-permute-start | bytes 1597448 | tf_op jit(solution)/shard_map/ppermute | solution.py:557
  179.6 13.1 %collective-permute-start.29 = (bf16[1040,256]{1,0:T(8,128)(2,1)S(1)}, bf16[1040,256]{1,0:T(8,128)(2,1)S(1)}, u32[]{:S(2)}, u32[]{:S(2)}) collective-permute-start(bf16[1040,256]{1,0:T(8,128)(2,1)S(1)} %broadcast_select_fusion), channel_id=1, source_target_pairs={{0,4},{4,0},{8,12},{12,8},{16,20},{20,16},{24,28},{28,24},{1,5},{5... | collective-permute-start | bytes 1597448 | tf_op jit(solution)/shard_map/ppermute | solution.py:560
  198.4 3.7 %collective-permute-start.33 = (f32[8,128]{1,0:T(8,128)S(1)}, f32[8,128]{1,0:T(8,128)S(1)}, u32[]{:S(2)}, u32[]{:S(2)}) collective-permute-start(f32[8,128]{1,0:T(8,128)S(1)} %add.268), channel_id=1, source_target_pairs={{0,2},{1,3},{2,0},{3,1},{4,6},{5,7},{6,4},{7,5},{8,10},{9,11},{10,... | collective-permute-start | bytes 12296 | tf_op jit(solution)/shard_map/ppermute | solution.py:685
  200.7 8.2 %collective-permute-start.31 = (bf16[8,1,32,512]{3,2,1,0:T(8,128)(2,1)S(1)}, bf16[8,1,32,512]{3,2,1,0:T(8,128)(2,1)}, u32[]{:S(2)}, u32[]{:S(2)}) collective-permute-start(bf16[8,1,32,512]{3,2,1,0:T(8,128)(2,1)S(1)} %dynamic-slice_convert_fusion.1), channel_id=1, source_target_pairs={{0,2},{1,3},{2,0},{3,1},{4,6},{5,7},{6,4},{7,5},{8,10},{9,11},{10,... | collective-permute-start | bytes 786440 | tf_op jit(solution)/shard_map/ppermute | solution.py:688
  210.7 14.1 %all-to-all-start = ((bf16[8,32,512]{2,1,0:T(8,128)(2,1)}), bf16[8,32,512]{2,1,0:T(8,128)(2,1)S(1)}, u32[]{:S(2)}, u32[]{:S(2)}) async-start(bf16[8,32,512]{2,1,0:T(8,128)(2,1)} %fusion.1), calls=%async_computation | async-start | bytes 524288 | tf_op jit(solution)/shard_map/all_to_all | solution.py:695
  (18 other events, 369.2 us)

commit v2 on v0

--- a/solution.py
+++ b/solution.py
@@ -176,7 +176,6 @@
 
 PAIR = 2
 LINE = 4
-PARTS = 2
 ROWS = 8
 SMEM = pl.BlockSpec(memory_space=pltpu.SMEM)
 HIGHEST = lax.Precision.HIGHEST
@@ -197,25 +196,30 @@
     )
 
 
-def project_kernel(place_ref, factor_ref, *refs):
-    outs = LINE + 4
-    ranks = len(refs) - 6 - outs
-    hidden = refs[:ranks]
-    own_x, other_x, own_bc, other_bc, own_dt, other_dt = refs[ranks : ranks + 6]
-    x_refs = refs[ranks + 6 : ranks + 6 + LINE]
-    bc_ref, largest_ref, quant_ref, dt_buf = refs[ranks + 6 + LINE :]
+def project_kernel(ranks, place_ref, factor_ref, *refs):
+    hidden = [refs[x * ranks : (x + 1) * ranks] for x in range(PAIR)]
+    refs = refs[PAIR * ranks :]
+    own_x, other_x = (refs[0], refs[1 : 1 + LINE])
+    own_bc, other_bc, own_dt, other_dt = refs[1 + LINE : 5 + LINE]
+    x_refs = refs[5 + LINE : 5 + 2 * LINE]
+    bc_ref, largest_ref, quant_ref, dt_buf = refs[5 + 2 * LINE :]
     side, z = (place_ref[1], place_ref[2])
     step = pl.program_id(0)
     factor = factor_ref[0]
     depth = own_x.shape[0]
     largest = None
-    for j in range(ranks):
-        for half in range(PAIR):
-            values = hidden[j][:, :, half * depth : (half + 1) * depth].astype(jnp.float32)
-            scaled = jnp.clip(values * factor, -quant_range, quant_range)
-            quant_ref[half, :, j] = scaled.astype(jnp.bfloat16)
-            top = jnp.max(jnp.abs(values).reshape(-1, ROWS, depth), axis=0)
-            largest = top if largest is None else jnp.maximum(largest, top)
+    each = hidden[0][0].shape[0]
+    for x in range(PAIR):
+        for k in range(each):
+            block = (k ^ (z % each)) * PAIR + (side ^ x)
+            for j in range(ranks):
+                for half in range(PAIR):
+                    cut = slice(half * depth, (half + 1) * depth)
+                    values = hidden[x][j][k, :, cut].astype(jnp.float32)
+                    scaled = jnp.clip(values * factor, -quant_range, quant_range)
+                    quant_ref[half, block, j] = scaled.astype(jnp.bfloat16)
+                    top = jnp.max(jnp.abs(values).reshape(-1, ROWS, depth), axis=0)
+                    largest = top if largest is None else jnp.maximum(largest, top)
     width = largest_ref.shape[1]
     top = largest[:, :width]
     for at in range(width, depth, width):
@@ -239,7 +243,7 @@
         )
 
     at_rows = pl.ds(pl.multiple_of(step * rows, rows), rows)
-    dt_buf[...] = (nt_dot(own_dt[...], near) + nt_dot(other_dt[...], far)).reshape(dt_buf.shape)
+    dt_buf[...] = both(own_dt[...], other_dt[...]).T[: LINE * ROWS].reshape(dt_buf.shape)
     channels = x_refs[0].shape[1]
     tokens = pl.num_programs(0) * rows
     extra = rows // channels * ROWS
@@ -247,7 +251,7 @@
     for m in reversed(range(LINE)):
         owner = z ^ m
         cut = pl.ds(pl.multiple_of(owner * channels, channels), channels)
-        x_refs[m][at_rows] = both(own_x[:, cut], other_x[:, cut]).astype(jnp.bfloat16)
+        x_refs[m][at_rows] = both(own_x[:, cut], other_x[m][...]).astype(jnp.bfloat16)
         dt = dt_buf[owner]
         pieces = [
             split_parts(dt[:, at : at + channels], upper) for at in range(0, rows, channels)
@@ -263,50 +267,49 @@
     return jnp.where(upper, top, values - top)
 
 
-def project(place, factor, hidden, weights, part):
-    count, own, wide = hidden[0].shape
-    ranks = len(hidden)
-    w_x, other_x = weights[:2]
-    depth, x_wide = other_x.shape
-    channels = x_wide // LINE
-    here = count // PARTS
-    steps = max(1, 2 // PARTS)
-    each = here // steps
-    tokens = here * ranks * own
+def project(place, factor, hidden, w_x, weights):
+    line, own, wide = hidden[0].shape
+    ranks = len(hidden) // PAIR
+    depth, channels = weights[0].shape
+    maps_wide = weights[LINE].shape[1]
+    x_wide = channels * LINE
+    steps = 2
+    each = line // steps
+    tokens = line * PAIR * ranks * own
     extra = tokens // channels * ROWS
 
     def fixed(array):
         return pl.BlockSpec(array.shape, lambda i, p: (0,) * array.ndim)
 
     payload = jax.ShapeDtypeStruct((tokens + extra, channels), jnp.bfloat16)
-    maps = jax.ShapeDtypeStruct((tokens, weights[2].shape[1]), jnp.bfloat16)
+    maps = jax.ShapeDtypeStruct((tokens, maps_wide), jnp.bfloat16)
     largest = jax.ShapeDtypeStruct((ROWS, 128), jnp.float32)
     outs = [payload] * LINE + [maps, largest]
-    first = part * steps
+    rows_of = pl.BlockSpec((each, own, wide), lambda i, p: (i ^ (p[2] // each), 0, 0))
     return pl.pallas_call(
-        project_kernel,
+        functools.partial(project_kernel, ranks),
         grid_spec=pltpu.PrefetchScalarGridSpec(
             num_scalar_prefetch=1,
             grid=(steps,),
             in_specs=[SMEM]
-            + [pl.BlockSpec((each, own, wide), lambda i, p: (first + i, 0, 0))] * ranks
+            + [rows_of] * (PAIR * ranks)
             + [pl.BlockSpec((depth, x_wide), lambda i, p: (0, p[1]))]
-            + [fixed(w) for w in weights[1:]],
+            + [fixed(w) for w in weights],
             out_specs=[fixed(out) for out in outs],
             scratch_shapes=[
-                pltpu.VMEM((PAIR, each, ranks, own, depth), jnp.bfloat16),
-                pltpu.VMEM((LINE, ROWS, each * ranks * own), jnp.float32),
+                pltpu.VMEM((PAIR, each * PAIR, ranks, own, depth), jnp.bfloat16),
+                pltpu.VMEM((LINE, ROWS, tokens // steps), jnp.float32),
             ],
         ),
         out_shape=outs,
-        compiler_params=pltpu.CompilerParams(vmem_limit_bytes=40 * 2**20),
+        compiler_params=pltpu.CompilerParams(vmem_limit_bytes=26 * 2**20),
         cost_estimate=pl.CostEstimate(
-            flops=2 * tokens * wide * (x_wide + maps.shape[1]),
+            flops=2 * tokens * wide * (x_wide + maps_wide),
             bytes_accessed=2 * tokens * (wide + x_wide),
             transcendentals=0,
         ),
         name="project",
-    )(place, factor, *hidden, *weights)
+    )(place, factor, *hidden, w_x, *weights)
 
 
 def onward_kernel(own_ref, received_ref, out_ref):
@@ -330,7 +333,7 @@
         in_specs=[whole, whole],
         out_specs=whole,
         out_shape=jax.ShapeDtypeStruct(own.shape, own.dtype),
-        compiler_params=pltpu.CompilerParams(vmem_limit_bytes=20 * 2**20),
+        compiler_params=pltpu.CompilerParams(vmem_limit_bytes=8 * 2**20),
         cost_estimate=pl.CostEstimate(
             flops=own.size, bytes_accessed=6 * own.size, transcendentals=0
         ),
@@ -505,7 +508,7 @@
             ],
         ),
         out_shape=outs,
-        compiler_params=pltpu.CompilerParams(vmem_limit_bytes=40 * 2**20),
+        compiler_params=pltpu.CompilerParams(vmem_limit_bytes=20 * 2**20),
         cost_estimate=pl.CostEstimate(
             flops=8 * tokens * SPAN * channels,
             bytes_accessed=8 * tokens * channels,
@@ -556,26 +559,44 @@
     def across(value):
         return lax.ppermute(value, "seq", [(s, s ^ 1) for s in range(count)])
 
-    half = w_x.shape[1] // PAIR
-    x_send = lax.dynamic_slice_in_dim(w_x, (1 - side) * half, half, axis=1)
+    other_side = (1 - side) * LINE
+    sent = [
+        lax.dynamic_slice_in_dim(w_x, (other_side + (z ^ m)) * channels, channels, axis=1)
+        for m in reversed(range(LINE))
+    ]
+    sent[0], hidden_in = lax.optimization_barrier((sent[0], hidden_in))
+    maps_sent = pick(w_bc, 1, 1 - side).reshape(depth, 2 * STATE)
+    sent.insert(LINE // 2, maps_sent)
+    swapped = []
+    for value in sent:
+        if swapped:
+            swapped[-1], value = lax.optimization_barrier((swapped[-1], value))
+        swapped.append(across(value))
+    bc_other = swapped.pop(LINE // 2)
+    swapped.reverse()
     bc_own = pick(w_bc, 1, side).reshape(depth, 2 * STATE)
-    bc_send = pick(w_bc, 1, 1 - side).reshape(depth, 2 * STATE)
-    x_send, bc_send, hidden_in = lax.optimization_barrier((x_send, bc_send, hidden_in))
-    x_other = across(x_send)
-    bc_other = across(bc_send)
-    dt_rows = w_dt.T.reshape(PAIR, LINE, 1, heads_here, depth)
-    dt_rows = jnp.broadcast_to(dt_rows, (PAIR, LINE, ROWS // heads_here, heads_here, depth))
-    dt_rows = dt_rows.reshape(PAIR, LINE * ROWS, depth)
-    dt_own = pick(dt_rows, 0, side)
-    dt_other = across(pick(dt_rows, 0, 1 - side))
-
-    pieces = hidden_in.reshape(own, LINE, 1, PAIR * depth).transpose(1, 2, 0, 3)
-    pieces = jnp.broadcast_to(pieces, (LINE, PAIR, own, PAIR * depth))
-    pieces = pieces.reshape(count, own, PAIR * depth)
-    rows = [lax.all_to_all(pieces, "seq", split_axis=0, concat_axis=0, tiled=True)]
-    for j in range(1, ranks):
-        bit = j & -j
-        rows.append(lax.ppermute(rows[j - bit], "tensor", [(t, t ^ bit) for t in range(ranks)]))
+    dt_columns = w_dt.reshape(depth, PAIR, LINE, 1, heads_here)
+    dt_columns = jnp.broadcast_to(
+        dt_columns, (depth, PAIR, LINE, ROWS // heads_here, heads_here)
+    ).reshape(depth, PAIR, LINE * ROWS)
+    dt_columns = jnp.pad(dt_columns, ((0, 0), (0, 0), (0, SPAN - LINE * ROWS)))
+    dt_own = pick(dt_columns, 1, side)
+    dt_other = across(pick(dt_columns, 1, 1 - side))
+
+    cut = hidden_in.reshape(own, LINE, PAIR * depth)
+    pieces = [pick(cut, 1, z ^ m) for m in range(LINE)]
+    arrived = [pieces[0]]
+    for m in range(1, LINE):
+        arrived.append(along(pieces[m], [(s, s ^ m) for s in range(LINE)]))
+    stacked = jnp.stack(arrived)
+    rows = []
+    for mine in (stacked, across(stacked)):
+        ours = [mine]
+        for j in range(1, ranks):
+            bit = j & -j
+            pairs = [(t, t ^ bit) for t in range(ranks)]
+            ours.append(lax.ppermute(ours[j - bit], "tensor", pairs))
+        rows.extend(ours)
 
     def of_heads(array):
         return jnp.repeat(array, HEAD_DIM)[None]
@@ -608,77 +629,99 @@
     start, end = (0, LINE - 1)
     at_end = (z == start) | (z == end)
     next_start, next_end = (1, LINE - 2)
-    weights = (w_x, x_other, bc_own, bc_other, dt_own, dt_other)
+    weights = (*swapped, bc_own, bc_other, dt_own, dt_other)
     carry = init_state.reshape(-1, STATE)
-    totals, tops = ([], [])
-    for part in range(PARTS):
-        mine, near, over, far, maps, largest = project(place, factor, rows, weights, part)
-        map_hop = along(maps, [(start, next_start), (end, next_end)])
-        hop_far = along(far, [(start, next_start), (end, next_end)])
-        hop_over = along(over, [(start, next_start), (end, next_end)])
-        got_near = along(near, [(s, s ^ 1) for s in range(LINE)])
-        map_sum = (maps.astype(f32) + map_hop.astype(f32)).astype(bf16)
-        map_far = along(map_sum, [(next_start, next_end), (next_end, next_start)])
-        map_done = ((map_sum.astype(f32) + map_far.astype(f32)) * in_scale).astype(bf16)
-        map_done, got_near = lax.optimization_barrier((map_done, got_near))
-        map_done = along(map_done, [(next_start, start), (next_end, end)])
-        sent_end = onward(over, hop_far)
-        hop_over, sent_end = lax.optimization_barrier((hop_over, sent_end))
-        got_end = along(sent_end, [(next_start, end), (next_end, start)])
-        got_next = along(onward(far, hop_over), [(next_start, next_end), (next_end, next_start)])
-        gained, carry = scan(
-            place,
-            in_scale,
-            [mine, got_near, got_end, got_next],
-            [map_sum, map_far, map_done],
-            small,
-            largest,
-            carry,
-            part == 0,
-        )
-        tokens = gained.shape[0] - 2 * ROWS
-        beside = along(gained, [(s, s ^ 1) for s in range(LINE)])
-        middle = [(next_start, next_end), (next_end, next_start)]
-        outward = [(next_start, start), (next_end, end)]
-        facing = along(gained, middle)
-        beyond = along(beside, middle)
-        second = jnp.where(at_end, along(facing, outward), facing)
-        third = jnp.where(at_end, along(beyond, outward), beyond)
-        two, three = (jnp.where(at_end, 2, 3), jnp.where(at_end, 3, 2))
-        got = ((0, gained), (1, beside), (two, second), (three, third))
-        total = squares = top = None
-        for m, block in got:
-            for x, piece in enumerate((block, across(block))):
-                at = ((side ^ x) * LINE + (z ^ m)) * channels
-                w_rows = lax.dynamic_slice_in_dim(w_out, at, channels, axis=0)
-                product = jnp.dot(piece, w_rows, preferred_element_type=f32)
-                tail = piece[tokens:].astype(f32)
-                low, high = (tail[:ROWS, :SPAN] + tail[:ROWS, SPAN:], tail[ROWS:, :SPAN])
-                if total is None:
-                    total, squares, top = (product, low, high)
-                else:
-                    total = total + product
-                    squares = squares + low
-                    top = jnp.maximum(top, high)
-        tops.append(top)
-        wide = w_out.shape[1]
-        blocks = tokens // SPAN
-        kept = total[:tokens].reshape(blocks, ranks, own, wide)
-        for bit in (1 << b for b in range(ranks.bit_length() - 1)):
-            pairs = [(t, t ^ bit) for t in range(ranks)]
-            squares = squares + lax.ppermute(squares, "tensor", pairs)
-            keeps = (rank // bit) % 2
-            halves = kept.reshape(blocks, -1, 2, own, wide)
-            received = lax.ppermute(pick(halves, 2, 1 - keeps).astype(bf16), "tensor", pairs)
-            kept = pick(halves, 2, keeps) + received.astype(f32)
-        kept = kept.reshape(blocks, own, wide)
-        mean_sq = squares[:blocks].reshape(blocks, ranks, own) / (HEADS * HEAD_DIM)
-        factors = lax.rsqrt(pick(mean_sq, 1, rank) + epsilon)
-        totals.append((kept * factors[:, :, None]).astype(bf16))
-    final = jnp.concatenate(totals, axis=0)
-    final = lax.all_to_all(final, "seq", split_axis=0, concat_axis=0, tiled=True)
-    layer_out = final.transpose(1, 0, 2).reshape(own, count * final.shape[2])
-    abs_max = jnp.max(functools.reduce(jnp.maximum, tops))
+    mine, near, over, far, maps, largest = project(place, factor, rows, w_x, weights)
+    map_hop = along(maps, [(start, next_start), (end, next_end)])
+    hop_far = along(far, [(start, next_start), (end, next_end)])
+    hop_over = along(over, [(start, next_start), (end, next_end)])
+    got_near = along(near, [(s, s ^ 1) for s in range(LINE)])
+    map_sum = (maps.astype(f32) + map_hop.astype(f32)).astype(bf16)
+    map_far = along(map_sum, [(next_start, next_end), (next_end, next_start)])
+    map_done = ((map_sum.astype(f32) + map_far.astype(f32)) * in_scale).astype(bf16)
+    sent_end = onward(over, hop_far)
+    hop_over, unused = lax.optimization_barrier((hop_over, sent_end))
+    got_end = along(sent_end, [(next_start, end), (next_end, start)])
+    map_done, got_near, got_end = lax.optimization_barrier((map_done, got_near, got_end))
+    map_done = along(map_done, [(next_start, start), (next_end, end)])
+    got_next = along(onward(far, hop_over), [(next_start, next_end), (next_end, next_start)])
+    gained, carry = scan(
+        place,
+        in_scale,
+        [mine, got_near, got_end, got_next],
+        [map_sum, map_far, map_done],
+        small,
+        largest,
+        carry,
+        True,
+    )
+    tokens = gained.shape[0] - 2 * ROWS
+    beside = along(gained, [(s, s ^ 1) for s in range(LINE)])
+    middle = [(next_start, next_end), (next_end, next_start)]
+    outward = [(next_start, start), (next_end, end)]
+    facing = along(gained, middle)
+    beyond = along(beside, middle)
+    second = jnp.where(at_end, along(facing, outward), facing)
+    third = jnp.where(at_end, along(beyond, outward), beyond)
+    two, three = (jnp.where(at_end, 2, 3), jnp.where(at_end, 3, 2))
+    far_own = across(gained)
+    far_beside = across(beside)
+    second, far_own = lax.optimization_barrier((second, far_own))
+    far_second = across(second)
+    third, far_beside = lax.optimization_barrier((third, far_beside))
+    far_third = across(third)
+    got = (
+        (0, (gained, far_own)),
+        (1, (beside, far_beside)),
+        (two, (second, far_second)),
+        (three, (third, far_third)),
+    )
+    total = squares = top = None
+    for m, pair in got:
+        for x, piece in enumerate(pair):
+            at = ((side ^ x) * LINE + (z ^ m)) * channels
+            w_rows = lax.dynamic_slice_in_dim(w_out, at, channels, axis=0)
+            product = jnp.dot(piece, w_rows, preferred_element_type=f32)
+            tail = piece[tokens:].astype(f32)
+            low, high = (tail[:ROWS, :SPAN] + tail[:ROWS, SPAN:], tail[ROWS:, :SPAN])
+            if total is None:
+                total, squares, top = (product, low, high)
+            else:
+                total = total + product
+                squares = squares + low
+                top = jnp.maximum(top, high)
+    wide = w_out.shape[1]
+    squares = squares + lax.ppermute(squares, "tensor", [(t, t ^ 1) for t in range(ranks)])
+    pairs = ranks // 2
+    kept = total[:tokens].reshape(count, pairs, 2, own, wide)
+    nearest = rank % 2
+    received = lax.ppermute(
+        pick(kept, 2, 1 - nearest).astype(bf16), "tensor", [(t, t ^ 1) for t in range(ranks)]
+    )
+    kept = (pick(kept, 2, nearest) + received.astype(f32)).astype(bf16)
+    groups = [
+        [s * ranks + t for s in range(count) for t in range(c, ranks, 2)] for c in range(2)
+    ]
+    final = lax.all_to_all(
+        kept.reshape(count * pairs, own, wide),
+        ("seq", "tensor"),
+        split_axis=0,
+        concat_axis=0,
+        axis_index_groups=groups,
+        tiled=True,
+    )
+    bit = 2
+    while bit < ranks:
+        swap = [(t, t ^ bit) for t in range(ranks)]
+        squares = squares + lax.ppermute(squares, "tensor", swap)
+        bit *= 2
+    mean_sq = squares.reshape(count, ranks, own) / (HEADS * HEAD_DIM)
+    factors = lax.rsqrt(lax.dynamic_slice_in_dim(mean_sq, here, 1)[0] + epsilon)
+    factors = pick(factors, 0, rank)[:, None, None]
+    final = jnp.sum(final.reshape(count, pairs, own, wide).astype(f32), axis=1)
+    final = final.transpose(1, 0, 2) * factors
+    layer_out = final.astype(bf16).reshape(own, count * wide)
+    abs_max = jnp.max(top)
     return (layer_out, abs_max)
 
 

time: 245 us -> 223 us (0.910)
  local copies, waits for them, and re-layouts: 31 us -> 19.7 us
  starting transfers between devices: 71.8 us -> 61.2 us
  waiting for transfers between devices: 96.8 us -> 103 us
  Pallas kernels: 24.8 us -> 21.7 us
    ppermute x26 -> x16, waiting for transfers between devices: 45 us -> 64 us  [along(): return lax.ppermute(value, 'seq', moves)]
    ppermute x11 -> x9, waiting for transfers between devices: 16.1 us -> 3.42 us  [the longest x1 1.18 us: by_heads(): lax.ppermute(pick(kept, 2, 1 - nearest).astype(bf16), 'tensor', [(t, t ^...]
    unnamed x88 -> x46, local copies, waits for them, and re-layouts: 18.2 us -> 7.71 us
    ppermute x26 -> x16, starting transfers between devices: 40.6 us -> 30.6 us  [along(): return lax.ppermute(value, 'seq', moves)]
    all_to_all x2 -> x1, waiting for transfers between devices: 19.4 us -> 9.74 us  [by_heads(): lax.all_to_all(kept.reshape(count * pairs, own, wide), ('seq', 'tensor'),...]
    ppermute x11, waiting for transfers between devices: 16.3 us -> 25.4 us  [across(): return lax.ppermute(value, 'seq', [(s, s ^ 1) for s in range(count)])]
    div x2 -> x1, local copies, waits for them, and re-layouts: 2.69 us -> 0.08 us  [by_heads(): mean_sq = squares.reshape(count, ranks, own) / (HEADS * HEAD_DIM)]
    dynamic_slice x2 -> x5, local copies, waits for them, and re-layouts: 3.05 us -> 5.61 us  [pick(): return lax.dynamic_index_in_dim(array, index, axis, keepdims=False)]
  transfers between devices with their start and end apart: 50 -> 37, of which waited for: 19 -> 23; matrix products, arithmetic and copies ran while one was open for 10% -> 10% of each run, Pallas kernels for 8% -> 2%
where the time goes in v2:
time: 223 us; the launch traced here: 222 us
  waiting for transfers between devices  103 us (46%)
  starting transfers between devices  61.2 us (27%)
  Pallas kernels  21.7 us (10%)
  local copies, waits for them, and re-layouts  19.7 us (9%)
  other arithmetic  10.1 us (5%)
  matrix products  4.55 us (2%)
    ppermute x16, waiting for transfers between devices, along(): return lax.ppermute(value, 'seq', moves)  64 us
    ppermute x16, starting transfers between devices, along(): return lax.ppermute(value, 'seq', moves)  30.6 us
    ppermute x11, waiting for transfers between devices, across(): return lax.ppermute(value, 'seq', [(s, s ^ 1) for s in range(count)])  25.4 us
    ppermute x11, starting transfers between devices, across(): return lax.ppermute(value, 'seq', [(s, s ^ 1) for s in range(count)])  12.5 us
    all_to_all x1, starting transfers between devices, by_heads(): lax.all_to_all(kept.reshape(count * pairs, own, wide), ('seq', 'tensor'),...  12.4 us
    pallas_call x1, Pallas kernels, scan(): pl.pallas_call(functools.partial(scan_kernel, first), grid_spec=pltpu.Pre...  10.2 us
    all_to_all x1, waiting for transfers between devices, by_heads(): lax.all_to_all(kept.reshape(count * pairs, own, wide), ('seq', 'tensor'),...  9.74 us
    unnamed x46, local copies, waits for them, and re-layouts  7.71 us
  transfers between devices with their start and end apart: 37, of which 23 were waited for; matrix products, arithmetic and copies ran while one was open for 10% of the time, Pallas kernels for 2%

profile of v2, /device:TPU:0, one launch (start us, length us, event | category | flops | bytes accessed | tf_op | source)
XLA Modules:
  0.0 221.8 jit_solution(3336078466518171264)
XLA Ops:
  0.7 2.3 %constant_dynamic-slice_fusion.3 = (bf16[512,256]{1,0:T(8,128)(2,1)}, bf16[512,256]{1,0:T(8,128)(2,1)}, bf16[512,256]{1,0:T(8,128)(2,1)}, bf16[512,256]{1,0:T(8,128)(2,1)S(1)}) fusion(bf16[512,2048]{1,0:T(8,128)(2,1)} %refs_8_.1, s32[]{:T(128)S(6)} %select_n.124, s32[]{:T(128)S(6)} %select_n.123, s32[]{:T(128)S(6)} %select_n.121, s32[]{:T(128)S(6)} %select_n.116), kind=kLoop, calls=%fused_computation.72 | loop fusion | bytes 2097168 | tf_op jit(solution)/shard_map/dynamic_slice | solution.py:564
  3.0 2.9 %collective-permute-start.10 = (bf16[512,256]{1,0:T(8,128)(2,1)S(1)}, bf16[512,256]{1,0:T(8,128)(2,1)S(1)}, u32[]{:S(2)}, u32[]{:S(2)}) collective-permute-start(bf16[512,256]{1,0:T(8,128)(2,1)S(1)} %get-tuple-element.28), channel_id=1, source_target_pairs={{0,4},{4,0},{8,12},{12,8},{16,20},{20,16},{24,28},{28,24},{1,5},{5... | collective-permute-start | bytes 786440 | tf_op jit(solution)/shard_map/ppermute | solution.py:560
  7.1 5.1 %collective-permute-done.10.refs_12_ = bf16[512,256]{1,0:T(8,128)(2,1)S(1)} collective-permute-done((bf16[512,256]{1,0:T(8,128)(2,1)S(1)}, bf16[512,256]{1,0:T(8,128)(2,1)S(1)}, u32[]{:S(2)}, u32[]{:S(2)}) %collective-permute-start.10) | collective-permute-done | bytes 262176 | tf_op jit(solution)/shard_map/ppermute | solution.py:560
  12.2 1.7 collective-permute-start.11
  14.5 3.7 %collective-permute-start.2 = (bf16[32,1024]{1,0:T(8,128)(2,1)S(1)}, bf16[32,1024]{1,0:T(8,128)(2,1)S(1)}, u32[]{:S(2)}, u32[]{:S(2)}) collective-permute-start(bf16[32,1024]{1,0:T(8,128)(2,1)S(1)} %bitcast.93), channel_id=1, source_target_pairs={{0,24},{4,28},{8,16},{12,20},{16,8},{20,12},{24,0},{28,4},{1,25},{... | collective-permute-start | bytes 196616 | tf_op jit(solution)/shard_map/ppermute | solution.py:557
  20.7 1.9 collective-permute-done
  28.2 5.1 %collective-permute-done.6.refs_4_ = bf16[4,32,1024]{2,1,0:T(8,128)(2,1)S(1)} collective-permute-done((bf16[4,32,1024]{2,1,0:T(8,128)(2,1)S(1)}, bf16[4,32,1024]{2,1,0:T(8,128)(2,1)S(1)}, u32[]{:S(2)}, u32[]{:S(2)}) %collective-permute-start.6) | collective-permute-done | bytes 262176 | tf_op jit(solution)/shard_map/ppermute | solution.py:560
  44.1 1.8 collective-permute-done.15.refs_16_
  50.4 2.8 %collective-permute-done.14.refs_9_ = bf16[512,256]{1,0:T(8,128)(2,1)} collective-permute-done((bf16[512,256]{1,0:T(8,128)(2,1)}, bf16[512,256]{1,0:T(8,128)(2,1)}, u32[]{:S(2)}, u32[]{:S(2)}) %collective-permute-start.14) | collective-permute-done | bytes 262176 | tf_op jit(solution)/shard_map/ppermute | solution.py:560
  56.6 7.2 %project.1 = (bf16[1056,256]{1,0:T(8,128)(2,1)S(1)}, bf16[1056,256]{1,0:T(8,128)(2,1)S(1)}, bf16[1056,256]{1,0:T(8,128)(2,1)}, bf16[1056,256]{1,0:T(8,128)(2,1)}...) custom-call(s32[7]{0:T(128)S(1)} %stack.43.place_ref, f32[1]{0:T(128)} %bitcast.4.factor_ref, ...), custom_call_target="tpu_custom_call" | custom-call | flops 2684354560 | bytes 4194304 | tf_op jit(solution)/shard_map/project/pallas_call | solution.py:289
  64.7 3.5 %collective-permute-start.16 = (bf16[1024,256]{1,0:T(8,128)(2,1)S(1)}, bf16[1024,256]{1,0:T(8,128)(2,1)S(1)}, u32[]{:S(2)}, u32[]{:S(2)}) collective-permute-start(bf16[1024,256]{1,0:T(8,128)(2,1)S(1)} %get-tuple-element.38), channel_id=1, source_target_pairs={{0,8},{4,12},{24,16},{28,20},{1,9},{5,13},{25,17},{29,21},{2,10},{... | collective-permute-start | bytes 1572872 | tf_op jit(solution)/shard_map/ppermute | solution.py:557
  68.2 2.1 collective-permute-start.19
  70.3 2.1 collective-permute-start.21
  72.4 8.1 %collective-permute-done.16 = bf16[1024,256]{1,0:T(8,128)(2,1)S(1)} collective-permute-done((bf16[1024,256]{1,0:T(8,128)(2,1)S(1)}, bf16[1024,256]{1,0:T(8,128)(2,1)S(1)}, u32[]{:S(2)}, u32[]{:S(2)}) %collective-permute-start.16) | collective-permute-done | bytes 524320 | tf_op jit(solution)/shard_map/ppermute | solution.py:557
  84.4 4.2 %collective-permute-start.18 = (bf16[1056,256]{1,0:T(8,128)(2,1)}, bf16[1056,256]{1,0:T(8,128)(2,1)}, u32[]{:S(2)}, u32[]{:S(2)}) collective-permute-start(bf16[1056,256]{1,0:T(8,128)(2,1)} %copy-done.5), channel_id=1, source_target_pairs={{0,8},{4,12},{8,0},{12,4},{16,24},{20,28},{24,16},{28,20},{1,9},{5... | collective-permute-start | bytes 1622024 | tf_op jit(solution)/shard_map/ppermute | solution.py:557
  88.6 3.6 %collective-permute-done.19.received_ref = bf16[1056,256]{1,0:T(8,128)(2,1)} collective-permute-done((bf16[1056,256]{1,0:T(8,128)(2,1)}, bf16[1056,256]{1,0:T(8,128)(2,1)}, u32[]{:S(2)}, u32[]{:S(2)}) %collective-permute-start.19) | collective-permute-done | bytes 540704 | tf_op jit(solution)/shard_map/ppermute | solution.py:557
  92.2 2.1 onward.2
  95.9 7.9 %collective-permute-done.21.received_ref = bf16[1056,256]{1,0:T(8,128)(2,1)} collective-permute-done((bf16[1056,256]{1,0:T(8,128)(2,1)}, bf16[1056,256]{1,0:T(8,128)(2,1)}, u32[]{:S(2)}, u32[]{:S(2)}) %collective-permute-start.21) | collective-permute-done | bytes 540704 | tf_op jit(solution)/shard_map/ppermute | solution.py:557
  103.8 2.1 onward.3
  108.4 2.5 %collective-permute-done.18.refs_1_ = bf16[1056,256]{1,0:T(8,128)(2,1)} collective-permute-done((bf16[1056,256]{1,0:T(8,128)(2,1)}, bf16[1056,256]{1,0:T(8,128)(2,1)}, u32[]{:S(2)}, u32[]{:S(2)}) %collective-permute-start.18) | collective-permute-done | bytes 540704 | tf_op jit(solution)/shard_map/ppermute | solution.py:557
  112.7 10.0 %collective-permute-done.23.refs_6_ = bf16[1024,256]{1,0:T(8,128)(2,1)} collective-permute-done((bf16[1024,256]{1,0:T(8,128)(2,1)}, bf16[1024,256]{1,0:T(8,128)(2,1)}, u32[]{:S(2)}, u32[]{:S(2)}) %collective-permute-start.23) | collective-permute-done | bytes 524320 | tf_op jit(solution)/shard_map/ppermute | solution.py:557
  125.0 10.2 %scan.1 = (bf16[1040,256]{1,0:T(8,128)(2,1)}, f32[144,256]{1,0:T(8,128)}) custom-call(s32[7]{0:T(128)S(1)} %stack.43.place_ref, f32[1]{0:T(128)} %bitcast.3.scale_ref, bf16[1056,256]{1,0:T(8,128)(2,1)S(1)} %copy-done.3, bf16[1056,256]{1,0:T(8,128)(2,1)} %collective-permute-done.18.refs_1_, bf16[1056,256]{1,0:T(8,128)(2,1)} %collective-permute-done.20.refs_2_, ...), custom_call_target="tpu_custom_call" | custom-call | flops 268435456 | bytes 2097152 | tf_op jit(solution)/shard_map/scan/pallas_call | solution.py:496
  136.7 4.4 %collective-permute-start.27 = (bf16[1040,256]{1,0:T(8,128)(2,1)}, bf16[1040,256]{1,0:T(8,128)(2,1)S(1)}, u32[]{:S(2)}, u32[]{:S(2)}) collective-permute-start(bf16[1040,256]{1,0:T(8,128)(2,1)} %get-tuple-element.47), channel_id=1, source_target_pairs={{0,8},{4,12},{8,0},{12,4},{16,24},{20,28},{24,16},{28,20},{1,9},{5... | collective-permute-start | bytes 1597448 | tf_op jit(solution)/shard_map/ppermute | solution.py:557
  143.1 8.1 %collective-permute-done.27 = bf16[1040,256]{1,0:T(8,128)(2,1)S(1)} collective-permute-done((bf16[1040,256]{1,0:T(8,128)(2,1)}, bf16[1040,256]{1,0:T(8,128)(2,1)S(1)}, u32[]{:S(2)}, u32[]{:S(2)}) %collective-permute-start.27) | collective-permute-done | bytes 532512 | tf_op jit(solution)/shard_map/ppermute | solution.py:557
  152.5 9.0 %collective-permute-done.25 = bf16[1040,256]{1,0:T(8,128)(2,1)S(1)} collective-permute-done((bf16[1040,256]{1,0:T(8,128)(2,1)}, bf16[1040,256]{1,0:T(8,128)(2,1)S(1)}, u32[]{:S(2)}, u32[]{:S(2)}) %collective-permute-start.25) | collective-permute-done | bytes 532512 | tf_op jit(solution)/shard_map/ppermute | solution.py:557
  165.3 11.3 %collective-permute-done.29 = bf16[1040,256]{1,0:T(8,128)(2,1)S(1)} collective-permute-done((bf16[1040,256]{1,0:T(8,128)(2,1)S(1)}, bf16[1040,256]{1,0:T(8,128)(2,1)S(1)}, u32[]{:S(2)}, u32[]{:S(2)}) %collective-permute-start.29) | collective-permute-done | bytes 532512 | tf_op jit(solution)/shard_map/ppermute | solution.py:557
  176.7 2.1 collective-permute-start.32
  180.7 7.0 %collective-permute-done.32 = bf16[1040,256]{1,0:T(8,128)(2,1)S(1)} collective-permute-done((bf16[1040,256]{1,0:T(8,128)(2,1)S(1)}, bf16[1040,256]{1,0:T(8,128)(2,1)S(1)}, u32[]{:S(2)}, u32[]{:S(2)}) %collective-permute-start.32) | collective-permute-done | bytes 532512 | tf_op jit(solution)/shard_map/ppermute | solution.py:560
  188.2 1.8 slice_add_fusion
  193.1 12.4 %all-to-all-start = ((bf16[16,32,512]{2,1,0:T(8,128)(2,1)}), bf16[16,32,512]{2,1,0:T(8,128)(2,1)S(1)}, u32[]{:S(2)}, u32[]{:S(2)}) async-start(bf16[16,32,512]{2,1,0:T(8,128)(2,1)} %bitcast.23), calls=%async_computation | async-start | bytes 1048576 | tf_op jit(solution)/shard_map/all_to_all | solution.py:705
  207.4 1.9 collective-permute-start.35
  211.2 9.7 %all-to-all-done = bf16[16,32,512]{2,1,0:T(8,128)(2,1)S(1)} async-done(((bf16[16,32,512]{2,1,0:T(8,128)(2,1)}), bf16[16,32,512]{2,1,0:T(8,128)(2,1)S(1)}, u32[]{:S(2)}, u32[]{:S(2)}) %all-to-all-start) | async-done | bytes 524320 | tf_op jit(solution)/shard_map/all_to_all | solution.py:705
  (153 shorter events, 58.7 us)
Async XLA Ops:
  3.0 9.2 %collective-permute-start.10 = (bf16[512,256]{1,0:T(8,128)(2,1)S(1)}, bf16[512,256]{1,0:T(8,128)(2,1)S(1)}, u32[]{:S(2)}, u32[]{:S(2)}) collective-permute-start(bf16[512,256]{1,0:T(8,128)(2,1)S(1)} %get-tuple-element.28), channel_id=1, source_target_pairs={{0,4},{4,0},{8,12},{12,8},{16,20},{20,16},{24,28},{28,24},{1,5},{5... | collective-permute-start | bytes 786440 | tf_op jit(solution)/shard_map/ppermute | solution.py:560
  12.2 13.0 %collective-permute-start.11 = (bf16[512,256]{1,0:T(8,128)(2,1)}, bf16[512,256]{1,0:T(8,128)(2,1)S(1)}, u32[]{:S(2)}, u32[]{:S(2)}) collective-permute-start(bf16[512,256]{1,0:T(8,128)(2,1)} %get-tuple-element.29), channel_id=1, source_target_pairs={{0,4},{4,0},{8,12},{12,8},{16,20},{20,16},{24,28},{28,24},{1,5},{5... | collective-permute-start | bytes 786440 | tf_op jit(solution)/shard_map/ppermute | solution.py:560
  14.5 6.2 %collective-permute-start.2 = (bf16[32,1024]{1,0:T(8,128)(2,1)S(1)}, bf16[32,1024]{1,0:T(8,128)(2,1)S(1)}, u32[]{:S(2)}, u32[]{:S(2)}) collective-permute-start(bf16[32,1024]{1,0:T(8,128)(2,1)S(1)} %bitcast.93), channel_id=1, source_target_pairs={{0,24},{4,28},{8,16},{12,20},{16,8},{20,12},{24,0},{28,4},{1,25},{... | collective-permute-start | bytes 196616 | tf_op jit(solution)/shard_map/ppermute | solution.py:557
  18.3 5.3 %collective-permute-start.1 = (bf16[32,1024]{1,0:T(8,128)(2,1)S(1)}, bf16[32,1024]{1,0:T(8,128)(2,1)}, u32[]{:S(2)}, u32[]{:S(2)}) collective-permute-start(bf16[32,1024]{1,0:T(8,128)(2,1)S(1)} %bitcast.95), channel_id=1, source_target_pairs={{0,16},{4,20},{8,24},{12,28},{16,0},{20,4},{24,8},{28,12},{1,17},{... | collective-permute-start | bytes 196616 | tf_op jit(solution)/shard_map/ppermute | solution.py:557
  24.6 8.7 %collective-permute-start.6 = (bf16[4,32,1024]{2,1,0:T(8,128)(2,1)S(1)}, bf16[4,32,1024]{2,1,0:T(8,128)(2,1)S(1)}, u32[]{:S(2)}, u32[]{:S(2)}) collective-permute-start(bf16[4,32,1024]{2,1,0:T(8,128)(2,1)S(1)} %pad_maximum_fusion.refs_0_), channel_id=1, source_target_pairs={{0,4},{4,0},{8,12},{12,8},{16,20},{20,16},{24,28},{28,24},{1,5},{5... | collective-permute-start | bytes 786440 | tf_op jit(solution)/shard_map/ppermute | solution.py:560
  25.2 11.2 %collective-permute-start.12 = (bf16[512,256]{1,0:T(8,128)(2,1)S(1)}, bf16[512,256]{1,0:T(8,128)(2,1)S(1)}, u32[]{:S(2)}, u32[]{:S(2)}) collective-permute-start(bf16[512,256]{1,0:T(8,128)(2,1)S(1)} %bitcast.89), channel_id=1, source_target_pairs={{0,4},{4,0},{8,12},{12,8},{16,20},{20,16},{24,28},{28,24},{1,5},{5... | collective-permute-start | bytes 786440 | tf_op jit(solution)/shard_map/ppermute | solution.py:560
  26.7 15.5 %collective-permute-start.4 = (bf16[4,32,1024]{2,1,0:T(8,128)(2,1)S(1)}, bf16[4,32,1024]{2,1,0:T(8,128)(2,1)}, u32[]{:S(2)}, u32[]{:S(2)}) collective-permute-start(bf16[4,32,1024]{2,1,0:T(8,128)(2,1)S(1)} %pad_maximum_fusion.refs_0_), channel_id=1, source_target_pairs={{0,2},{1,3},{2,0},{3,1},{4,6},{5,7},{6,4},{7,5},{8,10},{9,11},{10,... | collective-permute-start | bytes 786440 | tf_op jit(solution)/shard_map/ppermute | solution.py:598
  33.4 9.4 %collective-permute-start.8 = (bf16[4,32,1024]{2,1,0:T(8,128)(2,1)S(1)}, bf16[4,32,1024]{2,1,0:T(8,128)(2,1)}, u32[]{:S(2)}, u32[]{:S(2)}) collective-permute-start(bf16[4,32,1024]{2,1,0:T(8,128)(2,1)S(1)} %collective-permute-done.6.refs_4_), channel_id=1, source_target_pairs={{0,2},{1,3},{2,0},{3,1},{4,6},{5,7},{6,4},{7,5},{8,10},{9,11},{10,... | collective-permute-start | bytes 786440 | tf_op jit(solution)/shard_map/ppermute | solution.py:598
  36.5 7.7 %collective-permute-start.13 = (bf16[512,256]{1,0:T(8,128)(2,1)}, bf16[512,256]{1,0:T(8,128)(2,1)}, u32[]{:S(2)}, u32[]{:S(2)}) collective-permute-start(bf16[512,256]{1,0:T(8,128)(2,1)} %get-tuple-element.31), channel_id=1, source_target_pairs={{0,4},{4,0},{8,12},{12,8},{16,20},{20,16},{24,28},{28,24},{1,5},{5... | collective-permute-start | bytes 786440 | tf_op jit(solution)/shard_map/ppermute | solution.py:560
  42.2 8.1 %collective-permute-start.3 = (bf16[4,32,1024]{2,1,0:T(8,128)(2,1)S(1)}, bf16[4,32,1024]{2,1,0:T(8,128)(2,1)}, u32[]{:S(2)}, u32[]{:S(2)}) collective-permute-start(bf16[4,32,1024]{2,1,0:T(8,128)(2,1)S(1)} %pad_maximum_fusion.refs_0_), channel_id=1, source_target_pairs={{0,1},{1,0},{2,3},{3,2},{4,5},{5,4},{6,7},{7,6},{8,9},{9,8},{10,11... | collective-permute-start | bytes 786440 | tf_op jit(solution)/shard_map/ppermute | solution.py:598
  42.3 8.1 %collective-permute-start.7 = (bf16[4,32,1024]{2,1,0:T(8,128)(2,1)S(1)}, bf16[4,32,1024]{2,1,0:T(8,128)(2,1)}, u32[]{:S(2)}, u32[]{:S(2)}) collective-permute-start(bf16[4,32,1024]{2,1,0:T(8,128)(2,1)S(1)} %collective-permute-done.6.refs_4_), channel_id=1, source_target_pairs={{0,1},{1,0},{2,3},{3,2},{4,5},{5,4},{6,7},{7,6},{8,9},{9,8},{10,11... | collective-permute-start | bytes 786440 | tf_op jit(solution)/shard_map/ppermute | solution.py:598
  42.8 7.6 %collective-permute-start.5 = (bf16[4,32,1024]{2,1,0:T(8,128)(2,1)}, bf16[4,32,1024]{2,1,0:T(8,128)(2,1)}, u32[]{:S(2)}, u32[]{:S(2)}) collective-permute-start(bf16[4,32,1024]{2,1,0:T(8,128)(2,1)} %collective-permute-done.4.refs_2_), channel_id=1, source_target_pairs={{0,1},{1,0},{2,3},{3,2},{4,5},{5,4},{6,7},{7,6},{8,9},{9,8},{10,11... | collective-permute-start | bytes 786440 | tf_op jit(solution)/shard_map/ppermute | solution.py:598
  44.1 6.2 %collective-permute-start.9 = (bf16[4,32,1024]{2,1,0:T(8,128)(2,1)}, bf16[4,32,1024]{2,1,0:T(8,128)(2,1)}, u32[]{:S(2)}, u32[]{:S(2)}) collective-permute-start(bf16[4,32,1024]{2,1,0:T(8,128)(2,1)} %collective-permute-done.8.refs_6_), channel_id=1, source_target_pairs={{0,1},{1,0},{2,3},{3,2},{4,5},{5,4},{6,7},{7,6},{8,9},{9,8},{10,11... | collective-permute-start | bytes 786440 | tf_op jit(solution)/shard_map/ppermute | solution.py:598
  45.9 7.2 %collective-permute-start.14 = (bf16[512,256]{1,0:T(8,128)(2,1)}, bf16[512,256]{1,0:T(8,128)(2,1)}, u32[]{:S(2)}, u32[]{:S(2)}) collective-permute-start(bf16[512,256]{1,0:T(8,128)(2,1)} %get-tuple-element.32), channel_id=1, source_target_pairs={{0,4},{4,0},{8,12},{12,8},{16,20},{20,16},{24,28},{28,24},{1,5},{5... | collective-permute-start | bytes 786440 | tf_op jit(solution)/shard_map/ppermute | solution.py:560
  64.7 15.9 %collective-permute-start.16 = (bf16[1024,256]{1,0:T(8,128)(2,1)S(1)}, bf16[1024,256]{1,0:T(8,128)(2,1)S(1)}, u32[]{:S(2)}, u32[]{:S(2)}) collective-permute-start(bf16[1024,256]{1,0:T(8,128)(2,1)S(1)} %get-tuple-element.38), channel_id=1, source_target_pairs={{0,8},{4,12},{24,16},{28,20},{1,9},{5,13},{25,17},{29,21},{2,10},{... | collective-permute-start | bytes 1572872 | tf_op jit(solution)/shard_map/ppermute | solution.py:557
  68.2 24.0 %collective-permute-start.19 = (bf16[1056,256]{1,0:T(8,128)(2,1)}, bf16[1056,256]{1,0:T(8,128)(2,1)}, u32[]{:S(2)}, u32[]{:S(2)}) collective-permute-start(bf16[1056,256]{1,0:T(8,128)(2,1)} %get-tuple-element.41.own_ref), channel_id=1, source_target_pairs={{0,8},{4,12},{24,16},{28,20},{1,9},{5,13},{25,17},{29,21},{2,10},{... | collective-permute-start | bytes 1622024 | tf_op jit(solution)/shard_map/ppermute | solution.py:557
  70.3 33.5 %collective-permute-start.21 = (bf16[1056,256]{1,0:T(8,128)(2,1)}, bf16[1056,256]{1,0:T(8,128)(2,1)}, u32[]{:S(2)}, u32[]{:S(2)}) collective-permute-start(bf16[1056,256]{1,0:T(8,128)(2,1)} %get-tuple-element.40.own_ref), channel_id=1, source_target_pairs={{0,8},{4,12},{24,16},{28,20},{1,9},{5,13},{25,17},{29,21},{2,10},{... | collective-permute-start | bytes 1622024 | tf_op jit(solution)/shard_map/ppermute | solution.py:557
  80.7 26.8 %collective-permute-start.17 = (bf16[1024,256]{1,0:T(8,128)(2,1)S(1)}, bf16[1024,256]{1,0:T(8,128)(2,1)S(1)}, u32[]{:S(2)}, u32[]{:S(2)}) collective-permute-start(bf16[1024,256]{1,0:T(8,128)(2,1)S(1)} %add_convert_fusion.refs_4_), channel_id=1, source_target_pairs={{8,16},{12,20},{16,8},{20,12},{9,17},{13,21},{17,9},{21,13},{10,18... | collective-permute-start | bytes 1572872 | tf_op jit(solution)/shard_map/ppermute | solution.py:557
  84.4 26.6 %collective-permute-start.18 = (bf16[1056,256]{1,0:T(8,128)(2,1)}, bf16[1056,256]{1,0:T(8,128)(2,1)}, u32[]{:S(2)}, u32[]{:S(2)}) collective-permute-start(bf16[1056,256]{1,0:T(8,128)(2,1)} %copy-done.5), channel_id=1, source_target_pairs={{0,8},{4,12},{8,0},{12,4},{16,24},{20,28},{24,16},{28,20},{1,9},{5... | collective-permute-start | bytes 1622024 | tf_op jit(solution)/shard_map/ppermute | solution.py:557
  94.4 16.6 %collective-permute-start.20 = (bf16[1056,256]{1,0:T(8,128)(2,1)}, bf16[1056,256]{1,0:T(8,128)(2,1)}, u32[]{:S(2)}, u32[]{:S(2)}) collective-permute-start(bf16[1056,256]{1,0:T(8,128)(2,1)} %onward.2), channel_id=1, source_target_pairs={{8,24},{12,28},{16,0},{20,4},{9,25},{13,29},{17,1},{21,5},{10,26},... | collective-permute-start | bytes 1622024 | tf_op jit(solution)/shard_map/ppermute | solution.py:557
  106.0 6.7 %collective-permute-start.22 = (bf16[1056,256]{1,0:T(8,128)(2,1)}, bf16[1056,256]{1,0:T(8,128)(2,1)}, u32[]{:S(2)}, u32[]{:S(2)}) collective-permute-start(bf16[1056,256]{1,0:T(8,128)(2,1)} %onward.3), channel_id=1, source_target_pairs={{8,16},{12,20},{16,8},{20,12},{9,17},{13,21},{17,9},{21,13},{10,18... | collective-permute-start | bytes 1622024 | tf_op jit(solution)/shard_map/ppermute | solution.py:557
  111.0 11.8 %collective-permute-start.23 = (bf16[1024,256]{1,0:T(8,128)(2,1)}, bf16[1024,256]{1,0:T(8,128)(2,1)}, u32[]{:S(2)}, u32[]{:S(2)}) collective-permute-start(bf16[1024,256]{1,0:T(8,128)(2,1)} %multiply_convert_fusion), channel_id=1, source_target_pairs={{8,0},{12,4},{16,24},{20,28},{9,1},{13,5},{17,25},{21,29},{10,2},{... | collective-permute-start | bytes 1572872 | tf_op jit(solution)/shard_map/ppermute | solution.py:557
  135.2 5.9 %collective-permute-start.24 = (bf16[1040,256]{1,0:T(8,128)(2,1)}, bf16[1040,256]{1,0:T(8,128)(2,1)}, u32[]{:S(2)}, u32[]{:S(2)}) collective-permute-start(bf16[1040,256]{1,0:T(8,128)(2,1)} %get-tuple-element.47), channel_id=1, source_target_pairs={{8,16},{12,20},{16,8},{20,12},{9,17},{13,21},{17,9},{21,13},{10,18... | collective-permute-start | bytes 1597448 | tf_op jit(solution)/shard_map/ppermute | solution.py:557
  136.7 14.6 %collective-permute-start.27 = (bf16[1040,256]{1,0:T(8,128)(2,1)}, bf16[1040,256]{1,0:T(8,128)(2,1)S(1)}, u32[]{:S(2)}, u32[]{:S(2)}) collective-permute-start(bf16[1040,256]{1,0:T(8,128)(2,1)} %get-tuple-element.47), channel_id=1, source_target_pairs={{0,8},{4,12},{8,0},{12,4},{16,24},{20,28},{24,16},{28,20},{1,9},{5... | collective-permute-start | bytes 1597448 | tf_op jit(solution)/shard_map/ppermute | solution.py:557
  141.1 20.4 %collective-permute-start.25 = (bf16[1040,256]{1,0:T(8,128)(2,1)}, bf16[1040,256]{1,0:T(8,128)(2,1)S(1)}, u32[]{:S(2)}, u32[]{:S(2)}) collective-permute-start(bf16[1040,256]{1,0:T(8,128)(2,1)} %collective-permute-done.24), channel_id=1, source_target_pairs={{8,0},{12,4},{16,24},{20,28},{9,1},{13,5},{17,25},{21,29},{10,2},{... | collective-permute-start | bytes 1597448 | tf_op jit(solution)/shard_map/ppermute | solution.py:557
  143.1 18.4 %collective-permute-start.26 = (bf16[1040,256]{1,0:T(8,128)(2,1)}, bf16[1040,256]{1,0:T(8,128)(2,1)S(1)}, u32[]{:S(2)}, u32[]{:S(2)}) collective-permute-start(bf16[1040,256]{1,0:T(8,128)(2,1)} %get-tuple-element.47), channel_id=1, source_target_pairs={{0,4},{4,0},{8,12},{12,8},{16,20},{20,16},{24,28},{28,24},{1,5},{5... | collective-permute-start | bytes 1597448 | tf_op jit(solution)/shard_map/ppermute | solution.py:560
  151.7 25.0 %collective-permute-start.30 = (bf16[1040,256]{1,0:T(8,128)(2,1)S(1)}, bf16[1040,256]{1,0:T(8,128)(2,1)S(1)}, u32[]{:S(2)}, u32[]{:S(2)}) collective-permute-start(bf16[1040,256]{1,0:T(8,128)(2,1)S(1)} %collective-permute-done.27), channel_id=1, source_target_pairs={{0,4},{4,0},{8,12},{12,8},{16,20},{20,16},{24,28},{28,24},{1,5},{5... | collective-permute-start | bytes 1597448 | tf_op jit(solution)/shard_map/ppermute | solution.py:560
  151.8 10.3 %collective-permute-start.28 = (bf16[1040,256]{1,0:T(8,128)(2,1)S(1)}, bf16[1040,256]{1,0:T(8,128)(2,1)S(1)}, u32[]{:S(2)}, u32[]{:S(2)}) collective-permute-start(bf16[1040,256]{1,0:T(8,128)(2,1)S(1)} %collective-permute-done.27), channel_id=1, source_target_pairs={{8,16},{12,20},{16,8},{20,12},{9,17},{13,21},{17,9},{21,13},{10,18... | collective-permute-start | bytes 1597448 | tf_op jit(solution)/shard_map/ppermute | solution.py:557
  161.5 18.7 %collective-permute-start.31 = (bf16[1040,256]{1,0:T(8,128)(2,1)S(1)}, bf16[1040,256]{1,0:T(8,128)(2,1)S(1)}, u32[]{:S(2)}, u32[]{:S(2)}) collective-permute-start(bf16[1040,256]{1,0:T(8,128)(2,1)S(1)} %broadcast_select_fusion.1), channel_id=1, source_target_pairs={{0,4},{4,0},{8,12},{12,8},{16,20},{20,16},{24,28},{28,24},{1,5},{5... | collective-permute-start | bytes 1597448 | tf_op jit(solution)/shard_map/ppermute | solution.py:560
  162.1 14.5 %collective-permute-start.29 = (bf16[1040,256]{1,0:T(8,128)(2,1)S(1)}, bf16[1040,256]{1,0:T(8,128)(2,1)S(1)}, u32[]{:S(2)}, u32[]{:S(2)}) collective-permute-start(bf16[1040,256]{1,0:T(8,128)(2,1)S(1)} %collective-permute-done.28), channel_id=1, source_target_pairs={{8,0},{12,4},{16,24},{20,28},{9,1},{13,5},{17,25},{21,29},{10,2},{... | collective-permute-start | bytes 1597448 | tf_op jit(solution)/shard_map/ppermute | solution.py:557
  176.7 11.1 %collective-permute-start.32 = (bf16[1040,256]{1,0:T(8,128)(2,1)S(1)}, bf16[1040,256]{1,0:T(8,128)(2,1)S(1)}, u32[]{:S(2)}, u32[]{:S(2)}) collective-permute-start(bf16[1040,256]{1,0:T(8,128)(2,1)S(1)} %broadcast_select_fusion), channel_id=1, source_target_pairs={{0,4},{4,0},{8,12},{12,8},{16,20},{20,16},{24,28},{28,24},{1,5},{5... | collective-permute-start | bytes 1597448 | tf_op jit(solution)/shard_map/ppermute | solution.py:560
  193.1 27.8 %all-to-all-start = ((bf16[16,32,512]{2,1,0:T(8,128)(2,1)}), bf16[16,32,512]{2,1,0:T(8,128)(2,1)S(1)}, u32[]{:S(2)}, u32[]{:S(2)}) async-start(bf16[16,32,512]{2,1,0:T(8,128)(2,1)} %bitcast.23), calls=%async_computation | async-start | bytes 1048576 | tf_op jit(solution)/shard_map/all_to_all | solution.py:705
  (23 other events, 355.9 us)

commit v3 on v2

--- a/solution.py
+++ b/solution.py
@@ -176,6 +176,7 @@
 
 PAIR = 2
 LINE = 4
+PARTS = 2
 ROWS = 8
 SMEM = pl.BlockSpec(memory_space=pltpu.SMEM)
 HIGHEST = lax.Precision.HIGHEST
@@ -267,15 +268,15 @@
     return jnp.where(upper, top, values - top)
 
 
-def project(place, factor, hidden, w_x, weights):
+def project(place, factor, hidden, w_x, weights, part):
     line, own, wide = hidden[0].shape
     ranks = len(hidden) // PAIR
     depth, channels = weights[0].shape
     maps_wide = weights[LINE].shape[1]
     x_wide = channels * LINE
-    steps = 2
-    each = line // steps
-    tokens = line * PAIR * ranks * own
+    steps = 1
+    each = line // PARTS
+    tokens = each * PAIR * ranks * own
     extra = tokens // channels * ROWS
 
     def fixed(array):
@@ -285,7 +286,7 @@
     maps = jax.ShapeDtypeStruct((tokens, maps_wide), jnp.bfloat16)
     largest = jax.ShapeDtypeStruct((ROWS, 128), jnp.float32)
     outs = [payload] * LINE + [maps, largest]
-    rows_of = pl.BlockSpec((each, own, wide), lambda i, p: (i ^ (p[2] // each), 0, 0))
+    rows_of = pl.BlockSpec((each, own, wide), lambda i, p: (part ^ (p[2] // each), 0, 0))
     return pl.pallas_call(
         functools.partial(project_kernel, ranks),
         grid_spec=pltpu.PrefetchScalarGridSpec(
@@ -629,100 +630,104 @@
     start, end = (0, LINE - 1)
     at_end = (z == start) | (z == end)
     next_start, next_end = (1, LINE - 2)
+    inward = [(start, next_start), (end, next_end)]
+    outward = [(next_start, start), (next_end, end)]
+    middle = [(next_start, next_end), (next_end, next_start)]
+    over_middle = [(next_start, end), (next_end, start)]
+    beside_pairs = [(s, s ^ 1) for s in range(LINE)]
+    tie = lax.optimization_barrier
     weights = (*swapped, bc_own, bc_other, dt_own, dt_other)
+    parts = [project(place, factor, rows, w_x, weights, part) for part in range(PARTS)]
+    sends = []
+    for mine, near, over, far, maps, largest in parts:
+        sends.append(
+            (
+                along(maps, inward),
+                along(far, inward),
+                along(over, inward),
+                along(near, beside_pairs),
+            )
+        )
     carry = init_state.reshape(-1, STATE)
-    mine, near, over, far, maps, largest = project(place, factor, rows, w_x, weights)
-    map_hop = along(maps, [(start, next_start), (end, next_end)])
-    hop_far = along(far, [(start, next_start), (end, next_end)])
-    hop_over = along(over, [(start, next_start), (end, next_end)])
-    got_near = along(near, [(s, s ^ 1) for s in range(LINE)])
-    map_sum = (maps.astype(f32) + map_hop.astype(f32)).astype(bf16)
-    map_far = along(map_sum, [(next_start, next_end), (next_end, next_start)])
-    map_done = ((map_sum.astype(f32) + map_far.astype(f32)) * in_scale).astype(bf16)
-    sent_end = onward(over, hop_far)
-    hop_over, unused = lax.optimization_barrier((hop_over, sent_end))
-    got_end = along(sent_end, [(next_start, end), (next_end, start)])
-    map_done, got_near, got_end = lax.optimization_barrier((map_done, got_near, got_end))
-    map_done = along(map_done, [(next_start, start), (next_end, end)])
-    got_next = along(onward(far, hop_over), [(next_start, next_end), (next_end, next_start)])
-    gained, carry = scan(
-        place,
-        in_scale,
-        [mine, got_near, got_end, got_next],
-        [map_sum, map_far, map_done],
-        small,
-        largest,
-        carry,
-        True,
-    )
-    tokens = gained.shape[0] - 2 * ROWS
-    beside = along(gained, [(s, s ^ 1) for s in range(LINE)])
-    middle = [(next_start, next_end), (next_end, next_start)]
-    outward = [(next_start, start), (next_end, end)]
-    facing = along(gained, middle)
-    beyond = along(beside, middle)
-    second = jnp.where(at_end, along(facing, outward), facing)
-    third = jnp.where(at_end, along(beyond, outward), beyond)
+    scanned = []
+    for part, (mine, near, over, far, maps, largest) in enumerate(parts):
+        map_hop, hop_far, hop_over, got_near = sends[part]
+        if part:
+            map_hop, unused = tie((map_hop, scanned[-1]))
+        map_sum = (maps.astype(f32) + map_hop.astype(f32)).astype(bf16)
+        map_far = along(map_sum, middle)
+        map_done = ((map_sum.astype(f32) + map_far.astype(f32)) * in_scale).astype(bf16)
+        sent_end = onward(over, hop_far)
+        got_end = along(sent_end, over_middle)
+        hop_over, unused = tie((hop_over, sent_end))
+        got_next = along(onward(far, hop_over), middle)
+        map_done, got_near, got_end = tie((map_done, got_near, got_end))
+        map_done = along(map_done, outward)
+        if part + 1 < PARTS:
+            map_done, ahead = tie((map_done, sends[part + 1][0]))
+            sends[part + 1] = (ahead, *sends[part + 1][1:])
+        gained, carry = scan(
+            place,
+            in_scale,
+            [mine, got_near, got_end, got_next],
+            [map_sum, map_far, map_done],
+            small,
+            largest,
+            carry,
+            part == 0,
+        )
+        scanned.append(gained)
     two, three = (jnp.where(at_end, 2, 3), jnp.where(at_end, 3, 2))
-    far_own = across(gained)
-    far_beside = across(beside)
-    second, far_own = lax.optimization_barrier((second, far_own))
-    far_second = across(second)
-    third, far_beside = lax.optimization_barrier((third, far_beside))
-    far_third = across(third)
-    got = (
-        (0, (gained, far_own)),
-        (1, (beside, far_beside)),
-        (two, (second, far_second)),
-        (three, (third, far_third)),
-    )
-    total = squares = top = None
-    for m, pair in got:
-        for x, piece in enumerate(pair):
-            at = ((side ^ x) * LINE + (z ^ m)) * channels
-            w_rows = lax.dynamic_slice_in_dim(w_out, at, channels, axis=0)
-            product = jnp.dot(piece, w_rows, preferred_element_type=f32)
-            tail = piece[tokens:].astype(f32)
-            low, high = (tail[:ROWS, :SPAN] + tail[:ROWS, SPAN:], tail[ROWS:, :SPAN])
-            if total is None:
-                total, squares, top = (product, low, high)
-            else:
-                total = total + product
-                squares = squares + low
-                top = jnp.maximum(top, high)
     wide = w_out.shape[1]
-    squares = squares + lax.ppermute(squares, "tensor", [(t, t ^ 1) for t in range(ranks)])
-    pairs = ranks // 2
-    kept = total[:tokens].reshape(count, pairs, 2, own, wide)
-    nearest = rank % 2
-    received = lax.ppermute(
-        pick(kept, 2, 1 - nearest).astype(bf16), "tensor", [(t, t ^ 1) for t in range(ranks)]
-    )
-    kept = (pick(kept, 2, nearest) + received.astype(f32)).astype(bf16)
-    groups = [
-        [s * ranks + t for s in range(count) for t in range(c, ranks, 2)] for c in range(2)
-    ]
-    final = lax.all_to_all(
-        kept.reshape(count * pairs, own, wide),
-        ("seq", "tensor"),
-        split_axis=0,
-        concat_axis=0,
-        axis_index_groups=groups,
-        tiled=True,
-    )
-    bit = 2
-    while bit < ranks:
-        swap = [(t, t ^ bit) for t in range(ranks)]
-        squares = squares + lax.ppermute(squares, "tensor", swap)
-        bit *= 2
-    mean_sq = squares.reshape(count, ranks, own) / (HEADS * HEAD_DIM)
-    factors = lax.rsqrt(lax.dynamic_slice_in_dim(mean_sq, here, 1)[0] + epsilon)
-    factors = pick(factors, 0, rank)[:, None, None]
-    final = jnp.sum(final.reshape(count, pairs, own, wide).astype(f32), axis=1)
-    final = final.transpose(1, 0, 2) * factors
-    layer_out = final.astype(bf16).reshape(own, count * wide)
-    abs_max = jnp.max(top)
-    return (layer_out, abs_max)
+    totals, top = ([], None)
+    for gained in scanned:
+        tokens = gained.shape[0] - 2 * ROWS
+        blocks = tokens // SPAN
+        beside = along(gained, beside_pairs)
+        facing = along(gained, middle)
+        beyond = along(beside, middle)
+        second = jnp.where(at_end, along(facing, outward), facing)
+        third = jnp.where(at_end, along(beyond, outward), beyond)
+        far_own = across(gained)
+        far_beside = across(beside)
+        second, far_own = tie((second, far_own))
+        far_second = across(second)
+        third, far_beside = tie((third, far_beside))
+        far_third = across(third)
+        got = (
+            (0, (gained, far_own)),
+            (1, (beside, far_beside)),
+            (two, (second, far_second)),
+            (three, (third, far_third)),
+        )
+        total = squares = None
+        for m, pair in got:
+            for x, piece in enumerate(pair):
+                at = ((side ^ x) * LINE + (z ^ m)) * channels
+                w_rows = lax.dynamic_slice_in_dim(w_out, at, channels, axis=0)
+                product = jnp.dot(piece, w_rows, preferred_element_type=f32)
+                tail = piece[tokens:].astype(f32)
+                low, high = (tail[:ROWS, :SPAN] + tail[:ROWS, SPAN:], tail[ROWS:, :SPAN])
+                total = product if total is None else total + product
+                squares = low if squares is None else squares + low
+                top = high if top is None else jnp.maximum(top, high)
+        kept = total[:tokens].reshape(blocks, ranks, own, wide)
+        bit = 1
+        while bit < ranks:
+            pairs = [(t, t ^ bit) for t in range(ranks)]
+            squares = squares + lax.ppermute(squares, "tensor", pairs)
+            keeps = (rank // bit) % 2
+            halves = kept.reshape(blocks, -1, 2, own, wide)
+            received = lax.ppermute(pick(halves, 2, 1 - keeps).astype(bf16), "tensor", pairs)
+            kept = pick(halves, 2, keeps) + received.astype(f32)
+            bit *= 2
+        mean_sq = squares[:blocks].reshape(blocks, ranks, own) / (HEADS * HEAD_DIM)
+        factors = lax.rsqrt(pick(mean_sq, 1, rank) + epsilon)
+        totals.append((kept.reshape(blocks, own, wide) * factors[:, :, None]).astype(bf16))
+    final = jnp.concatenate(totals, axis=0)
+    final = lax.all_to_all(final, "seq", split_axis=0, concat_axis=0, tiled=True)
+    layer_out = final.transpose(1, 0, 2).reshape(own, count * wide)
+    return (layer_out, jnp.max(top))
 
 
 def solution(mesh):

time: 223 us -> 245 us (1.099)
  waiting for transfers between devices: 103 us -> 60.9 us
  starting transfers between devices: 61.2 us -> 91.3 us
  local copies, waits for them, and re-layouts: 19.7 us -> 35.8 us
  other arithmetic: 10.1 us -> 19.1 us
  matrix products: 4.55 us -> 9.65 us
    ppermute x16 -> x29, waiting for transfers between devices: 64 us -> 26.7 us  [along(): return lax.ppermute(value, 'seq', moves)]
    ppermute x16 -> x29, starting transfers between devices: 30.6 us -> 59.6 us  [along(): return lax.ppermute(value, 'seq', moves)]
    unnamed x46 -> x114, local copies, waits for them, and re-layouts: 7.71 us -> 17.5 us
    ppermute x11 -> x15, waiting for transfers between devices: 25.4 us -> 17.1 us  [across(): return lax.ppermute(value, 'seq', [(s, s ^ 1) for s in range(count)])]
    all_to_all x1, starting transfers between devices: 12.4 us -> 5.58 us  [by_heads(): lax.all_to_all(final, 'seq', split_axis=0, concat_axis=0, tiled=True)]
    ppermute x3 -> x8, waiting for transfers between devices: 3.41 us -> 9.79 us  [the longest x4 7.78 us: by_heads(): lax.ppermute(pick(halves, 2, 1 - keeps).astype(bf16), 'tensor', pairs)]
    dot_general x8 -> x16, matrix products: 4.55 us -> 9.65 us  [by_heads(): product = jnp.dot(piece, w_rows, preferred_element_type=f32)]
    ppermute x3 -> x8, starting transfers between devices: 2.07 us -> 6.31 us  [the longest x4 3.33 us: by_heads(): squares = squares + lax.ppermute(squares, 'tensor', pairs)]
  transfers between devices with their start and end apart: 37 -> 59, of which waited for: 23 -> 22; matrix products, arithmetic and copies ran while one was open for 10% -> 18% of each run, Pallas kernels for 2% -> 8%
where the time goes in v3:
time: 245 us; the launch traced here: 243 us
  starting transfers between devices  91.3 us (37%)
  waiting for transfers between devices  60.9 us (25%)
  local copies, waits for them, and re-layouts  35.8 us (15%)
  Pallas kernels  23.6 us (10%)
  other arithmetic  19.1 us (8%)
  matrix products  9.65 us (4%)
  between operations  2.51 us (1%)
    ppermute x29, starting transfers between devices, along(): return lax.ppermute(value, 'seq', moves)  59.6 us
    ppermute x29, waiting for transfers between devices, along(): return lax.ppermute(value, 'seq', moves)  26.7 us
    unnamed x114, local copies, waits for them, and re-layouts  17.5 us
    ppermute x15, waiting for transfers between devices, across(): return lax.ppermute(value, 'seq', [(s, s ^ 1) for s in range(count)])  17.1 us
    ppermute x15, starting transfers between devices, across(): return lax.ppermute(value, 'seq', [(s, s ^ 1) for s in range(count)])  16.2 us
    pallas_call x2, Pallas kernels, scan(): pl.pallas_call(functools.partial(scan_kernel, first), grid_spec=pltpu.Pre...  9.93 us
    dot_general x16, matrix products, by_heads(): product = jnp.dot(piece, w_rows, preferred_element_type=f32)  9.65 us
    pallas_call x2, Pallas kernels, project(): pl.pallas_call(functools.partial(project_kernel, ranks), grid_spec=pltpu....  9.42 us
  transfers between devices with their start and end apart: 59, of which 22 were waited for; matrix products, arithmetic and copies ran while one was open for 18% of the time, Pallas kernels for 8%

profile of v3, /device:TPU:0, one launch (start us, length us, event | category | flops | bytes accessed | tf_op | source)
XLA Modules:
  0.0 242.8 jit_solution(5582761114657335372)
XLA Ops:
  0.7 2.2 constant_dynamic-slice_fusion.7
  2.9 2.9 %collective-permute-start.10 = (bf16[512,256]{1,0:T(8,128)(2,1)S(1)}, bf16[512,256]{1,0:T(8,128)(2,1)S(1)}, u32[]{:S(2)}, u32[]{:S(2)}) collective-permute-start(bf16[512,256]{1,0:T(8,128)(2,1)S(1)} %get-tuple-element.47), channel_id=1, source_target_pairs={{0,4},{4,0},{8,12},{12,8},{16,20},{20,16},{24,28},{28,24},{1,5},{5... | collective-permute-start | bytes 786440 | tf_op jit(solution)/shard_map/ppermute | solution.py:561
  7.1 5.1 %collective-permute-done.10.refs_12_ = bf16[512,256]{1,0:T(8,128)(2,1)S(1)} collective-permute-done((bf16[512,256]{1,0:T(8,128)(2,1)S(1)}, bf16[512,256]{1,0:T(8,128)(2,1)S(1)}, u32[]{:S(2)}, u32[]{:S(2)}) %collective-permute-start.10) | collective-permute-done | bytes 262176 | tf_op jit(solution)/shard_map/ppermute | solution.py:561
  14.5 3.7 %collective-permute-start.2 = (bf16[32,1024]{1,0:T(8,128)(2,1)S(1)}, bf16[32,1024]{1,0:T(8,128)(2,1)S(1)}, u32[]{:S(2)}, u32[]{:S(2)}) collective-permute-start(bf16[32,1024]{1,0:T(8,128)(2,1)S(1)} %bitcast.114), channel_id=1, source_target_pairs={{0,24},{4,28},{8,16},{12,20},{16,8},{20,12},{24,0},{28,4},{1,25},{... | collective-permute-start | bytes 196616 | tf_op jit(solution)/shard_map/ppermute | solution.py:558
  20.7 1.9 collective-permute-done
  28.2 5.1 %collective-permute-done.6.refs_4_ = bf16[4,32,1024]{2,1,0:T(8,128)(2,1)S(1)} collective-permute-done((bf16[4,32,1024]{2,1,0:T(8,128)(2,1)S(1)}, bf16[4,32,1024]{2,1,0:T(8,128)(2,1)S(1)}, u32[]{:S(2)}, u32[]{:S(2)}) %collective-permute-start.6) | collective-permute-done | bytes 262176 | tf_op jit(solution)/shard_map/ppermute | solution.py:561
  50.9 2.2 collective-permute-done.14.refs_9_
  56.5 4.7 %project.2 = (bf16[528,256]{1,0:T(8,128)(2,1)S(1)}, bf16[528,256]{1,0:T(8,128)(2,1)S(1)}, bf16[528,256]{1,0:T(8,128)(2,1)}, bf16[528,256]{1,0:T(8,128)(2,1)}, bf...) custom-call(s32[7]{0:T(128)S(1)} %stack.43.place_ref, f32[1]{0:T(128)} %bitcast.4.factor_ref, ...), custom_call_target="tpu_custom_call" | custom-call | flops 1342177280 | bytes 2097152 | tf_op jit(solution)/shard_map/project/pallas_call | solution.py:290
  62.0 3.7 %collective-permute-start.16 = (bf16[512,256]{1,0:T(8,128)(2,1)S(1)}, bf16[512,256]{1,0:T(8,128)(2,1)S(1)}, u32[]{:S(2)}, u32[]{:S(2)}) collective-permute-start(bf16[512,256]{1,0:T(8,128)(2,1)S(1)} %get-tuple-element.57), channel_id=1, source_target_pairs={{0,8},{4,12},{24,16},{28,20},{1,9},{5,13},{25,17},{29,21},{2,10},{... | collective-permute-start | bytes 786440 | tf_op jit(solution)/shard_map/ppermute | solution.py:558
  65.7 2.0 collective-permute-start.19
  67.7 2.0 collective-permute-start.21
  69.7 2.7 %collective-permute-done.16 = bf16[512,256]{1,0:T(8,128)(2,1)S(1)} collective-permute-done((bf16[512,256]{1,0:T(8,128)(2,1)S(1)}, bf16[512,256]{1,0:T(8,128)(2,1)S(1)}, u32[]{:S(2)}, u32[]{:S(2)}) %collective-permute-start.16) | collective-permute-done | bytes 262176 | tf_op jit(solution)/shard_map/ppermute | solution.py:558
  82.0 3.9 %collective-permute-start.18 = (bf16[528,256]{1,0:T(8,128)(2,1)}, bf16[528,256]{1,0:T(8,128)(2,1)S(1)}, u32[]{:S(2)}, u32[]{:S(2)}) collective-permute-start(bf16[528,256]{1,0:T(8,128)(2,1)} %copy-done.30), channel_id=1, source_target_pairs={{0,8},{4,12},{8,0},{12,4},{16,24},{20,28},{24,16},{28,20},{1,9},{5... | collective-permute-start | bytes 811016 | tf_op jit(solution)/shard_map/ppermute | solution.py:558
  90.8 4.7 %project.3 = (bf16[528,256]{1,0:T(8,128)(2,1)S(1)}, bf16[528,256]{1,0:T(8,128)(2,1)S(1)}, bf16[528,256]{1,0:T(8,128)(2,1)S(1)}, bf16[528,256]{1,0:T(8,128)(2,1)S...) custom-call(s32[7]{0:T(128)S(1)} %stack.43.place_ref, f32[1]{0:T(128)} %bitcast.4.factor_ref, ...), custom_call_target="tpu_custom_call" | custom-call | flops 1342177280 | bytes 2097152 | tf_op jit(solution)/shard_map/project/pallas_call | solution.py:290
  95.6 6.0 %collective-permute-start.24 = (bf16[512,256]{1,0:T(8,128)(2,1)}, bf16[512,256]{1,0:T(8,128)(2,1)}, u32[]{:S(2)}, u32[]{:S(2)}) collective-permute-start(bf16[512,256]{1,0:T(8,128)(2,1)} %get-tuple-element.65), channel_id=1, source_target_pairs={{0,8},{4,12},{24,16},{28,20},{1,9},{5,13},{25,17},{29,21},{2,10},{... | collective-permute-start | bytes 786440 | tf_op jit(solution)/shard_map/ppermute | solution.py:558
  108.2 5.9 %collective-permute-start.40 = (bf16[528,256]{1,0:T(8,128)(2,1)}, bf16[528,256]{1,0:T(8,128)(2,1)}, u32[]{:S(2)}, u32[]{:S(2)}) collective-permute-start(bf16[528,256]{1,0:T(8,128)(2,1)} %copy-done.14), channel_id=1, source_target_pairs={{0,8},{4,12},{24,16},{28,20},{1,9},{5,13},{25,17},{29,21},{2,10},{... | collective-permute-start | bytes 811016 | tf_op jit(solution)/shard_map/ppermute | solution.py:558
  114.1 2.0 collective-permute-start.42
  120.9 5.2 %scan.2 = (bf16[528,256]{1,0:T(8,128)(2,1)S(1)}, f32[144,256]{1,0:T(8,128)S(1)}) custom-call(s32[7]{0:T(128)S(1)} %stack.43.place_ref, f32[1]{0:T(128)} %bitcast.3.scale_ref, bf16[528,256]{1,0:T(8,128)(2,1)S(1)} %copy-done.19, bf16[528,256]{1,0:T(8,128)(2,1)S(1)} %copy-done.21, bf16[528,256]{1,0:T(8,128)(2,1)S(1)} %copy-done.23, ...), custom_call_target="tpu_custom_call" | custom-call | flops 134217728 | bytes 1048576 | tf_op jit(solution)/shard_map/scan/pallas_call | solution.py:497
  134.7 5.4 %collective-permute-start.28 = (bf16[528,256]{1,0:T(8,128)(2,1)S(1)}, bf16[528,256]{1,0:T(8,128)(2,1)S(1)}, u32[]{:S(2)}, u32[]{:S(2)}) collective-permute-start(bf16[528,256]{1,0:T(8,128)(2,1)S(1)} %get-tuple-element.68), channel_id=1, source_target_pairs={{0,8},{4,12},{8,0},{12,4},{16,24},{20,28},{24,16},{28,20},{1,9},{5... | collective-permute-start | bytes 811016 | tf_op jit(solution)/shard_map/ppermute | solution.py:558
  141.7 2.2 collective-permute-done.41.refs_2_
  146.4 2.1 collective-permute-done.28
  150.3 2.9 %collective-permute-done.44.refs_6_ = bf16[512,256]{1,0:T(8,128)(2,1)S(1)} collective-permute-done((bf16[512,256]{1,0:T(8,128)(2,1)S(1)}, bf16[512,256]{1,0:T(8,128)(2,1)S(1)}, u32[]{:S(2)}, u32[]{:S(2)}) %collective-permute-start.44) | collective-permute-done | bytes 262176 | tf_op jit(solution)/shard_map/ppermute | solution.py:558
  153.2 4.8 %scan.3 = (bf16[528,256]{1,0:T(8,128)(2,1)S(1)}, f32[144,256]{1,0:T(8,128)}) custom-call(s32[7]{0:T(128)S(1)} %stack.43.place_ref, f32[1]{0:T(128)} %bitcast.3.scale_ref, bf16[528,256]{1,0:T(8,128)(2,1)S(1)} %copy-done.13, bf16[528,256]{1,0:T(8,128)(2,1)S(1)} %collective-permute-done.39.refs_1_, bf16[528,256]{1,0:T(8,128)(2,1)S(1)} %collective-permute-done.41.refs_2_, ...), custom_call_target="tpu_custom_call" | custom-call | flops 134217728 | bytes 1048576 | tf_op jit(solution)/shard_map/scan/pallas_call | solution.py:497
  159.3 6.0 %collective-permute-start.48 = (bf16[528,256]{1,0:T(8,128)(2,1)S(1)}, bf16[528,256]{1,0:T(8,128)(2,1)}, u32[]{:S(2)}, u32[]{:S(2)}) collective-permute-start(bf16[528,256]{1,0:T(8,128)(2,1)S(1)} %get-tuple-element.85), channel_id=1, source_target_pairs={{0,8},{4,12},{8,0},{12,4},{16,24},{20,28},{24,16},{28,20},{1,9},{5... | collective-permute-start | bytes 811016 | tf_op jit(solution)/shard_map/ppermute | solution.py:558
  166.6 3.3 %collective-permute-done.48 = bf16[528,256]{1,0:T(8,128)(2,1)} collective-permute-done((bf16[528,256]{1,0:T(8,128)(2,1)S(1)}, bf16[528,256]{1,0:T(8,128)(2,1)}, u32[]{:S(2)}, u32[]{:S(2)}) %collective-permute-start.48) | collective-permute-done | bytes 270368 | tf_op jit(solution)/shard_map/ppermute | solution.py:558
  173.7 5.3 %collective-permute-done.30 = bf16[528,256]{1,0:T(8,128)(2,1)S(1)} collective-permute-done((bf16[528,256]{1,0:T(8,128)(2,1)S(1)}, bf16[528,256]{1,0:T(8,128)(2,1)S(1)}, u32[]{:S(2)}, u32[]{:S(2)}) %collective-permute-start.30) | collective-permute-done | bytes 270368 | tf_op jit(solution)/shard_map/ppermute | solution.py:558
  184.8 4.9 %collective-permute-done.46 = bf16[528,256]{1,0:T(8,128)(2,1)S(1)} collective-permute-done((bf16[528,256]{1,0:T(8,128)(2,1)S(1)}, bf16[528,256]{1,0:T(8,128)(2,1)S(1)}, u32[]{:S(2)}, u32[]{:S(2)}) %collective-permute-start.46) | collective-permute-done | bytes 270368 | tf_op jit(solution)/shard_map/ppermute | solution.py:558
  211.0 2.7 %collective-permute-done.35 = bf16[4,1,32,512]{3,2,1,0:T(8,128)(2,1)S(1)} collective-permute-done((bf16[4,1,32,512]{3,2,1,0:T(8,128)(2,1)S(1)}, bf16[4,1,32,512]{3,2,1,0:T(8,128)(2,1)S(1)}, u32[]{:S(2)}, u32[]{:S(2)}) %collective-permute-start.35) | collective-permute-done | bytes 131104 | tf_op jit(solution)/shard_map/ppermute | solution.py:721
  214.3 1.9 slice_add_fusion
  222.6 4.6 %collective-permute-done.55 = bf16[4,1,32,512]{3,2,0,1:T(8,128)(2,1)S(1)} collective-permute-done((bf16[4,1,32,512]{3,2,0,1:T(8,128)(2,1)S(1)}, bf16[4,1,32,512]{3,2,0,1:T(8,128)(2,1)S(1)}, u32[]{:S(2)}, u32[]{:S(2)}) %collective-permute-start.55) | collective-permute-done | bytes 131104 | tf_op jit(solution)/shard_map/ppermute | solution.py:721
  228.0 5.6 %all-to-all-start = ((bf16[8,32,512]{2,1,0:T(8,128)(2,1)}), bf16[8,32,512]{2,1,0:T(8,128)(2,1)S(1)}, u32[]{:S(2)}, u32[]{:S(2)}) async-start(bf16[8,32,512]{2,1,0:T(8,128)(2,1)} %pad_maximum_fusion.1), calls=%async_computation | async-start | bytes 524288 | tf_op jit(solution)/shard_map/all_to_all | solution.py:728
  234.9 7.2 %all-to-all-done = bf16[8,32,512]{2,1,0:T(8,128)(2,1)S(1)} async-done(((bf16[8,32,512]{2,1,0:T(8,128)(2,1)}), bf16[8,32,512]{2,1,0:T(8,128)(2,1)S(1)}, u32[]{:S(2)}, u32[]{:S(2)}) %all-to-all-start) | async-done | bytes 262176 | tf_op jit(solution)/shard_map/all_to_all | solution.py:728
  (301 shorter events, 115.7 us)
Async XLA Ops:
  12.2 13.0 %collective-permute-start.11 = (bf16[512,256]{1,0:T(8,128)(2,1)}, bf16[512,256]{1,0:T(8,128)(2,1)S(1)}, u32[]{:S(2)}, u32[]{:S(2)}) collective-permute-start(bf16[512,256]{1,0:T(8,128)(2,1)} %get-tuple-element.48), channel_id=1, source_target_pairs={{0,4},{4,0},{8,12},{12,8},{16,20},{20,16},{24,28},{28,24},{1,5},{5... | collective-permute-start | bytes 786440 | tf_op jit(solution)/shard_map/ppermute | solution.py:561
  25.2 11.2 %collective-permute-start.12 = (bf16[512,256]{1,0:T(8,128)(2,1)S(1)}, bf16[512,256]{1,0:T(8,128)(2,1)S(1)}, u32[]{:S(2)}, u32[]{:S(2)}) collective-permute-start(bf16[512,256]{1,0:T(8,128)(2,1)S(1)} %bitcast.110), channel_id=1, source_target_pairs={{0,4},{4,0},{8,12},{12,8},{16,20},{20,16},{24,28},{28,24},{1,5},{5... | collective-permute-start | bytes 786440 | tf_op jit(solution)/shard_map/ppermute | solution.py:561
  26.7 14.8 %collective-permute-start.4 = (bf16[4,32,1024]{2,1,0:T(8,128)(2,1)S(1)}, bf16[4,32,1024]{2,1,0:T(8,128)(2,1)}, u32[]{:S(2)}, u32[]{:S(2)}) collective-permute-start(bf16[4,32,1024]{2,1,0:T(8,128)(2,1)S(1)} %pad_maximum_fusion.refs_0_), channel_id=1, source_target_pairs={{0,2},{1,3},{2,0},{3,1},{4,6},{5,7},{6,4},{7,5},{8,10},{9,11},{10,... | collective-permute-start | bytes 786440 | tf_op jit(solution)/shard_map/ppermute | solution.py:599
  62.0 10.4 %collective-permute-start.16 = (bf16[512,256]{1,0:T(8,128)(2,1)S(1)}, bf16[512,256]{1,0:T(8,128)(2,1)S(1)}, u32[]{:S(2)}, u32[]{:S(2)}) collective-permute-start(bf16[512,256]{1,0:T(8,128)(2,1)S(1)} %get-tuple-element.57), channel_id=1, source_target_pairs={{0,8},{4,12},{24,16},{28,20},{1,9},{5,13},{25,17},{29,21},{2,10},{... | collective-permute-start | bytes 786440 | tf_op jit(solution)/shard_map/ppermute | solution.py:558
  65.7 20.2 %collective-permute-start.19 = (bf16[528,256]{1,0:T(8,128)(2,1)}, bf16[528,256]{1,0:T(8,128)(2,1)}, u32[]{:S(2)}, u32[]{:S(2)}) collective-permute-start(bf16[528,256]{1,0:T(8,128)(2,1)} %get-tuple-element.60.own_ref), channel_id=1, source_target_pairs={{0,8},{4,12},{24,16},{28,20},{1,9},{5,13},{25,17},{29,21},{2,10},{... | collective-permute-start | bytes 811016 | tf_op jit(solution)/shard_map/ppermute | solution.py:558
  67.7 33.9 %collective-permute-start.21 = (bf16[528,256]{1,0:T(8,128)(2,1)}, bf16[528,256]{1,0:T(8,128)(2,1)}, u32[]{:S(2)}, u32[]{:S(2)}) collective-permute-start(bf16[528,256]{1,0:T(8,128)(2,1)} %get-tuple-element.59.own_ref), channel_id=1, source_target_pairs={{0,8},{4,12},{24,16},{28,20},{1,9},{5,13},{25,17},{29,21},{2,10},{... | collective-permute-start | bytes 811016 | tf_op jit(solution)/shard_map/ppermute | solution.py:558
  72.4 30.9 %collective-permute-start.17 = (bf16[512,256]{1,0:T(8,128)(2,1)S(1)}, bf16[512,256]{1,0:T(8,128)(2,1)}, u32[]{:S(2)}, u32[]{:S(2)}) collective-permute-start(bf16[512,256]{1,0:T(8,128)(2,1)S(1)} %add_convert_fusion.1.refs_4_), channel_id=1, source_target_pairs={{8,16},{12,20},{16,8},{20,12},{9,17},{13,21},{17,9},{21,13},{10,18... | collective-permute-start | bytes 786440 | tf_op jit(solution)/shard_map/ppermute | solution.py:558
  82.0 23.2 %collective-permute-start.18 = (bf16[528,256]{1,0:T(8,128)(2,1)}, bf16[528,256]{1,0:T(8,128)(2,1)S(1)}, u32[]{:S(2)}, u32[]{:S(2)}) collective-permute-start(bf16[528,256]{1,0:T(8,128)(2,1)} %copy-done.30), channel_id=1, source_target_pairs={{0,8},{4,12},{8,0},{12,4},{16,24},{20,28},{24,16},{28,20},{1,9},{5... | collective-permute-start | bytes 811016 | tf_op jit(solution)/shard_map/ppermute | solution.py:558
  87.0 18.9 %collective-permute-start.20 = (bf16[528,256]{1,0:T(8,128)(2,1)S(1)}, bf16[528,256]{1,0:T(8,128)(2,1)S(1)}, u32[]{:S(2)}, u32[]{:S(2)}) collective-permute-start(bf16[528,256]{1,0:T(8,128)(2,1)S(1)} %onward.4), channel_id=1, source_target_pairs={{8,24},{12,28},{16,0},{20,4},{9,25},{13,29},{17,1},{21,5},{10,26},... | collective-permute-start | bytes 811016 | tf_op jit(solution)/shard_map/ppermute | solution.py:558
  95.6 20.5 %collective-permute-start.24 = (bf16[512,256]{1,0:T(8,128)(2,1)}, bf16[512,256]{1,0:T(8,128)(2,1)}, u32[]{:S(2)}, u32[]{:S(2)}) collective-permute-start(bf16[512,256]{1,0:T(8,128)(2,1)} %get-tuple-element.65), channel_id=1, source_target_pairs={{0,8},{4,12},{24,16},{28,20},{1,9},{5,13},{25,17},{29,21},{2,10},{... | collective-permute-start | bytes 786440 | tf_op jit(solution)/shard_map/ppermute | solution.py:558
  102.7 13.4 %collective-permute-start.22 = (bf16[528,256]{1,0:T(8,128)(2,1)S(1)}, bf16[528,256]{1,0:T(8,128)(2,1)S(1)}, u32[]{:S(2)}, u32[]{:S(2)}) collective-permute-start(bf16[528,256]{1,0:T(8,128)(2,1)S(1)} %onward.5), channel_id=1, source_target_pairs={{8,16},{12,20},{16,8},{20,12},{9,17},{13,21},{17,9},{21,13},{10,18... | collective-permute-start | bytes 811016 | tf_op jit(solution)/shard_map/ppermute | solution.py:558
  108.2 21.4 %collective-permute-start.40 = (bf16[528,256]{1,0:T(8,128)(2,1)}, bf16[528,256]{1,0:T(8,128)(2,1)}, u32[]{:S(2)}, u32[]{:S(2)}) collective-permute-start(bf16[528,256]{1,0:T(8,128)(2,1)} %copy-done.14), channel_id=1, source_target_pairs={{0,8},{4,12},{24,16},{28,20},{1,9},{5,13},{25,17},{29,21},{2,10},{... | collective-permute-start | bytes 811016 | tf_op jit(solution)/shard_map/ppermute | solution.py:558
  114.1 18.8 %collective-permute-start.42 = (bf16[528,256]{1,0:T(8,128)(2,1)}, bf16[528,256]{1,0:T(8,128)(2,1)}, u32[]{:S(2)}, u32[]{:S(2)}) collective-permute-start(bf16[528,256]{1,0:T(8,128)(2,1)} %copy-done.16), channel_id=1, source_target_pairs={{0,8},{4,12},{24,16},{28,20},{1,9},{5,13},{25,17},{29,21},{2,10},{... | collective-permute-start | bytes 811016 | tf_op jit(solution)/shard_map/ppermute | solution.py:558
  127.9 12.2 %collective-permute-start.38 = (bf16[512,256]{1,0:T(8,128)(2,1)S(1)}, bf16[512,256]{1,0:T(8,128)(2,1)S(1)}, u32[]{:S(2)}, u32[]{:S(2)}) collective-permute-start(bf16[512,256]{1,0:T(8,128)(2,1)S(1)} %add_convert_fusion.refs_4_), channel_id=1, source_target_pairs={{8,16},{12,20},{16,8},{20,12},{9,17},{13,21},{17,9},{21,13},{10,18... | collective-permute-start | bytes 786440 | tf_op jit(solution)/shard_map/ppermute | solution.py:558
  128.9 12.1 %collective-permute-start.39 = (bf16[528,256]{1,0:T(8,128)(2,1)S(1)}, bf16[528,256]{1,0:T(8,128)(2,1)S(1)}, u32[]{:S(2)}, u32[]{:S(2)}) collective-permute-start(bf16[528,256]{1,0:T(8,128)(2,1)S(1)} %copy-done.29), channel_id=1, source_target_pairs={{0,8},{4,12},{8,0},{12,4},{16,24},{20,28},{24,16},{28,20},{1,9},{5... | collective-permute-start | bytes 811016 | tf_op jit(solution)/shard_map/ppermute | solution.py:558
  131.6 12.2 %collective-permute-start.41 = (bf16[528,256]{1,0:T(8,128)(2,1)S(1)}, bf16[528,256]{1,0:T(8,128)(2,1)S(1)}, u32[]{:S(2)}, u32[]{:S(2)}) collective-permute-start(bf16[528,256]{1,0:T(8,128)(2,1)S(1)} %onward.6), channel_id=1, source_target_pairs={{8,24},{12,28},{16,0},{20,4},{9,25},{13,29},{17,1},{21,5},{10,26},... | collective-permute-start | bytes 811016 | tf_op jit(solution)/shard_map/ppermute | solution.py:558
  134.0 11.2 %collective-permute-start.25 = (bf16[528,256]{1,0:T(8,128)(2,1)S(1)}, bf16[528,256]{1,0:T(8,128)(2,1)S(1)}, u32[]{:S(2)}, u32[]{:S(2)}) collective-permute-start(bf16[528,256]{1,0:T(8,128)(2,1)S(1)} %get-tuple-element.68), channel_id=1, source_target_pairs={{8,16},{12,20},{16,8},{20,12},{9,17},{13,21},{17,9},{21,13},{10,18... | collective-permute-start | bytes 811016 | tf_op jit(solution)/shard_map/ppermute | solution.py:558
  134.7 13.9 %collective-permute-start.28 = (bf16[528,256]{1,0:T(8,128)(2,1)S(1)}, bf16[528,256]{1,0:T(8,128)(2,1)S(1)}, u32[]{:S(2)}, u32[]{:S(2)}) collective-permute-start(bf16[528,256]{1,0:T(8,128)(2,1)S(1)} %get-tuple-element.68), channel_id=1, source_target_pairs={{0,8},{4,12},{8,0},{12,4},{16,24},{20,28},{24,16},{28,20},{1,9},{5... | collective-permute-start | bytes 811016 | tf_op jit(solution)/shard_map/ppermute | solution.py:558
  141.0 18.3 %collective-permute-start.27 = (bf16[528,256]{1,0:T(8,128)(2,1)S(1)}, bf16[528,256]{1,0:T(8,128)(2,1)S(1)}, u32[]{:S(2)}, u32[]{:S(2)}) collective-permute-start(bf16[528,256]{1,0:T(8,128)(2,1)S(1)} %get-tuple-element.68), channel_id=1, source_target_pairs={{0,4},{4,0},{8,12},{12,8},{16,20},{20,16},{24,28},{28,24},{1,5},{5... | collective-permute-start | bytes 811016 | tf_op jit(solution)/shard_map/ppermute | solution.py:561
  145.1 14.1 %collective-permute-start.26 = (bf16[528,256]{1,0:T(8,128)(2,1)S(1)}, bf16[528,256]{1,0:T(8,128)(2,1)S(1)}, u32[]{:S(2)}, u32[]{:S(2)}) collective-permute-start(bf16[528,256]{1,0:T(8,128)(2,1)S(1)} %collective-permute-done.25), channel_id=1, source_target_pairs={{8,0},{12,4},{16,24},{20,28},{9,1},{13,5},{17,25},{21,29},{10,2},{... | collective-permute-start | bytes 811016 | tf_op jit(solution)/shard_map/ppermute | solution.py:558
  148.6 17.6 %collective-permute-start.29 = (bf16[528,256]{1,0:T(8,128)(2,1)S(1)}, bf16[528,256]{1,0:T(8,128)(2,1)S(1)}, u32[]{:S(2)}, u32[]{:S(2)}) collective-permute-start(bf16[528,256]{1,0:T(8,128)(2,1)S(1)} %collective-permute-done.28), channel_id=1, source_target_pairs={{8,16},{12,20},{16,8},{20,12},{9,17},{13,21},{17,9},{21,13},{10,18... | collective-permute-start | bytes 811016 | tf_op jit(solution)/shard_map/ppermute | solution.py:558
  149.6 30.8 %collective-permute-start.31 = (bf16[528,256]{1,0:T(8,128)(2,1)S(1)}, bf16[528,256]{1,0:T(8,128)(2,1)S(1)}, u32[]{:S(2)}, u32[]{:S(2)}) collective-permute-start(bf16[528,256]{1,0:T(8,128)(2,1)S(1)} %collective-permute-done.28), channel_id=1, source_target_pairs={{0,4},{4,0},{8,12},{12,8},{16,20},{20,16},{24,28},{28,24},{1,5},{5... | collective-permute-start | bytes 811016 | tf_op jit(solution)/shard_map/ppermute | solution.py:561
  158.0 23.1 %collective-permute-start.45 = (bf16[528,256]{1,0:T(8,128)(2,1)S(1)}, bf16[528,256]{1,0:T(8,128)(2,1)S(1)}, u32[]{:S(2)}, u32[]{:S(2)}) collective-permute-start(bf16[528,256]{1,0:T(8,128)(2,1)S(1)} %get-tuple-element.85), channel_id=1, source_target_pairs={{8,16},{12,20},{16,8},{20,12},{9,17},{13,21},{17,9},{21,13},{10,18... | collective-permute-start | bytes 811016 | tf_op jit(solution)/shard_map/ppermute | solution.py:558
  159.3 30.5 %collective-permute-start.47 = (bf16[528,256]{1,0:T(8,128)(2,1)S(1)}, bf16[528,256]{1,0:T(8,128)(2,1)S(1)}, u32[]{:S(2)}, u32[]{:S(2)}) collective-permute-start(bf16[528,256]{1,0:T(8,128)(2,1)S(1)} %get-tuple-element.85), channel_id=1, source_target_pairs={{0,4},{4,0},{8,12},{12,8},{16,20},{20,16},{24,28},{28,24},{1,5},{5... | collective-permute-start | bytes 811016 | tf_op jit(solution)/shard_map/ppermute | solution.py:561
  159.3 10.5 %collective-permute-start.48 = (bf16[528,256]{1,0:T(8,128)(2,1)S(1)}, bf16[528,256]{1,0:T(8,128)(2,1)}, u32[]{:S(2)}, u32[]{:S(2)}) collective-permute-start(bf16[528,256]{1,0:T(8,128)(2,1)S(1)} %get-tuple-element.85), channel_id=1, source_target_pairs={{0,8},{4,12},{8,0},{12,4},{16,24},{20,28},{24,16},{28,20},{1,9},{5... | collective-permute-start | bytes 811016 | tf_op jit(solution)/shard_map/ppermute | solution.py:558
  166.2 16.8 %collective-permute-start.32 = (bf16[528,256]{1,0:T(8,128)(2,1)S(1)}, bf16[528,256]{1,0:T(8,128)(2,1)S(1)}, u32[]{:S(2)}, u32[]{:S(2)}) collective-permute-start(bf16[528,256]{1,0:T(8,128)(2,1)S(1)} %broadcast_select_fusion.3), channel_id=1, source_target_pairs={{0,4},{4,0},{8,12},{12,8},{16,20},{20,16},{24,28},{28,24},{1,5},{5... | collective-permute-start | bytes 811016 | tf_op jit(solution)/shard_map/ppermute | solution.py:561
  179.0 13.5 %collective-permute-start.49 = (bf16[528,256]{1,0:T(8,128)(2,1)}, bf16[528,256]{1,0:T(8,128)(2,1)}, u32[]{:S(2)}, u32[]{:S(2)}) collective-permute-start(bf16[528,256]{1,0:T(8,128)(2,1)} %collective-permute-done.48), channel_id=1, source_target_pairs={{8,16},{12,20},{16,8},{20,12},{9,17},{13,21},{17,9},{21,13},{10,18... | collective-permute-start | bytes 811016 | tf_op jit(solution)/shard_map/ppermute | solution.py:558
  180.4 22.6 %collective-permute-start.51 = (bf16[528,256]{1,0:T(8,128)(2,1)}, bf16[528,256]{1,0:T(8,128)(2,1)}, u32[]{:S(2)}, u32[]{:S(2)}) collective-permute-start(bf16[528,256]{1,0:T(8,128)(2,1)} %collective-permute-done.48), channel_id=1, source_target_pairs={{0,4},{4,0},{8,12},{12,8},{16,20},{20,16},{24,28},{28,24},{1,5},{5... | collective-permute-start | bytes 811016 | tf_op jit(solution)/shard_map/ppermute | solution.py:561
  183.0 12.0 %collective-permute-start.33 = (bf16[528,256]{1,0:T(8,128)(2,1)S(1)}, bf16[528,256]{1,0:T(8,128)(2,1)S(1)}, u32[]{:S(2)}, u32[]{:S(2)}) collective-permute-start(bf16[528,256]{1,0:T(8,128)(2,1)S(1)} %broadcast_select_fusion.2), channel_id=1, source_target_pairs={{0,4},{4,0},{8,12},{12,8},{16,20},{20,16},{24,28},{28,24},{1,5},{5... | collective-permute-start | bytes 811016 | tf_op jit(solution)/shard_map/ppermute | solution.py:561
  191.3 15.0 %collective-permute-start.52 = (bf16[528,256]{1,0:T(8,128)(2,1)S(1)}, bf16[528,256]{1,0:T(8,128)(2,1)}, u32[]{:S(2)}, u32[]{:S(2)}) collective-permute-start(bf16[528,256]{1,0:T(8,128)(2,1)S(1)} %broadcast_select_fusion.1), channel_id=1, source_target_pairs={{0,4},{4,0},{8,12},{12,8},{16,20},{20,16},{24,28},{28,24},{1,5},{5... | collective-permute-start | bytes 811016 | tf_op jit(solution)/shard_map/ppermute | solution.py:561
  203.0 10.8 %collective-permute-start.53 = (bf16[528,256]{1,0:T(8,128)(2,1)S(1)}, bf16[528,256]{1,0:T(8,128)(2,1)S(1)}, u32[]{:S(2)}, u32[]{:S(2)}) collective-permute-start(bf16[528,256]{1,0:T(8,128)(2,1)S(1)} %broadcast_select_fusion), channel_id=1, source_target_pairs={{0,4},{4,0},{8,12},{12,8},{16,20},{20,16},{24,28},{28,24},{1,5},{5... | collective-permute-start | bytes 811016 | tf_op jit(solution)/shard_map/ppermute | solution.py:561
  228.0 14.1 %all-to-all-start = ((bf16[8,32,512]{2,1,0:T(8,128)(2,1)}), bf16[8,32,512]{2,1,0:T(8,128)(2,1)S(1)}, u32[]{:S(2)}, u32[]{:S(2)}) async-start(bf16[8,32,512]{2,1,0:T(8,128)(2,1)} %pad_maximum_fusion.1), calls=%async_computation | async-start | bytes 524288 | tf_op jit(solution)/shard_map/all_to_all | solution.py:728
  (79 other events, 767.1 us)
